TPU v7x, 32 devices: a whole 2x2x4 slice. The times are simulated.
32 devices in a mesh: ctx: 4 (over y, x), exp: 8 (over z, core).
Axes of the slice: x: 2, y: 2, z: 4, core: 2. Of those that a mesh axis runs over, the one named last changes fastest.
Arguments:
- moe_input: bfloat16 [1024, 3584], P('exp', 'ctx'), may hold values from -6 to 6
- moe_grad: bfloat16 [1024, 3584], P('exp', 'ctx'), may hold values from -6 to 6
- routes: int32 [1024, 8], P('exp'), may hold values from 0 to 15, all different within a row; in each aligned block of 128 rows (0 to 127, 128 to 255, ...) at most 80 rows name the same one
- gates: float32 [1024, 8], P('exp'), may hold values from 0.05 to 0.5
- w_gate: bfloat16 [16, 3584, 1024], P('exp', 'ctx'), may hold values from -0.09375 to 0.09375
- w_up: bfloat16 [16, 3584, 1024], P('exp', 'ctx'), may hold values from -0.09375 to 0.09375
- w_down: bfloat16 [16, 1024, 3584], P('exp', None, 'ctx'), may hold values from -0.1875 to 0.1875
- queries: bfloat16 [512, 9216], P('ctx', 'exp'), may hold values from -16 to 16
- out_grad: bfloat16 [512, 8192], P('ctx', 'exp'), may hold values from -6 to 6
- positions: int32 [512], P('ctx'), may hold values from 0 to 1023, as said below
- latents: bfloat16 [1024, 576], P('ctx'), may hold values from -6 to 6
Outputs:
- moe_input_grad: bfloat16 [1024, 3584], P('exp', 'ctx')
- query_grad: bfloat16 [512, 9216], P('ctx', 'exp')
- latent_grad: float32 [1024, 576], P(('ctx', 'exp'))
Inputs may be any that keep to these rules, and one draw needn't show every extreme that they name: `routes`: each row names 8 different experts; among the 128 rows of one index of exp no expert is named more than 80 times, and in some such block one is named exactly 80 times. Row i lies within the keys of its own context shard, (i // 128) * 256 <= positions[i] < (i // 128 + 1) * 256; the first row of each shard sits at the shard's first key and the last row at its last key.
All inputs are finite; a program needn't handle non-finite values.
Results may differ from a plain program's by a relative error of at most 0.018.
Values may be sent and summed in bfloat16 or wider, within the bound.
No kernel may reach another device: no remote copies, remote signals or barrier semaphores. Data moves between devices by JAX's collectives and lax.ppermute only.
A program may use at most 128 MiB of HBM per device.

v0:
```python
import jax
import jax.numpy as jnp
from jax import lax
from jax.sharding import PartitionSpec as P

SCORE_SCALE = 192.0 ** (-0.5)
MASKED = -1e30


def swiglu_back(gate_pre, up_pre, hidden_grad):
    sigma = jax.nn.sigmoid(gate_pre)
    gate_back = hidden_grad * up_pre * sigma * (1.0 + gate_pre * (1.0 - sigma))
    up_back = hidden_grad * gate_pre * sigma
    return (gate_back.astype(jnp.bfloat16), up_back.astype(jnp.bfloat16))


def expert_layer(moe_input, moe_grad, routes, gates, w_gate, w_up, w_down):
    tok_rows, width_part = moe_input.shape
    fanout = routes.shape[1]
    local_experts = w_gate.shape[0]
    exp_count = lax.axis_size("exp")
    experts = local_experts * exp_count
    capacity = tok_rows * fanout // experts * 5 // 4
    flat_routes = routes.reshape(-1)
    onehot = (flat_routes[:, None] == jnp.arange(experts, dtype=jnp.int32)[None, :]).astype(
        jnp.int32
    )
    before = jnp.cumsum(onehot, axis=0) - onehot
    slot_index = jnp.sum(before * onehot, axis=1)
    target = flat_routes * capacity + slot_index
    source_rows = jnp.arange(tok_rows * fanout, dtype=jnp.int32) // fanout
    empty = jnp.zeros((experts * capacity, width_part), jnp.bfloat16)
    send_shape = (exp_count, local_experts * capacity, width_part)
    send_input = empty.at[target].set(moe_input[source_rows]).reshape(send_shape)
    send_grad = empty.at[target].set(moe_grad[source_rows]).reshape(send_shape)
    recv_input, recv_grad = (
        lax.all_to_all(send_input, "exp", split_axis=0, concat_axis=0, tiled=True),
        lax.all_to_all(send_grad, "exp", split_axis=0, concat_axis=0, tiled=True),
    )
    slot_shape = (exp_count, local_experts, capacity, width_part)
    recv_input = recv_input.reshape(slot_shape)
    recv_grad = recv_grad.reshape(slot_shape)
    gate_part = jnp.einsum("sekd,edh->sekh", recv_input, w_gate, preferred_element_type=jnp.float32)
    up_part = jnp.einsum("sekd,edh->sekh", recv_input, w_up, preferred_element_type=jnp.float32)
    down_part = jnp.einsum("sekd,ehd->sekh", recv_grad, w_down, preferred_element_type=jnp.float32)
    gate_pre, up_pre, hidden_grad = (
        lax.psum(gate_part.astype(jnp.bfloat16), "ctx").astype(jnp.float32),
        lax.psum(up_part.astype(jnp.bfloat16), "ctx").astype(jnp.float32),
        lax.psum(down_part.astype(jnp.bfloat16), "ctx").astype(jnp.float32),
    )
    gate_back, up_back = swiglu_back(gate_pre, up_pre, hidden_grad)
    route_part = jnp.einsum("sekh,edh->sekd", gate_back, w_gate, preferred_element_type=jnp.float32)
    route_part = route_part + jnp.einsum(
        "sekh,edh->sekd", up_back, w_up, preferred_element_type=jnp.float32
    )
    route_part = route_part.astype(jnp.bfloat16).reshape(send_shape)
    returned = lax.all_to_all(route_part, "exp", split_axis=0, concat_axis=0, tiled=True).reshape(
        experts * capacity, width_part
    )
    per_route = returned[target].reshape(tok_rows, fanout, width_part).astype(jnp.float32)
    return jnp.sum(per_route * gates[:, :, None], axis=1).astype(jnp.bfloat16)


def attention_layer(queries, out_grad, positions, latents):
    q_rows = queries.shape[0]
    lat_width = latents.shape[1]
    head_count = queries.shape[1] // lat_width
    val_width = out_grad.shape[1] // head_count
    query_heads = queries.reshape(q_rows, head_count, lat_width)
    grad_heads = out_grad.reshape(q_rows, head_count, val_width)
    gathered = lax.all_gather(latents, "ctx", axis=0, tiled=True)
    key_count = gathered.shape[0]
    visible = (jnp.arange(key_count, dtype=jnp.int32)[None, :] <= positions[:, None])[None]
    scores = (
        jnp.einsum("qhc,kc->hqk", query_heads, gathered, preferred_element_type=jnp.float32)
        * SCORE_SCALE
    )
    scores = jnp.where(visible, scores, MASKED)
    peak = jnp.max(scores, axis=2, keepdims=True)
    raw = jnp.where(visible, jnp.exp(scores - peak), 0.0)
    attend = raw / jnp.sum(raw, axis=2, keepdims=True)
    value_dot = jnp.einsum(
        "qhv,kv->hqk", grad_heads, gathered[:, :val_width], preferred_element_type=jnp.float32
    )
    row_dot = jnp.sum(attend * value_dot, axis=2, keepdims=True)
    score_grad = (attend * (value_dot - row_dot)).astype(jnp.bfloat16)
    query_grad = (
        jnp.einsum("hqk,kc->qhc", score_grad, gathered, preferred_element_type=jnp.float32)
        * SCORE_SCALE
    )
    key_grad = (
        jnp.einsum("hqk,qhc->kc", score_grad, query_heads, preferred_element_type=jnp.float32)
        * SCORE_SCALE
    )
    value_grad = jnp.einsum(
        "hqk,qhv->kv", attend.astype(jnp.bfloat16), grad_heads, preferred_element_type=jnp.float32
    )
    latent_part = key_grad + jnp.pad(value_grad, ((0, 0), (0, lat_width - val_width)))
    latent_grad = lax.psum_scatter(latent_part, ("ctx", "exp"), scatter_dimension=0, tiled=True)
    query_out = query_grad.astype(jnp.bfloat16).reshape(q_rows, head_count * lat_width)
    return (query_out, latent_grad)


def per_device(
    moe_input, moe_grad, routes, gates, w_gate, w_up, w_down, queries, out_grad, positions, latents
):
    input_grad = expert_layer(moe_input, moe_grad, routes, gates, w_gate, w_up, w_down)
    query_out, latent_grad = attention_layer(queries, out_grad, positions, latents)
    return (input_grad, query_out, latent_grad)


def solution(mesh):
    return jax.shard_map(
        per_device,
        mesh=mesh,
        in_specs=(
            P("exp", "ctx"),
            P("exp", "ctx"),
            P("exp", None),
            P("exp", None),
            P("exp", "ctx", None),
            P("exp", "ctx", None),
            P("exp", None, "ctx"),
            P("ctx", "exp"),
            P("ctx", "exp"),
            P("ctx"),
            P("ctx", None),
        ),
        out_specs=(P("exp", "ctx"), P("ctx", "exp"), P(("ctx", "exp"), None)),
        check_vma=False,
    )
```

profile of v0, /device:TPU:0, one launch (start us, length us, event | category | flops | bytes accessed | tf_op | source)
XLA Modules:
  0.0 468.5 jit_solution(17278955433293576790)
XLA Ops:
  7.2 0.8 copy.27
  8.2 0.7 broadcast_multiply_fusion
  8.9 4.5 reduce-window.6
  14.1 13.7 %scatter_custom_fusion.1 = bf16[1280,896]{1,0:T(8,128)(2,1)} fusion(s32[1024]{0:T(1024)S(1)} %bitcast.114, bf16[128,896]{1,0:T(8,128)(2,1)S(1)} %copy-done, s32[1024]{0:T(1024)S(1)} %broadcast_clamp_fusion.1, bf16[]{:T(256)} %constant.14.clone.1), kind=kCustom, calls=%fused_computation.41 | custom fusion | bytes 2293762 | tf_op jit(solution)/shard_map/scatter | solution.py:34
  27.8 6.3 %all-to-all-start.1 = ((bf16[8,160,896]{2,1,0:T(8,128)(2,1)}), bf16[8,160,896]{2,1,0:T(8,128)(2,1)S(1)}, u32[]{:S(2)}, u32[]{:S(2)}) async-start(bf16[8,160,896]{2,1,0:T(8,128)(2,1)} %bitcast.10), calls=%async_computation.1 | async-start | bytes 4587520 | tf_op jit(solution)/shard_map/all_to_all | solution.py:37
  34.2 16.0 %scatter_custom_fusion = bf16[1280,896]{1,0:T(8,128)(2,1)} fusion(s32[1024]{0:T(1024)S(1)} %bitcast.115, bf16[128,896]{1,0:T(8,128)(2,1)} %param.12, s32[1024]{0:T(1024)S(1)} %broadcast_clamp_fusion.1, bf16[]{:T(256)} %constant.14.clone.1), kind=kCustom, calls=%fused_computation.43 | custom fusion | bytes 2294272 | tf_op jit(solution)/shard_map/scatter | solution.py:35
  50.1 37.3 %all-to-all-done.1 = bf16[8,160,896]{2,1,0:T(8,128)(2,1)S(1)} async-done(((bf16[8,160,896]{2,1,0:T(8,128)(2,1)}), bf16[8,160,896]{2,1,0:T(8,128)(2,1)S(1)}, u32[]{:S(2)}, u32[]{:S(2)}) %all-to-all-start.1) | async-done | bytes 2293792 | tf_op jit(solution)/shard_map/all_to_all | solution.py:37
  87.4 4.4 all-to-all-start
  91.9 0.7 all-gather.2.cloned.1.call-update
  92.6 6.5 %convert_bitcast_fusion = bf16[8,2,80,1024]{3,2,0,1:T(8,128)(2,1)} fusion(bf16[2,896,1024]{2,1,0:T(8,128)(2,1)} %param.15, bf16[8,2,80,896]{3,2,1,0:T(8,128)(2,1)S(1)} %bitcast.104), kind=kOutput, calls=%fused_computation.34 | convolution fusion | flops 2350120960 | bytes 8585216 | tf_op jit(solution)/shard_map/sekd,edh->sekh/dot_general | solution.py:43
  99.1 4.1 convert_bitcast_fusion.1
  103.2 41.9 %all-to-all-done = bf16[8,160,896]{2,1,0:T(8,128)(2,1)} async-done(((bf16[8,160,896]{2,1,0:T(8,128)(2,1)}), bf16[8,160,896]{2,1,0:T(8,128)(2,1)}, u32[]{:S(2)}, u32[]{:S(2)}) %all-to-all-start) | async-done | bytes 2293792 | tf_op jit(solution)/shard_map/all_to_all | solution.py:38
  145.1 7.2 %convert_bitcast_fusion.2 = bf16[8,2,80,1024]{3,2,0,1:T(8,128)(2,1)} fusion(bf16[2,1024,896]{2,1,0:T(8,128)(2,1)} %param.17, bf16[8,2,80,896]{3,2,1,0:T(8,128)(2,1)} %bitcast.6), kind=kOutput, calls=%fused_computation.36 | convolution fusion | flops 2350120960 | bytes 8585216 | tf_op jit(solution)/shard_map/sekd,ehd->sekh/dot_general | solution.py:45
  152.3 0.3 reduce-scatter.2.cloned.1.call-start
  152.6 0.7 copy-done.1
  153.3 0.2 copy.35
  153.8 2.2 fusion.61
  156.0 0.5 convolution_bitcast_fusion
  156.5 1.1 copy-done.9
  157.7 0.5 multiply_reduce_fusion
  158.3 2.1 fusion.21
  160.5 156.0 %all-reduce.4.cloned.1.call-done = (bf16[8,2,80,1024]{3,2,0,1:T(8,128)(2,1)}, bf16[8,2,80,1024]{3,2,0,1:T(8,128)(2,1)}, bf16[8,2,80,1024]{3,2,0,1:T(8,128)(2,1)}) async-done(((bf16[8,2,80,1024]{3,2,0,1:T(8,128)(2,1)}, bf16[8,2,80,1024]{3,2,0,1:T(8,128)(2,1)}, bf16[8,2,80,1024]{3,2,0,1:T(8,128)(2,1)}), (bf16[8,2,80,1024]{3,2,0,1:T(8,128)(2,1)}, bf16[8,2,80,1024]{3,2,0,1:T(8,128)(2,1)}, ...) | async-done | bytes 7864336 | tf_op jit(solution)/shard_map/psum | solution.py:49
  316.5 7.7 %fusion.11 = f32[2,8,80,896]{3,2,1,0:T(8,128)S(1)} fusion(bf16[2,896,1024]{2,1,0:T(8,128)(2,1)} %param.15, bf16[8,2,80,1024]{3,2,0,1:T(8,128)(2,1)} %get-tuple-element.9, bf16[8,2,80,1024]{3,2,0,1:T(8,128)(2,1)} %get-tuple-element.10, bf16[8,2,80,1024]{3,2,0,1:T(8,128)(2,1)} %get-tuple-element.11), kind=kOutput, calls=%fused_computation.22 | convolution fusion | flops 2365849600 | bytes 16121856 | tf_op jit(solution)/shard_map/sekh,edh->sekd/dot_general | solution.py:52
  324.2 3.4 fusion.24
  327.6 1.6 copy.33
  329.2 4.7 %all-to-all-start.2 = ((bf16[8,160,896]{2,1,0:T(8,128)(2,1)}), bf16[8,160,896]{2,1,0:T(8,128)(2,1)S(1)}, u32[]{:S(2)}, u32[]{:S(2)}) async-start(bf16[8,160,896]{2,1,0:T(8,128)(2,1)} %bitcast.103), calls=%async_computation.2 | async-start | bytes 4587520 | tf_op jit(solution)/shard_map/all_to_all | solution.py:57
  334.0 1.8 fusion.49
  335.8 0.9 copy.42
  336.7 63.5 %all-to-all-done.2 = bf16[8,160,896]{2,1,0:T(8,128)(2,1)S(1)} async-done(((bf16[8,160,896]{2,1,0:T(8,128)(2,1)}), bf16[8,160,896]{2,1,0:T(8,128)(2,1)S(1)}, u32[]{:S(2)}, u32[]{:S(2)}) %all-to-all-start.2) | async-done | bytes 2293792 | tf_op jit(solution)/shard_map/all_to_all | solution.py:57
  400.2 5.2 %gather_fusion = bf16[1024,896]{1,0:T(8,128)(2,1)} fusion(bf16[1280,896]{1,0:T(8,128)(2,1)S(1)} %bitcast.102, s32[1024]{0:T(1024)S(1)} %broadcast_clamp_fusion), kind=kCustom, calls=%fused_computation.2 | custom fusion | bytes 3674112 | tf_op jit(solution)/shard_map/gather | solution.py:60
  405.4 3.4 fusion.10
  408.8 53.1 %reduce-scatter.2.cloned.1.call-done = f32[32,576]{1,0:T(8,128)} async-done(((f32[1024,576]{1,0:T(8,128)}), f32[32,576]{1,0:T(8,128)}) %reduce-scatter.2.cloned.1.call-update) | async-done | bytes 73744 | tf_op jit(solution)/shard_map/reduce_scatter | solution.py:99
  (43 shorter events, 1.5 us)
Async XLA Ops:
  7.2 6.9 %copy-start = (bf16[128,896]{1,0:T(8,128)(2,1)S(1)}, bf16[128,896]{1,0:T(8,128)(2,1)}, u32[]{:S(2)}) copy-start(bf16[128,896]{1,0:T(8,128)(2,1)} %param.11) | copy-start | bytes 688132
  27.8 59.6 %all-to-all-start.1 = ((bf16[8,160,896]{2,1,0:T(8,128)(2,1)}), bf16[8,160,896]{2,1,0:T(8,128)(2,1)S(1)}, u32[]{:S(2)}, u32[]{:S(2)}) async-start(bf16[8,160,896]{2,1,0:T(8,128)(2,1)} %bitcast.10), calls=%async_computation.1 | async-start | bytes 4587520 | tf_op jit(solution)/shard_map/all_to_all | solution.py:37
  87.4 57.6 %all-to-all-start = ((bf16[8,160,896]{2,1,0:T(8,128)(2,1)}), bf16[8,160,896]{2,1,0:T(8,128)(2,1)}, u32[]{:S(2)}, u32[]{:S(2)}) async-start(bf16[8,160,896]{2,1,0:T(8,128)(2,1)} %bitcast.5), calls=%async_computation | async-start | bytes 4587520 | tf_op jit(solution)/shard_map/all_to_all | solution.py:38
  91.8 62.0 %all-gather.2.cloned.1.call-start = ((), (), s32[]{:S(2)}) async-start(), calls=%async_computation.4 | async-start | bytes 1474560 | tf_op jit(solution)/shard_map/all_gather | solution.py:71
  92.5 223.9 %all-reduce.4.cloned.1.call-start = ((), (), s32[]{:S(2)}) async-start(), calls=%async_computation.6 | async-start | bytes 15728640 | tf_op jit(solution)/shard_map/psum | solution.py:49
  92.6 6.5 %copy-start.5 = (bf16[2,896,1024]{2,1,0:T(8,128)(2,1)S(1)}, bf16[2,896,1024]{2,1,0:T(8,128)(2,1)}, u32[]{:S(2)}) copy-start(bf16[2,896,1024]{2,1,0:T(8,128)(2,1)} %param.16) | copy-start | bytes 11010052
  152.3 1.0 copy-start.1
  152.3 1.2 copy-start.2
  152.3 1.4 copy-start.4
  152.3 309.6 %reduce-scatter.2.cloned.1.call-start = ((), (), s32[]{:S(2)}) async-start(), calls=%async_computation.5 | async-start | bytes 2703360 | tf_op jit(solution)/shard_map/reduce_scatter | solution.py:99
  156.0 1.6 copy-start.9
  316.5 7.7 %copy-start.6 = (bf16[2,896,1024]{2,1,0:T(8,128)(2,1)S(1)}, bf16[2,896,1024]{2,1,0:T(8,128)(2,1)}, u32[]{:S(2)}) copy-start(bf16[2,896,1024]{2,1,0:T(8,128)(2,1)} %param.16) | copy-start | bytes 11010052
  316.5 7.7 %copy-start.7 = (bf16[8,2,80,1024]{3,2,0,1:T(8,128)(2,1)S(1)}, bf16[8,2,80,1024]{3,2,0,1:T(8,128)(2,1)}, u32[]{:S(2)}) copy-start(bf16[8,2,80,1024]{3,2,0,1:T(8,128)(2,1)} %get-tuple-element.9) | copy-start | bytes 7864324
  316.5 7.7 %copy-start.8 = (bf16[8,2,80,1024]{3,2,0,1:T(8,128)(2,1)S(1)}, bf16[8,2,80,1024]{3,2,0,1:T(8,128)(2,1)}, u32[]{:S(2)}) copy-start(bf16[8,2,80,1024]{3,2,0,1:T(8,128)(2,1)} %get-tuple-element.10) | copy-start | bytes 7864324
  329.2 4.7 %copy-start.3 = (f32[128,8]{0,1:T(8,128)S(1)}, f32[128,8]{0,1:T(8,128)}, u32[]{:S(2)}) copy-start(f32[128,8]{0,1:T(8,128)} %param.14) | copy-start | bytes 12292
  329.2 71.0 %all-to-all-start.2 = ((bf16[8,160,896]{2,1,0:T(8,128)(2,1)}), bf16[8,160,896]{2,1,0:T(8,128)(2,1)S(1)}, u32[]{:S(2)}, u32[]{:S(2)}) async-start(bf16[8,160,896]{2,1,0:T(8,128)(2,1)} %bitcast.103), calls=%async_computation.2 | async-start | bytes 4587520 | tf_op jit(solution)/shard_map/all_to_all | solution.py:57
Sparse Core Ops, SparseCore 0:
  94.5 28.9 all-gather.1
  152.4 164.0 all-reduce.3
  319.3 142.5 reduce-scatter.1
where the time goes:
time: 469 us; the launch traced here: 468 us
  waiting for transfers between devices  353 us (75%)
  local copies, waits for them, and re-layouts  41.2 us (9%)
  matrix products  35.9 us (8%)
  starting transfers between devices  15.8 us (3%)
  between operations  13.9 us (3%)
  other arithmetic  9 us (2%)
    psum x1, waiting for transfers between devices, expert_layer(): lax.psum(down_part.astype(jnp.bfloat16), 'ctx').astype(jnp.float32)  156 us
    all_to_all x1, waiting for transfers between devices, expert_layer(): lax.all_to_all(route_part, 'exp', split_axis=0, concat_axis=0, tiled=True)  63.5 us
    reduce_scatter x1, waiting for transfers between devices, attention_layer(): lax.psum_scatter(latent_part, ('ctx', 'exp'), scatter_dimension=0, tiled=...  53.1 us
    all_to_all x1, waiting for transfers between devices, expert_layer(): lax.all_to_all(send_grad, 'exp', split_axis=0, concat_axis=0, tiled=True)  41.9 us
    all_to_all x1, waiting for transfers between devices, expert_layer(): lax.all_to_all(send_input, 'exp', split_axis=0, concat_axis=0, tiled=True)  37.3 us
    scatter x1, local copies, waits for them, and re-layouts, expert_layer(): send_grad = empty.at[target].set(moe_grad[source_rows]).reshape(send_shape)  16 us
    scatter x1, local copies, waits for them, and re-layouts, expert_layer(): empty.at[target].set(moe_input[source_rows]).reshape(send_shape)  13.7 us
  transfers between devices with their start and end apart: 6, of which 5 were waited for; matrix products, arithmetic and copies ran while one was open for 14% of the time, Pallas kernels for 0%

commit v1 on v0

v1 whole, which is shorter than its diff:
```python
import functools

import jax
import jax.numpy as jnp
from jax import lax
from jax.experimental import pallas as pl
from jax.experimental.pallas import tpu as pltpu
from jax.sharding import PartitionSpec as P

SCORE_SCALE = 192.0 ** (-0.5)
MASKED = -1e30
BF16 = jnp.bfloat16
F32 = jnp.float32
META = 128
VMEM_LIMIT = 48 * 1024 * 1024


def swiglu_back(gate_pre, up_pre, hidden_grad):
    sigma = jax.nn.sigmoid(gate_pre)
    gate_back = hidden_grad * up_pre * sigma * (1.0 + gate_pre * (1.0 - sigma))
    up_back = hidden_grad * gate_pre * sigma
    return (gate_back.astype(BF16), up_back.astype(BF16))


def shift(value, axis, bits):
    count = lax.axis_size(axis)
    return lax.ppermute(value, axis, [(i, i ^ bits) for i in range(count)])


def dot(left, right):
    return jnp.dot(left, right, preferred_element_type=F32)


def dot_t(left, right):
    return lax.dot_general(left, right, (((1,), (1,)), ((), ())), preferred_element_type=F32)


def pack_kernel(experts, routes_ref, gates_ref, input_ref, grad_ref, out_ref):
    rows, width = input_ref.shape
    out_ref[:, :width] = input_ref[...]
    out_ref[:, width : 2 * width] = grad_ref[...]
    lane = lax.broadcasted_iota(jnp.int32, (rows, META), 1)
    expert = lane % experts
    section = lane // experts
    gate = jnp.zeros((rows, META), F32)
    named = jnp.zeros((rows, META), F32)
    for k in range(routes_ref.shape[1]):
        hit = routes_ref[:, k : k + 1] == expert
        gate = gate + jnp.where(hit, gates_ref[:, k : k + 1], 0.0)
        named = named + jnp.where(hit, 1.0, 0.0)
    low = lax.broadcasted_iota(jnp.int32, (rows, rows), 0)
    high = lax.broadcasted_iota(jnp.int32, (rows, rows), 1)
    before = jnp.where(high < low, 1.0, 0.0).astype(BF16)
    slot = jnp.where(named > 0.0, dot(before, named.astype(BF16)), -1.0)
    gate_high = gate.astype(BF16).astype(F32)
    meta = jnp.where(section == 0, gate_high, jnp.where(section == 1, gate - gate_high, slot))
    out_ref[:, 2 * width :] = meta.astype(BF16)


def pack_tokens(moe_input, moe_grad, routes, gates, experts):
    rows, width = moe_input.shape
    return pl.pallas_call(
        functools.partial(pack_kernel, experts),
        out_shape=jax.ShapeDtypeStruct((rows, 2 * width + META), BF16),
        compiler_params=pltpu.CompilerParams(vmem_limit_bytes=VMEM_LIMIT),
        cost_estimate=pl.CostEstimate(
            flops=2 * rows * rows * META, bytes_accessed=8 * rows * width, transcendentals=0
        ),
        name="pack_tokens",
    )(routes, gates, moe_input, moe_grad)


def fill_rows(plan_ref, expert, experts, capacity, token_refs, rows_ref):
    width = rows_ref.shape[-1]
    tokens = token_refs[0].shape[0]
    lane = lax.broadcasted_iota(jnp.int32, (16, META), 1)
    pick = jnp.where(lane == 2 * experts + plan_ref[0] + expert, 1.0, 0.0).astype(BF16)
    for b, token_ref in enumerate(token_refs):
        slot_of = dot_t(pick, token_ref[:, 2 * width :])[0:1, :].astype(jnp.int32)
        slot = lax.broadcasted_iota(jnp.int32, (capacity, tokens), 0)
        chosen = jnp.where(slot == slot_of, 1.0, 0.0).astype(BF16)
        part = pl.ds(b * capacity, capacity)
        rows_ref[expert, 0, part, :] = dot(chosen, token_ref[:, :width]).astype(BF16)
        rows_ref[expert, 1, part, :] = dot(chosen, token_ref[:, width : 2 * width]).astype(BF16)


def products_kernel(blocks, experts, capacity, plan_ref, *refs):
    expert, piece = pl.program_id(0), pl.program_id(1)
    if blocks:
        token_refs, refs = refs[:blocks], refs[blocks:]
        gate_ref, up_ref, down_ref, first_ref, second_ref, rows_ref = refs

        @pl.when(piece == 0)
        def _():
            fill_rows(plan_ref, expert, experts, capacity, token_refs, rows_ref)
    else:
        rows_ref, gate_ref, up_ref, down_ref, first_ref, second_ref = refs
    rows_in, rows_grad = rows_ref[expert, 0], rows_ref[expert, 1]
    gate = dot(rows_in, gate_ref[0]).astype(BF16)
    up = dot(rows_in, up_ref[0]).astype(BF16)
    down = dot_t(rows_grad, down_ref[0]).astype(BF16)

    def store(out_ref):
        out_ref[0, piece] = gate
        out_ref[1, piece] = up
        out_ref[2, piece] = down

    pl.when(expert == 0)(lambda: store(first_ref))
    pl.when(expert == 1)(lambda: store(second_ref))


def products(plan, base, tokens, rows, w_gate, w_up, w_down, capacity, experts):
    local, width, hidden = w_gate.shape
    quarter = hidden // 4
    blocks = len(tokens)
    slots = blocks * capacity if blocks else rows.shape[2]

    def column(e, j, plan_ref):
        return (e, 0, plan_ref[base + 2 * e + j])

    def line(e, j, plan_ref):
        return (e, plan_ref[base + 2 * e + j], 0)

    whole = pl.BlockSpec(memory_space=pltpu.VMEM)
    part_shape = jax.ShapeDtypeStruct((3, 2, slots, quarter), BF16)
    rows_shape = jax.ShapeDtypeStruct((local, 2, slots, width), BF16)

    def fixed(shape):
        return pl.BlockSpec(shape, lambda e, j, plan_ref: (0,) * len(shape))

    head = list(tokens) if blocks else [rows]
    out_shape = [part_shape, part_shape] + ([rows_shape] if blocks else [])
    return pl.pallas_call(
        functools.partial(products_kernel, blocks, experts, capacity),
        out_shape=out_shape,
        grid_spec=pltpu.PrefetchScalarGridSpec(
            num_scalar_prefetch=1,
            grid=(local, 2),
            in_specs=[fixed(a.shape) for a in head]
            + [
                pl.BlockSpec((1, width, quarter), column),
                pl.BlockSpec((1, width, quarter), column),
                pl.BlockSpec((1, quarter, width), line),
            ],
            out_specs=[fixed(s.shape) for s in out_shape],
        ),
        compiler_params=pltpu.CompilerParams(vmem_limit_bytes=VMEM_LIMIT),
        cost_estimate=pl.CostEstimate(
            flops=2 * local * 3 * slots * width * hidden // 2,
            bytes_accessed=2 * local * 3 * width * hidden // 2 + 4 * local * slots * width,
            transcendentals=0,
        ),
        name="products",
    )(plan, *head, w_gate, w_up, w_down)


def route_kernel(blocks, experts, capacity, plan_ref, *refs):
    expert, piece = pl.program_id(0), pl.program_id(1)
    meta_refs, refs = refs[:blocks], refs[blocks:]
    piece_refs, refs = refs[:8], refs[8:]
    gate_ref, up_ref = refs[:2]
    out_refs = refs[2 : 2 + blocks]
    route_ref, total_ref = refs[2 + blocks :]
    tokens = meta_refs[0].shape[0]

    def add(back_ref, first):
        value = dot_t(back_ref[0], gate_ref[0]) + dot_t(back_ref[1], up_ref[0])
        if first:
            route_ref[...] = value
        else:
            route_ref[...] += value

    for e in range(2):
        for p in range(4):
            pl.when((expert == e) & (piece == p))(
                functools.partial(add, piece_refs[4 * e + p], p == 0)
            )

    @pl.when(piece == 3)
    def _():
        row = lax.broadcasted_iota(jnp.int32, (META, META), 0)
        lane = lax.broadcasted_iota(jnp.int32, (META, META), 1)
        pick = jnp.where(lane == row * experts + plan_ref[0] + expert, 1.0, 0.0).astype(BF16)
        slot = lax.broadcasted_iota(jnp.int32, (tokens, capacity), 1)
        for b in range(blocks):
            found = dot_t(meta_refs[b][...], pick)
            mine = found[:, 2:3].astype(jnp.int32) == slot
            high = jnp.where(mine, found[:, 0:1], 0.0).astype(BF16)
            low = jnp.where(mine, found[:, 1:2], 0.0).astype(BF16)
            route = route_ref[pl.ds(b * capacity, capacity), :].astype(BF16)
            value = dot(high, route) + dot(low, route)

            @pl.when(expert == 0)
            def _():
                total_ref[b] = value

            @pl.when(expert == 1)
            def _():
                out_refs[b][...] = (total_ref[b] + value).astype(out_refs[b].dtype)


def route_sums(plan, base, tokens, pieces, w_gate, w_up, capacity, experts, out_type):
    local, width, hidden = w_gate.shape
    quarter = hidden // 4
    blocks = len(tokens)
    slots = blocks * capacity
    count = tokens[0].shape[0]
    meta_at = 2 * width // META

    def column(e, p, plan_ref):
        return (e, 0, plan_ref[base + 4 * e + p])

    def fixed(shape):
        return pl.BlockSpec(shape, lambda e, p, plan_ref: (0,) * len(shape))

    return pl.pallas_call(
        functools.partial(route_kernel, blocks, experts, capacity),
        out_shape=[jax.ShapeDtypeStruct((count, width), out_type)] * blocks,
        grid_spec=pltpu.PrefetchScalarGridSpec(
            num_scalar_prefetch=1,
            grid=(local, 4),
            in_specs=[pl.BlockSpec((count, META), lambda e, p, plan_ref: (0, meta_at))] * blocks
            + [fixed(a.shape) for a in pieces]
            + [pl.BlockSpec((1, width, quarter), column)] * 2,
            out_specs=[fixed((count, width))] * blocks,
            scratch_shapes=[pltpu.VMEM((slots, width), F32), pltpu.VMEM((blocks, count, width), F32)],
        ),
        compiler_params=pltpu.CompilerParams(vmem_limit_bytes=VMEM_LIMIT),
        cost_estimate=pl.CostEstimate(
            flops=2 * local * 2 * slots * width * hidden,
            bytes_accessed=2 * local * 2 * width * hidden + 4 * local * slots * hidden,
            transcendentals=0,
        ),
        name="route_sums",
    )(plan, *tokens, *pieces, w_gate, w_up)


def chunk_layer(plan, tokens, w_gate, w_up, w_down, capacity, experts, out_type):
    sent = products(plan, 1, tokens, None, w_gate, w_up, w_down, capacity, experts)
    rows = sent[2]
    kept = products(plan, 5, [], rows, w_gate, w_up, w_down, capacity, experts)
    pieces = []
    for e, (near, far) in enumerate(((1, 2), (2, 1))):
        got = shift(sent[e], "ctx", near)
        half = got.astype(F32) + kept[e].astype(F32)
        other = shift(half[:, 0].astype(BF16), "ctx", far)
        full = half[:, 1] + other.astype(F32)
        own = jnp.stack(swiglu_back(full[0], full[1], full[2]))
        from_far = shift(own, "ctx", far)
        from_near = shift(own, "ctx", near)
        from_both = shift(from_far, "ctx", near)
        pieces += [own, from_far, from_near, from_both]
    return route_sums(plan, 9, tokens, pieces, w_gate, w_up, capacity, experts, out_type)


def near_expert_layer(moe_input, moe_grad, routes, gates, w_gate, w_up, w_down):
    tok_rows = moe_input.shape[0]
    fanout = routes.shape[1]
    local = w_gate.shape[0]
    exp_count = lax.axis_size("exp")
    experts = local * exp_count
    capacity = tok_rows * fanout // experts * 5 // 4
    ctx = lax.axis_index("ctx")
    x, y = ctx % 2, ctx // 2
    plan = jnp.stack(
        [
            lax.axis_index("exp") * local,
            (1 - x) * 2 + 1 - y,
            (1 - x) * 2 + y,
            (1 - y) * 2 + 1 - x,
            (1 - y) * 2 + x,
            x * 2 + 1 - y,
            x * 2 + y,
            y * 2 + 1 - x,
            y * 2 + x,
            x * 2 + y,
            x * 2 + 1 - y,
            (1 - x) * 2 + y,
            (1 - x) * 2 + 1 - y,
            y * 2 + x,
            y * 2 + 1 - x,
            (1 - y) * 2 + x,
            (1 - y) * 2 + 1 - x,
        ]
    ).astype(jnp.int32)
    own = pack_tokens(moe_input, moe_grad, routes, gates, experts)
    layer = functools.partial(
        chunk_layer, plan, w_gate=w_gate, w_up=w_up, w_down=w_down, capacity=capacity, experts=experts
    )
    far_tokens = {bits: shift(own, "exp", bits) for bits in range(2, exp_count, 2)}
    partner = shift(own, "exp", 1)
    far_pairs = {bits: [value, shift(value, "exp", 1)] for bits, value in far_tokens.items()}
    total = layer([own], out_type=F32)[0]
    for bits, pair in far_pairs.items():
        mine, theirs = layer(pair, out_type=BF16)
        both = mine.astype(F32) + shift(theirs, "exp", 1).astype(F32)
        total = total + shift(both.astype(BF16), "exp", bits).astype(F32)
    total = total + shift(layer([partner], out_type=BF16)[0], "exp", 1).astype(F32)
    return total.astype(BF16)


def far_expert_layer(moe_input, moe_grad, routes, gates, w_gate, w_up, w_down):
    tok_rows, width_part = moe_input.shape
    fanout = routes.shape[1]
    local_experts = w_gate.shape[0]
    exp_count = lax.axis_size("exp")
    experts = local_experts * exp_count
    capacity = tok_rows * fanout // experts * 5 // 4
    flat_routes = routes.reshape(-1)
    onehot = (flat_routes[:, None] == jnp.arange(experts, dtype=jnp.int32)[None, :]).astype(
        jnp.int32
    )
    before = jnp.cumsum(onehot, axis=0) - onehot
    slot_index = jnp.sum(before * onehot, axis=1)
    target = flat_routes * capacity + slot_index
    source_rows = jnp.arange(tok_rows * fanout, dtype=jnp.int32) // fanout
    empty = jnp.zeros((experts * capacity, width_part), BF16)
    send_shape = (exp_count, local_experts * capacity, width_part)
    send_input = empty.at[target].set(moe_input[source_rows]).reshape(send_shape)
    send_grad = empty.at[target].set(moe_grad[source_rows]).reshape(send_shape)
    recv_input, recv_grad = (
        lax.all_to_all(send_input, "exp", split_axis=0, concat_axis=0, tiled=True),
        lax.all_to_all(send_grad, "exp", split_axis=0, concat_axis=0, tiled=True),
    )
    slot_shape = (exp_count, local_experts, capacity, width_part)
    recv_input = recv_input.reshape(slot_shape)
    recv_grad = recv_grad.reshape(slot_shape)
    gate_part = jnp.einsum("sekd,edh->sekh", recv_input, w_gate, preferred_element_type=F32)
    up_part = jnp.einsum("sekd,edh->sekh", recv_input, w_up, preferred_element_type=F32)
    down_part = jnp.einsum("sekd,ehd->sekh", recv_grad, w_down, preferred_element_type=F32)
    gate_pre, up_pre, hidden_grad = (
        lax.psum(gate_part.astype(BF16), "ctx").astype(F32),
        lax.psum(up_part.astype(BF16), "ctx").astype(F32),
        lax.psum(down_part.astype(BF16), "ctx").astype(F32),
    )
    gate_back, up_back = swiglu_back(gate_pre, up_pre, hidden_grad)
    route_part = jnp.einsum("sekh,edh->sekd", gate_back, w_gate, preferred_element_type=F32)
    route_part = route_part + jnp.einsum(
        "sekh,edh->sekd", up_back, w_up, preferred_element_type=F32
    )
    route_part = route_part.astype(BF16).reshape(send_shape)
    returned = lax.all_to_all(route_part, "exp", split_axis=0, concat_axis=0, tiled=True).reshape(
        experts * capacity, width_part
    )
    per_route = returned[target].reshape(tok_rows, fanout, width_part).astype(F32)
    return jnp.sum(per_route * gates[:, :, None], axis=1).astype(BF16)


def gather_latents(latents):
    across = shift(latents, "ctx", 1)
    along = shift(latents, "ctx", 2)
    return jnp.concatenate([latents, across, along, shift(along, "ctx", 1)], axis=0)


def sum_latent_grad(part):
    shards, keys, width = part.shape
    exp_count = lax.axis_size("exp")
    if exp_count > 8:
        ctx = lax.axis_index("ctx")
        order = jnp.arange(shards) ^ ctx
        whole = part[order].reshape(shards * keys, width)
        return lax.psum_scatter(whole, ("ctx", "exp"), scatter_dimension=0, tiled=True)
    me = lax.axis_index("exp")
    core, chip = me % 2, me // 2
    part = part.reshape(shards, exp_count // 2, 2, keys // exp_count, width)
    keep = lax.dynamic_index_in_dim(part, core, axis=2, keepdims=False)
    give = lax.dynamic_index_in_dim(part, 1 - core, axis=2, keepdims=False).astype(BF16)
    part = keep + shift(give, "exp", 1).astype(F32)
    total = lax.dynamic_index_in_dim(part, chip, axis=1, keepdims=False)
    for bits in range(1, exp_count // 2):
        give = lax.dynamic_index_in_dim(part, chip ^ bits, axis=1, keepdims=False).astype(BF16)
        total = total + shift(give, "exp", 2 * bits).astype(F32)
    out = total[0]
    for bits in range(1, shards):
        out = out + shift(total[bits].astype(BF16), "ctx", bits).astype(F32)
    return out


def attention_layer(queries, out_grad, positions, latents):
    q_rows = queries.shape[0]
    keys, lat_width = latents.shape
    shards = lax.axis_size("ctx")
    head_count = queries.shape[1] // lat_width
    val_width = out_grad.shape[1] // head_count
    query_heads = queries.reshape(q_rows, head_count, lat_width)
    grad_heads = out_grad.reshape(q_rows, head_count, val_width)
    gathered = gather_latents(latents)
    shard_of = jnp.arange(shards, dtype=jnp.int32) ^ lax.axis_index("ctx")
    key_ids = (shard_of[:, None] * keys + jnp.arange(keys, dtype=jnp.int32)[None, :]).reshape(-1)
    visible = (key_ids[None, :] <= positions[:, None])[None]
    scores = (
        jnp.einsum("qhc,kc->hqk", query_heads, gathered, preferred_element_type=F32) * SCORE_SCALE
    )
    scores = jnp.where(visible, scores, MASKED)
    peak = jnp.max(scores, axis=2, keepdims=True)
    raw = jnp.where(visible, jnp.exp(scores - peak), 0.0)
    attend = raw / jnp.sum(raw, axis=2, keepdims=True)
    value_dot = jnp.einsum(
        "qhv,kv->hqk", grad_heads, gathered[:, :val_width], preferred_element_type=F32
    )
    row_dot = jnp.sum(attend * value_dot, axis=2, keepdims=True)
    score_grad = (attend * (value_dot - row_dot)).astype(BF16)
    query_grad = (
        jnp.einsum("hqk,kc->qhc", score_grad, gathered, preferred_element_type=F32) * SCORE_SCALE
    )
    key_grad = (
        jnp.einsum("hqk,qhc->kc", score_grad, query_heads, preferred_element_type=F32)
        * SCORE_SCALE
    )
    value_grad = jnp.einsum(
        "hqk,qhv->kv", attend.astype(BF16), grad_heads, preferred_element_type=F32
    )
    latent_part = key_grad + jnp.pad(value_grad, ((0, 0), (0, lat_width - val_width)))
    latent_grad = sum_latent_grad(latent_part.reshape(shards, keys, lat_width))
    query_out = query_grad.astype(BF16).reshape(q_rows, head_count * lat_width)
    return (query_out, latent_grad)


def per_device(
    moe_input, moe_grad, routes, gates, w_gate, w_up, w_down, queries, out_grad, positions, latents
):
    near = lax.axis_size("exp") <= routes.shape[1]
    expert_layer = near_expert_layer if near else far_expert_layer
    query_out, latent_grad = attention_layer(queries, out_grad, positions, latents)
    input_grad = expert_layer(moe_input, moe_grad, routes, gates, w_gate, w_up, w_down)
    return (input_grad, query_out, latent_grad)


def solution(mesh):
    return jax.shard_map(
        per_device,
        mesh=mesh,
        in_specs=(
            P("exp", "ctx"),
            P("exp", "ctx"),
            P("exp", None),
            P("exp", None),
            P("exp", "ctx", None),
            P("exp", "ctx", None),
            P("exp", None, "ctx"),
            P("ctx", "exp"),
            P("ctx", "exp"),
            P("ctx"),
            P("ctx", None),
        ),
        out_specs=(P("exp", "ctx"), P("ctx", "exp"), P(("ctx", "exp"), None)),
        check_vma=False,
    )
```

time: 469 us -> 298 us (0.64)
  waiting for transfers between devices: 353 us -> 69.1 us
  Pallas kernels: 0 us -> 102 us
  starting transfers between devices: 15.8 us -> 76.8 us
  matrix products: 35.9 us -> 9.1 us
  local copies, waits for them, and re-layouts: 41.2 us -> 27.1 us
  between operations: 13.9 us -> 1.65 us
    psum x1 -> x0, waiting for transfers between devices: 156 us -> none  [expert_layer(): lax.psum(down_part.astype(jnp.bfloat16), 'ctx').astype(jnp.float32)]
    all_to_all x3 -> x0, waiting for transfers between devices: 143 us -> none  [the longest x1 63.5 us: expert_layer(): lax.all_to_all(route_part, 'exp', split_axis=0, concat_axis=0, tiled=True)]
    pallas_call x0 -> x16, Pallas kernels: none -> 102 us  [the longest x10 53.5 us: products(): pl.pallas_call(functools.partial(products_kernel, blocks, experts, capaci...]
    ppermute x0 -> x74, starting transfers between devices: none -> 76.8 us  [shift(): return lax.ppermute(value, axis, [(i, i ^ bits) for i in range(count)])]
    ppermute x0 -> x74, waiting for transfers between devices: none -> 69.1 us  [shift(): return lax.ppermute(value, axis, [(i, i ^ bits) for i in range(count)])]
    reduce_scatter x1 -> x0, waiting for transfers between devices: 53.1 us -> none  [attention_layer(): lax.psum_scatter(latent_part, ('ctx', 'exp'), scatter_dimension=0, tiled=...]
    scatter x2 -> x0, local copies, waits for them, and re-layouts: 29.7 us -> none  [the longest x1 16 us: expert_layer(): send_grad = empty.at[target].set(moe_grad[source_rows]).reshape(send_shape)]
    dot_general x7 -> x2, matrix products: 31.1 us -> 1.68 us  [the longest x1 1.2 us: attention_layer(): jnp.einsum('hqk,kc->qhc', score_grad, gathered, preferred_element_type=F32)]
  transfers between devices with their start and end apart: 6 -> 74, of which waited for: 5 -> 20; matrix products, arithmetic and copies ran while one was open for 14% -> 12% of each run, Pallas kernels for 0% -> 34%
where the time goes in v1:
time: 298 us; the launch traced here: 296 us
  Pallas kernels  102 us (34%)
  starting transfers between devices  76.8 us (26%)
  waiting for transfers between devices  69.1 us (23%)
  local copies, waits for them, and re-layouts  27.1 us (9%)
  other arithmetic  11.1 us (4%)
  matrix products  9.1 us (3%)
    ppermute x74, starting transfers between devices, shift(): return lax.ppermute(value, axis, [(i, i ^ bits) for i in range(count)])  76.8 us
    ppermute x74, waiting for transfers between devices, shift(): return lax.ppermute(value, axis, [(i, i ^ bits) for i in range(count)])  69.1 us
    pallas_call x10, Pallas kernels, products(): pl.pallas_call(functools.partial(products_kernel, blocks, experts, capaci...  53.5 us
    pallas_call x5, Pallas kernels, route_sums(): pl.pallas_call(functools.partial(route_kernel, blocks, experts, capacity)...  47.6 us
    unnamed x58, local copies, waits for them, and re-layouts  16.4 us
    add x10, other arithmetic, chunk_layer(): half = got.astype(F32) + kept[e].astype(F32)  6.86 us
  transfers between devices with their start and end apart: 74, of which 20 were waited for; matrix products, arithmetic and copies ran while one was open for 12% of the time, Pallas kernels for 34%

profile of v1, /device:TPU:0, one launch (start us, length us, event | category | flops | bytes accessed | tf_op | source)
XLA Modules:
  0.0 296.3 jit_solution(15135097543622544755)
XLA Ops:
  11.3 5.5 %products.10 = (bf16[3,2,80,256]{3,2,1,0:T(8,128)(2,1)S(1)}, bf16[3,2,80,256]{3,2,1,0:T(8,128)(2,1)S(1)}, bf16[2,2,80,896]{3,2,1,0:T(8,128)(2,1)S(1)}) custom-call(s32[17]{0:T(128)S(1)} %stack.97.plan_ref, bf16[128,1920]{1,0:T(8,128)(2,1)S(1)} %pack_tokens.1.refs_0_, bf16[2,896,1024]{2,1,0:T(8,128)(2,1)S(1)} %copy-done, bf16[2,896,1024]{2,1,0:T(8,128)(2,1)} %refs_10_.9, ...), custom_call_target="tpu_custom_call" | custom-call | flops 440401920 | bytes 6078464 | tf_op jit(solution)/shard_map/products/pallas_call | solution.py:133
  17.7 4.5 %products.11 = (bf16[3,2,80,256]{3,2,1,0:T(8,128)(2,1)S(1)}, bf16[3,2,80,256]{3,2,1,0:T(8,128)(2,1)S(1)}) custom-call(s32[17]{0:T(128)S(1)} %stack.97.plan_ref, bf16[2,2,80,896]{3,2,1,0:T(8,128)(2,1)S(1)} %get-tuple-element.35.refs_0_, bf16[2,896,1024]{2,1,0:T(8,128)(2,1)S(1)} %copy-done.1, bf16[2,896,1024]{2,1,0:T(8,128)(2,1)} %refs_10_.9, ...), custom_call_target="tpu_custom_call" | custom-call | flops 440401920 | bytes 6078464 | tf_op jit(solution)/shard_map/products/pallas_call | solution.py:133
  22.2 3.0 %collective-permute-done = bf16[3,2,80,256]{3,2,0,1:T(8,128)(2,1)S(1)} collective-permute-done((bf16[3,2,80,256]{3,2,0,1:T(8,128)(2,1)S(1)}, bf16[3,2,80,256]{3,2,0,1:T(8,128)(2,1)S(1)}, u32[]{:S(2)}, u32[]{:S(2)}) %collective-permute-start) | collective-permute-done | bytes 245792 | tf_op jit(solution)/shard_map/ppermute | solution.py:27
  27.2 3.0 %collective-permute-done.1 = bf16[3,80,256]{2,1,0:T(8,128)(2,1)S(1)} collective-permute-done((bf16[3,80,256]{2,1,0:T(8,128)(2,1)S(1)}, bf16[3,80,256]{2,1,0:T(8,128)(2,1)S(1)}, u32[]{:S(2)}, u32[]{:S(2)}) %collective-permute-start.1) | collective-permute-done | bytes 122912 | tf_op jit(solution)/shard_map/ppermute | solution.py:27
  35.8 3.6 %collective-permute-start.38 = (bf16[128,1920]{1,0:T(8,128)(2,1)S(1)}, bf16[128,1920]{1,0:T(8,128)(2,1)S(1)}, u32[]{:S(2)}, u32[]{:S(2)}) collective-permute-start(bf16[128,1920]{1,0:T(8,128)(2,1)S(1)} %pack_tokens.1.refs_0_), channel_id=1, source_target_pairs={{0,6},{1,7},{2,4},{3,5},{4,2},{5,3},{6,0},{7,1},{8,14},{9,15},{10,... | collective-permute-start | bytes 1474568 | tf_op jit(solution)/shard_map/ppermute | solution.py:27
  48.7 3.7 %collective-permute-done.4.refs_4_ = bf16[2,80,256]{2,1,0:T(8,128)(2,1)S(1)} collective-permute-done((bf16[2,80,256]{2,1,0:T(8,128)(2,1)S(1)}, bf16[2,80,256]{2,1,0:T(8,128)(2,1)S(1)}, u32[]{:S(2)}, u32[]{:S(2)}) %collective-permute-start.4) | collective-permute-done | bytes 81952 | tf_op jit(solution)/shard_map/ppermute | solution.py:27
  56.0 5.5 %products.18 = (bf16[3,2,80,256]{3,2,1,0:T(8,128)(2,1)S(1)}, bf16[3,2,80,256]{3,2,1,0:T(8,128)(2,1)S(1)}, bf16[2,2,80,896]{3,2,1,0:T(8,128)(2,1)S(1)}) custom-call(s32[17]{0:T(128)S(1)} %stack.97.plan_ref, bf16[128,1920]{1,0:T(8,128)(2,1)S(1)} %collective-permute-done.52.refs_0_, bf16[2,896,1024]{2,1,0:T(8,128)(2,1)S(1)} %copy-done.2, ...), custom_call_target="tpu_custom_call" | custom-call | flops 440401920 | bytes 6078464 | tf_op jit(solution)/shard_map/products/pallas_call | solution.py:133
  62.9 4.5 %products.19 = (bf16[3,2,80,256]{3,2,1,0:T(8,128)(2,1)S(1)}, bf16[3,2,80,256]{3,2,1,0:T(8,128)(2,1)S(1)}) custom-call(s32[17]{0:T(128)S(1)} %stack.97.plan_ref, bf16[2,2,80,896]{3,2,1,0:T(8,128)(2,1)S(1)} %get-tuple-element.61.refs_0_, bf16[2,896,1024]{2,1,0:T(8,128)(2,1)S(1)} %copy-done.3, bf16[2,896,1024]{2,1,0:T(8,128)(2,1)} %refs_10_.9, ...), custom_call_target="tpu_custom_call" | custom-call | flops 440401920 | bytes 6078464 | tf_op jit(solution)/shard_map/products/pallas_call | solution.py:133
  69.4 8.5 %route_sums.5 = f32[128,896]{1,0:T(8,128)S(1)} custom-call(s32[17]{0:T(128)S(1)} %stack.97.plan_ref, bf16[128,1920]{1,0:T(8,128)(2,1)S(1)} %pack_tokens.1.refs_0_, bf16[2,80,256]{2,1,0:T(8,128)(2,1)S(1)} %pad_maximum_fusion.6.refs_1_, bf16[2,80,256]{2,1,0:T(8,128)(2,1)S(1)} %collective-permute-done.2.refs_2_, ...), custom_call_target="tpu_custom_call" | custom-call | flops 587202560 | bytes 7995392 | tf_op jit(solution)/shard_map/route_sums/pallas_call | solution.py:216
  81.5 3.3 %fusion.72 = (f32[2,128]{1,0:T(2,128)S(1)}, f32[2,128,1024]{1,2,0:T(8,128)}) fusion(pred[128,1024]{0,1:T(8,128)(4,1)} %broadcast_compare_fusion, bf16[128,2,576]{0,2,1:T(8,128)(2,1)} %bitcast.151, bf16[1024,576]{0,1:T(8,128)(2,1)} %copy-done.22), kind=kOutput, calls=%fused_computation.171 | convolution fusion | flops 303301632 | bytes 2655232 | tf_op jit(solution)/shard_map/sub | solution.py:396
  93.4 3.2 %copy.76 = f32[1024,576]{1,0:T(8,128)} copy(f32[1024,576]{0,1:T(8,128)} %fusion.1) | data formatting | bytes 4718592 | tf_op jit(solution)/shard_map/add | solution.py:413
  101.8 3.2 %collective-permute-done.54 = bf16[3,80,256]{2,1,0:T(8,128)(2,1)S(1)} collective-permute-done((bf16[3,80,256]{2,1,0:T(8,128)(2,1)S(1)}, bf16[3,80,256]{2,1,0:T(8,128)(2,1)S(1)}, u32[]{:S(2)}, u32[]{:S(2)}) %collective-permute-start.54) | collective-permute-done | bytes 122912 | tf_op jit(solution)/shard_map/ppermute | solution.py:27
  105.9 3.9 %collective-permute-done.59 = bf16[3,80,256]{2,1,0:T(8,128)(2,1)S(1)} collective-permute-done((bf16[3,80,256]{2,1,0:T(8,128)(2,1)S(1)}, bf16[3,80,256]{2,1,0:T(8,128)(2,1)S(1)}, u32[]{:S(2)}, u32[]{:S(2)}) %collective-permute-start.59) | collective-permute-done | bytes 122912 | tf_op jit(solution)/shard_map/ppermute | solution.py:27
  112.4 6.3 %products.16 = (bf16[3,2,160,256]{3,2,1,0:T(8,128)(2,1)S(1)}, bf16[3,2,160,256]{3,2,1,0:T(8,128)(2,1)S(1)}, bf16[2,2,160,896]{3,2,1,0:T(8,128)(2,1)S(1)}) custom-call(s32[17]{0:T(128)S(1)} %stack.97.plan_ref, bf16[128,1920]{1,0:T(8,128)(2,1)S(1)} %collective-permute-done.38.refs_0_, bf16[128,1920]{1,0:T(8,128)(2,1)S(1)} %collective-permute-done.39.refs_1_, ...), custom_call_target="tpu_custom_call" | custom-call | flops 880803840 | bytes 6651904 | tf_op jit(solution)/shard_map/products/pallas_call | solution.py:133
  118.8 5.0 %products.17 = (bf16[3,2,160,256]{3,2,1,0:T(8,128)(2,1)S(1)}, bf16[3,2,160,256]{3,2,1,0:T(8,128)(2,1)S(1)}) custom-call(s32[17]{0:T(128)S(1)} %stack.97.plan_ref, bf16[2,2,160,896]{3,2,1,0:T(8,128)(2,1)S(1)} %get-tuple-element.54.refs_0_, bf16[2,896,1024]{2,1,0:T(8,128)(2,1)S(1)} %copy-done.4, bf16[2,896,1024]{2,1,0:T(8,128)(2,1)} %refs_10_.9, ...), custom_call_target="tpu_custom_call" | custom-call | flops 880803840 | bytes 6651904 | tf_op jit(solution)/shard_map/products/pallas_call | solution.py:133
  124.5 6.3 %products.14 = (bf16[3,2,160,256]{3,2,1,0:T(8,128)(2,1)S(1)}, bf16[3,2,160,256]{3,2,1,0:T(8,128)(2,1)S(1)}, bf16[2,2,160,896]{3,2,1,0:T(8,128)(2,1)S(1)}) custom-call(s32[17]{0:T(128)S(1)} %stack.97.plan_ref, bf16[128,1920]{1,0:T(8,128)(2,1)S(1)} %collective-permute-done.24.refs_0_, bf16[128,1920]{1,0:T(8,128)(2,1)S(1)} %collective-permute-done.25.refs_1_, ...), custom_call_target="tpu_custom_call" | custom-call | flops 880803840 | bytes 6651904 | tf_op jit(solution)/shard_map/products/pallas_call | solution.py:133
  130.8 4.8 %products.15 = (bf16[3,2,160,256]{3,2,1,0:T(8,128)(2,1)S(1)}, bf16[3,2,160,256]{3,2,1,0:T(8,128)(2,1)S(1)}) custom-call(s32[17]{0:T(128)S(1)} %stack.97.plan_ref, bf16[2,2,160,896]{3,2,1,0:T(8,128)(2,1)S(1)} %get-tuple-element.47.refs_0_, bf16[2,896,1024]{2,1,0:T(8,128)(2,1)S(1)} %copy-done.5, bf16[2,896,1024]{2,1,0:T(8,128)(2,1)} %refs_10_.9, ...), custom_call_target="tpu_custom_call" | custom-call | flops 880803840 | bytes 6651904 | tf_op jit(solution)/shard_map/products/pallas_call | solution.py:133
  139.1 6.3 %products.12 = (bf16[3,2,160,256]{3,2,1,0:T(8,128)(2,1)S(1)}, bf16[3,2,160,256]{3,2,1,0:T(8,128)(2,1)S(1)}, bf16[2,2,160,896]{3,2,1,0:T(8,128)(2,1)S(1)}) custom-call(s32[17]{0:T(128)S(1)} %stack.97.plan_ref, bf16[128,1920]{1,0:T(8,128)(2,1)S(1)} %collective-permute-done.10.refs_0_, bf16[128,1920]{1,0:T(8,128)(2,1)S(1)} %collective-permute-done.11.refs_1_, ...), custom_call_target="tpu_custom_call" | custom-call | flops 880803840 | bytes 6651904 | tf_op jit(solution)/shard_map/products/pallas_call | solution.py:133
  146.2 4.8 %products.13 = (bf16[3,2,160,256]{3,2,1,0:T(8,128)(2,1)S(1)}, bf16[3,2,160,256]{3,2,1,0:T(8,128)(2,1)S(1)}) custom-call(s32[17]{0:T(128)S(1)} %stack.97.plan_ref, bf16[2,2,160,896]{3,2,1,0:T(8,128)(2,1)S(1)} %get-tuple-element.40.refs_0_, bf16[2,896,1024]{2,1,0:T(8,128)(2,1)S(1)} %copy-done.6, bf16[2,896,1024]{2,1,0:T(8,128)(2,1)} %refs_10_.9, ...), custom_call_target="tpu_custom_call" | custom-call | flops 880803840 | bytes 6651904 | tf_op jit(solution)/shard_map/products/pallas_call | solution.py:133
  157.8 8.5 %route_sums.9 = bf16[128,896]{1,0:T(8,128)(2,1)S(1)} custom-call(s32[17]{0:T(128)S(1)} %stack.97.plan_ref, bf16[128,1920]{1,0:T(8,128)(2,1)S(1)} %collective-permute-done.52.refs_0_, bf16[2,80,256]{2,1,0:T(8,128)(2,1)S(1)} %pad_maximum_fusion.8.refs_1_, bf16[2,80,256]{2,1,0:T(8,128)(2,1)S(1)} %collective-permute-done.55.refs_2_, ...), custom_call_target="tpu_custom_call" | custom-call | flops 587202560 | bytes 7995392 | tf_op jit(solution)/shard_map/route_sums/pallas_call | solution.py:216
  169.5 3.7 %collective-permute-start.70 = (bf16[4,32,576]{2,1,0:T(8,128)(2,1)S(1)}, bf16[4,32,576]{2,1,0:T(8,128)(2,1)S(1)}, u32[]{:S(2)}, u32[]{:S(2)}) collective-permute-start(bf16[4,32,576]{2,1,0:T(8,128)(2,1)S(1)} %get-tuple-element.74), channel_id=1, source_target_pairs={{0,6},{1,7},{2,4},{3,5},{4,2},{5,3},{6,0},{7,1},{8,14},{9,15},{10,... | collective-permute-start | bytes 442376 | tf_op jit(solution)/shard_map/ppermute | solution.py:27
  175.5 3.9 %collective-permute-done.31 = bf16[3,2,160,256]{3,2,0,1:T(8,128)(2,1)} collective-permute-done((bf16[3,2,160,256]{3,2,0,1:T(8,128)(2,1)}, bf16[3,2,160,256]{3,2,0,1:T(8,128)(2,1)}, u32[]{:S(2)}, u32[]{:S(2)}) %collective-permute-start.31) | collective-permute-done | bytes 491552 | tf_op jit(solution)/shard_map/ppermute | solution.py:27
  183.1 4.4 %collective-permute-done.17 = bf16[3,2,160,256]{3,2,0,1:T(8,128)(2,1)S(1)} collective-permute-done((bf16[3,2,160,256]{3,2,0,1:T(8,128)(2,1)S(1)}, bf16[3,2,160,256]{3,2,0,1:T(8,128)(2,1)S(1)}, u32[]{:S(2)}, u32[]{:S(2)}) %collective-permute-start.17) | collective-permute-done | bytes 491552 | tf_op jit(solution)/shard_map/ppermute | solution.py:27
  189.1 3.3 %collective-permute-done.41 = bf16[3,160,256]{2,1,0:T(8,128)(2,1)S(1)} collective-permute-done((bf16[3,160,256]{2,1,0:T(8,128)(2,1)S(1)}, bf16[3,160,256]{2,1,0:T(8,128)(2,1)S(1)}, u32[]{:S(2)}, u32[]{:S(2)}) %collective-permute-start.41) | collective-permute-done | bytes 245792 | tf_op jit(solution)/shard_map/ppermute | solution.py:27
  195.3 5.5 %collective-permute-done.27 = bf16[3,160,256]{2,1,0:T(8,128)(2,1)S(1)} collective-permute-done((bf16[3,160,256]{2,1,0:T(8,128)(2,1)S(1)}, bf16[3,160,256]{2,1,0:T(8,128)(2,1)S(1)}, u32[]{:S(2)}, u32[]{:S(2)}) %collective-permute-start.27) | collective-permute-done | bytes 245792 | tf_op jit(solution)/shard_map/ppermute | solution.py:27
  203.0 6.2 %collective-permute-done.13 = bf16[3,160,256]{2,1,0:T(8,128)(2,1)S(1)} collective-permute-done((bf16[3,160,256]{2,1,0:T(8,128)(2,1)S(1)}, bf16[3,160,256]{2,1,0:T(8,128)(2,1)S(1)}, u32[]{:S(2)}, u32[]{:S(2)}) %collective-permute-start.13) | collective-permute-done | bytes 245792 | tf_op jit(solution)/shard_map/ppermute | solution.py:27
  230.4 10.4 %route_sums.8 = (bf16[128,896]{1,0:T(8,128)(2,1)S(1)}, bf16[128,896]{1,0:T(8,128)(2,1)S(1)}) custom-call(s32[17]{0:T(128)S(1)} %stack.97.plan_ref, bf16[128,1920]{1,0:T(8,128)(2,1)S(1)} %collective-permute-done.38.refs_0_, bf16[128,1920]{1,0:T(8,128)(2,1)S(1)} %collective-permute-done.39.refs_1_, bf16[2,160,256]{2,1,0:T(8,128)(2,1)S(1)} %pad_maximum_fusion.4.refs_2_, ...), custom_call_target="tpu_custom_call" | custom-call | flops 1174405120 | bytes 8650752 | tf_op jit(solution)/shard_map/route_sums/pallas_call | solution.py:216
  244.9 10.1 %route_sums.7 = (bf16[128,896]{1,0:T(8,128)(2,1)S(1)}, bf16[128,896]{1,0:T(8,128)(2,1)S(1)}) custom-call(s32[17]{0:T(128)S(1)} %stack.97.plan_ref, bf16[128,1920]{1,0:T(8,128)(2,1)S(1)} %collective-permute-done.24.refs_0_, bf16[128,1920]{1,0:T(8,128)(2,1)S(1)} %collective-permute-done.25.refs_1_, bf16[2,160,256]{2,1,0:T(8,128)(2,1)S(1)} %pad_maximum_fusion.2.refs_2_, ...), custom_call_target="tpu_custom_call" | custom-call | flops 1174405120 | bytes 8650752 | tf_op jit(solution)/shard_map/route_sums/pallas_call | solution.py:216
  259.1 10.1 %route_sums.6 = (bf16[128,896]{1,0:T(8,128)(2,1)S(1)}, bf16[128,896]{1,0:T(8,128)(2,1)S(1)}) custom-call(s32[17]{0:T(128)S(1)} %stack.97.plan_ref, bf16[128,1920]{1,0:T(8,128)(2,1)S(1)} %collective-permute-done.10.refs_0_, bf16[128,1920]{1,0:T(8,128)(2,1)S(1)} %collective-permute-done.11.refs_1_, bf16[2,160,256]{2,1,0:T(8,128)(2,1)S(1)} %pad_maximum_fusion.refs_2_, ...), custom_call_target="tpu_custom_call" | custom-call | flops 1174405120 | bytes 8650752 | tf_op jit(solution)/shard_map/route_sums/pallas_call | solution.py:216
  272.3 3.6 %collective-permute-start.51 = (bf16[128,896]{1,0:T(8,128)(2,1)S(1)}, bf16[128,896]{1,0:T(8,128)(2,1)S(1)}, u32[]{:S(2)}, u32[]{:S(2)}) collective-permute-start(bf16[128,896]{1,0:T(8,128)(2,1)S(1)} %add_convert_fusion.1), channel_id=1, source_target_pairs={{0,6},{1,7},{2,4},{3,5},{4,2},{5,3},{6,0},{7,1},{8,14},{9,15},{10,... | collective-permute-start | bytes 688136 | tf_op jit(solution)/shard_map/ppermute | solution.py:27
  277.5 5.2 %collective-permute-done.51 = bf16[128,896]{1,0:T(8,128)(2,1)S(1)} collective-permute-done((bf16[128,896]{1,0:T(8,128)(2,1)S(1)}, bf16[128,896]{1,0:T(8,128)(2,1)S(1)}, u32[]{:S(2)}, u32[]{:S(2)}) %collective-permute-start.51) | collective-permute-done | bytes 229408 | tf_op jit(solution)/shard_map/ppermute | solution.py:27
  282.7 12.8 %collective-permute-done.37 = bf16[128,896]{1,0:T(8,128)(2,1)S(1)} collective-permute-done((bf16[128,896]{1,0:T(8,128)(2,1)S(1)}, bf16[128,896]{1,0:T(8,128)(2,1)S(1)}, u32[]{:S(2)}, u32[]{:S(2)}) %collective-permute-start.37) | collective-permute-done | bytes 229408 | tf_op jit(solution)/shard_map/ppermute | solution.py:27
  (273 shorter events, 118.2 us)
Async XLA Ops:
  0.6 31.6 %collective-permute-start.64 = (bf16[256,576]{0,1:T(8,128)(2,1)}, bf16[256,576]{0,1:T(8,128)(2,1)}, u32[]{:S(2)}, u32[]{:S(2)}) collective-permute-start(bf16[256,576]{0,1:T(8,128)(2,1)} %param.21), channel_id=1, source_target_pairs={{0,8},{8,0},{16,24},{24,16},{1,9},{9,1},{17,25},{25,17},{2,10},{10... | collective-permute-start | bytes 884744 | tf_op jit(solution)/shard_map/ppermute | solution.py:27
  3.6 32.1 %collective-permute-start.65 = (bf16[256,576]{0,1:T(8,128)(2,1)}, bf16[256,576]{0,1:T(8,128)(2,1)}, u32[]{:S(2)}, u32[]{:S(2)}) collective-permute-start(bf16[256,576]{0,1:T(8,128)(2,1)} %param.21), channel_id=1, source_target_pairs={{0,16},{8,24},{16,0},{24,8},{1,17},{9,25},{17,1},{25,9},{2,18},{10... | collective-permute-start | bytes 884744 | tf_op jit(solution)/shard_map/ppermute | solution.py:27
  9.1 37.7 %collective-permute-start.52 = (bf16[128,1920]{1,0:T(8,128)(2,1)S(1)}, bf16[128,1920]{1,0:T(8,128)(2,1)S(1)}, u32[]{:S(2)}, u32[]{:S(2)}) collective-permute-start(bf16[128,1920]{1,0:T(8,128)(2,1)S(1)} %pack_tokens.1.refs_0_), channel_id=1, source_target_pairs={{0,1},{1,0},{2,3},{3,2},{4,5},{5,4},{6,7},{7,6},{8,9},{9,8},{10,11... | collective-permute-start | bytes 1474568 | tf_op jit(solution)/shard_map/ppermute | solution.py:27
  35.8 42.9 %collective-permute-start.38 = (bf16[128,1920]{1,0:T(8,128)(2,1)S(1)}, bf16[128,1920]{1,0:T(8,128)(2,1)S(1)}, u32[]{:S(2)}, u32[]{:S(2)}) collective-permute-start(bf16[128,1920]{1,0:T(8,128)(2,1)S(1)} %pack_tokens.1.refs_0_), channel_id=1, source_target_pairs={{0,6},{1,7},{2,4},{3,5},{4,2},{5,3},{6,0},{7,1},{8,14},{9,15},{10,... | collective-permute-start | bytes 1474568 | tf_op jit(solution)/shard_map/ppermute | solution.py:27
  39.4 40.4 %collective-permute-start.24 = (bf16[128,1920]{1,0:T(8,128)(2,1)S(1)}, bf16[128,1920]{1,0:T(8,128)(2,1)S(1)}, u32[]{:S(2)}, u32[]{:S(2)}) collective-permute-start(bf16[128,1920]{1,0:T(8,128)(2,1)S(1)} %pack_tokens.1.refs_0_), channel_id=1, source_target_pairs={{0,4},{1,5},{2,6},{3,7},{4,0},{5,1},{6,2},{7,3},{8,12},{9,13},{10,... | collective-permute-start | bytes 1474568 | tf_op jit(solution)/shard_map/ppermute | solution.py:27
  39.4 40.4 %collective-permute-start.10 = (bf16[128,1920]{1,0:T(8,128)(2,1)S(1)}, bf16[128,1920]{1,0:T(8,128)(2,1)S(1)}, u32[]{:S(2)}, u32[]{:S(2)}) collective-permute-start(bf16[128,1920]{1,0:T(8,128)(2,1)S(1)} %pack_tokens.1.refs_0_), channel_id=1, source_target_pairs={{0,2},{1,3},{2,0},{3,1},{4,6},{5,7},{6,4},{7,5},{8,10},{9,11},{10,... | collective-permute-start | bytes 1474568 | tf_op jit(solution)/shard_map/ppermute | solution.py:27
  44.6 35.7 %collective-permute-start.66 = (bf16[256,576]{0,1:T(8,128)(2,1)}, bf16[256,576]{0,1:T(8,128)(2,1)S(1)}, u32[]{:S(2)}, u32[]{:S(2)}) collective-permute-start(bf16[256,576]{0,1:T(8,128)(2,1)} %collective-permute-done.65), channel_id=1, source_target_pairs={{0,8},{8,0},{16,24},{24,16},{1,9},{9,1},{17,25},{25,17},{2,10},{10... | collective-permute-start | bytes 884744 | tf_op jit(solution)/shard_map/ppermute | solution.py:27
  68.8 29.2 %collective-permute-start.53 = (bf16[3,2,80,256]{3,2,0,1:T(8,128)(2,1)}, bf16[3,2,80,256]{3,2,0,1:T(8,128)(2,1)}, u32[]{:S(2)}, u32[]{:S(2)}) collective-permute-start(bf16[3,2,80,256]{3,2,0,1:T(8,128)(2,1)} %copy.65), channel_id=1, source_target_pairs={{0,8},{8,0},{16,24},{24,16},{1,9},{9,1},{17,25},{25,17},{2,10},{10... | collective-permute-start | bytes 737288 | tf_op jit(solution)/shard_map/ppermute | solution.py:27
  78.7 20.9 %collective-permute-start.58 = (bf16[3,2,80,256]{3,2,0,1:T(8,128)(2,1)}, bf16[3,2,80,256]{3,2,0,1:T(8,128)(2,1)}, u32[]{:S(2)}, u32[]{:S(2)}) collective-permute-start(bf16[3,2,80,256]{3,2,0,1:T(8,128)(2,1)} %copy.67), channel_id=1, source_target_pairs={{0,16},{8,24},{16,0},{24,8},{1,17},{9,25},{17,1},{25,9},{2,18},{10... | collective-permute-start | bytes 737288 | tf_op jit(solution)/shard_map/ppermute | solution.py:27
  79.8 31.2 %collective-permute-start.39 = (bf16[128,1920]{1,0:T(8,128)(2,1)S(1)}, bf16[128,1920]{1,0:T(8,128)(2,1)S(1)}, u32[]{:S(2)}, u32[]{:S(2)}) collective-permute-start(bf16[128,1920]{1,0:T(8,128)(2,1)S(1)} %collective-permute-done.38.refs_0_), channel_id=1, source_target_pairs={{0,1},{1,0},{2,3},{3,2},{4,5},{5,4},{6,7},{7,6},{8,9},{9,8},{10,11... | collective-permute-start | bytes 1474568 | tf_op jit(solution)/shard_map/ppermute | solution.py:27
  79.8 44.0 %collective-permute-start.25 = (bf16[128,1920]{1,0:T(8,128)(2,1)S(1)}, bf16[128,1920]{1,0:T(8,128)(2,1)S(1)}, u32[]{:S(2)}, u32[]{:S(2)}) collective-permute-start(bf16[128,1920]{1,0:T(8,128)(2,1)S(1)} %collective-permute-done.24.refs_0_), channel_id=1, source_target_pairs={{0,1},{1,0},{2,3},{3,2},{4,5},{5,4},{6,7},{7,6},{8,9},{9,8},{10,11... | collective-permute-start | bytes 1474568 | tf_op jit(solution)/shard_map/ppermute | solution.py:27
  80.3 57.3 %collective-permute-start.11 = (bf16[128,1920]{1,0:T(8,128)(2,1)S(1)}, bf16[128,1920]{1,0:T(8,128)(2,1)S(1)}, u32[]{:S(2)}, u32[]{:S(2)}) collective-permute-start(bf16[128,1920]{1,0:T(8,128)(2,1)S(1)} %collective-permute-done.10.refs_0_), channel_id=1, source_target_pairs={{0,1},{1,0},{2,3},{3,2},{4,5},{5,4},{6,7},{7,6},{8,9},{9,8},{10,11... | collective-permute-start | bytes 1474568 | tf_op jit(solution)/shard_map/ppermute | solution.py:27
  98.0 68.3 %collective-permute-start.67 = (bf16[4,4,32,576]{3,2,1,0:T(8,128)(2,1)S(1)}, bf16[4,4,32,576]{3,2,1,0:T(8,128)(2,1)S(1)}, u32[]{:S(2)}, u32[]{:S(2)}) collective-permute-start(bf16[4,4,32,576]{3,2,1,0:T(8,128)(2,1)S(1)} %fusion.10), channel_id=1, source_target_pairs={{0,1},{1,0},{2,3},{3,2},{4,5},{5,4},{6,7},{7,6},{8,9},{9,8},{10,11... | collective-permute-start | bytes 1769480 | tf_op jit(solution)/shard_map/ppermute | solution.py:27
  109.8 25.8 %collective-permute-start.55 = (bf16[2,80,256]{2,1,0:T(8,128)(2,1)S(1)}, bf16[2,80,256]{2,1,0:T(8,128)(2,1)S(1)}, u32[]{:S(2)}, u32[]{:S(2)}) collective-permute-start(bf16[2,80,256]{2,1,0:T(8,128)(2,1)S(1)} %pad_maximum_fusion.8.refs_1_), channel_id=1, source_target_pairs={{0,16},{8,24},{16,0},{24,8},{1,17},{9,25},{17,1},{25,9},{2,18},{10... | collective-permute-start | bytes 245768 | tf_op jit(solution)/shard_map/ppermute | solution.py:27
  111.0 34.4 %collective-permute-start.56 = (bf16[2,80,256]{2,1,0:T(8,128)(2,1)S(1)}, bf16[2,80,256]{2,1,0:T(8,128)(2,1)S(1)}, u32[]{:S(2)}, u32[]{:S(2)}) collective-permute-start(bf16[2,80,256]{2,1,0:T(8,128)(2,1)S(1)} %pad_maximum_fusion.8.refs_1_), channel_id=1, source_target_pairs={{0,8},{8,0},{16,24},{24,16},{1,9},{9,1},{17,25},{25,17},{2,10},{10... | collective-permute-start | bytes 245768 | tf_op jit(solution)/shard_map/ppermute | solution.py:27
  135.6 18.7 %collective-permute-start.61 = (bf16[2,80,256]{2,1,0:T(8,128)(2,1)S(1)}, bf16[2,80,256]{2,1,0:T(8,128)(2,1)S(1)}, u32[]{:S(2)}, u32[]{:S(2)}) collective-permute-start(bf16[2,80,256]{2,1,0:T(8,128)(2,1)S(1)} %pad_maximum_fusion.9.refs_5_), channel_id=1, source_target_pairs={{0,16},{8,24},{16,0},{24,8},{1,17},{9,25},{17,1},{25,9},{2,18},{10... | collective-permute-start | bytes 245768 | tf_op jit(solution)/shard_map/ppermute | solution.py:27
  136.7 18.7 %collective-permute-start.57 = (bf16[2,80,256]{2,1,0:T(8,128)(2,1)S(1)}, bf16[2,80,256]{2,1,0:T(8,128)(2,1)S(1)}, u32[]{:S(2)}, u32[]{:S(2)}) collective-permute-start(bf16[2,80,256]{2,1,0:T(8,128)(2,1)S(1)} %collective-permute-done.55.refs_2_), channel_id=1, source_target_pairs={{0,8},{8,0},{16,24},{24,16},{1,9},{9,1},{17,25},{25,17},{2,10},{10... | collective-permute-start | bytes 245768 | tf_op jit(solution)/shard_map/ppermute | solution.py:27
  137.6 18.7 %collective-permute-start.62 = (bf16[2,80,256]{2,1,0:T(8,128)(2,1)S(1)}, bf16[2,80,256]{2,1,0:T(8,128)(2,1)S(1)}, u32[]{:S(2)}, u32[]{:S(2)}) collective-permute-start(bf16[2,80,256]{2,1,0:T(8,128)(2,1)S(1)} %collective-permute-done.60.refs_6_), channel_id=1, source_target_pairs={{0,16},{8,24},{16,0},{24,8},{1,17},{9,25},{17,1},{25,9},{2,18},{10... | collective-permute-start | bytes 245768 | tf_op jit(solution)/shard_map/ppermute | solution.py:27
  145.4 21.9 %collective-permute-start.40 = (bf16[3,2,160,256]{3,2,0,1:T(8,128)(2,1)S(1)}, bf16[3,2,160,256]{3,2,0,1:T(8,128)(2,1)}, u32[]{:S(2)}, u32[]{:S(2)}) collective-permute-start(bf16[3,2,160,256]{3,2,0,1:T(8,128)(2,1)S(1)} %copy.61), channel_id=1, source_target_pairs={{0,8},{8,0},{16,24},{24,16},{1,9},{9,1},{17,25},{25,17},{2,10},{10... | collective-permute-start | bytes 1474568 | tf_op jit(solution)/shard_map/ppermute | solution.py:27
  155.4 18.9 %collective-permute-start.26 = (bf16[3,2,160,256]{3,2,0,1:T(8,128)(2,1)}, bf16[3,2,160,256]{3,2,0,1:T(8,128)(2,1)}, u32[]{:S(2)}, u32[]{:S(2)}) collective-permute-start(bf16[3,2,160,256]{3,2,0,1:T(8,128)(2,1)} %copy.57), channel_id=1, source_target_pairs={{0,8},{8,0},{16,24},{24,16},{1,9},{9,1},{17,25},{25,17},{2,10},{10... | collective-permute-start | bytes 1474568 | tf_op jit(solution)/shard_map/ppermute | solution.py:27
  156.3 23.1 %collective-permute-start.31 = (bf16[3,2,160,256]{3,2,0,1:T(8,128)(2,1)}, bf16[3,2,160,256]{3,2,0,1:T(8,128)(2,1)}, u32[]{:S(2)}, u32[]{:S(2)}) collective-permute-start(bf16[3,2,160,256]{3,2,0,1:T(8,128)(2,1)} %copy.59), channel_id=1, source_target_pairs={{0,16},{8,24},{16,0},{24,8},{1,17},{9,25},{17,1},{25,9},{2,18},{10... | collective-permute-start | bytes 1474568 | tf_op jit(solution)/shard_map/ppermute | solution.py:27
  167.3 20.3 %collective-permute-start.17 = (bf16[3,2,160,256]{3,2,0,1:T(8,128)(2,1)S(1)}, bf16[3,2,160,256]{3,2,0,1:T(8,128)(2,1)S(1)}, u32[]{:S(2)}, u32[]{:S(2)}) collective-permute-start(bf16[3,2,160,256]{3,2,0,1:T(8,128)(2,1)S(1)} %copy.55), channel_id=1, source_target_pairs={{0,16},{8,24},{16,0},{24,8},{1,17},{9,25},{17,1},{25,9},{2,18},{10... | collective-permute-start | bytes 1474568 | tf_op jit(solution)/shard_map/ppermute | solution.py:27
  169.5 42.5 %collective-permute-start.70 = (bf16[4,32,576]{2,1,0:T(8,128)(2,1)S(1)}, bf16[4,32,576]{2,1,0:T(8,128)(2,1)S(1)}, u32[]{:S(2)}, u32[]{:S(2)}) collective-permute-start(bf16[4,32,576]{2,1,0:T(8,128)(2,1)S(1)} %get-tuple-element.74), channel_id=1, source_target_pairs={{0,6},{1,7},{2,4},{3,5},{4,2},{5,3},{6,0},{7,1},{8,14},{9,15},{10,... | collective-permute-start | bytes 442376 | tf_op jit(solution)/shard_map/ppermute | solution.py:27
  174.3 38.8 %collective-permute-start.69 = (bf16[4,32,576]{2,1,0:T(8,128)(2,1)S(1)}, bf16[4,32,576]{2,1,0:T(8,128)(2,1)S(1)}, u32[]{:S(2)}, u32[]{:S(2)}) collective-permute-start(bf16[4,32,576]{2,1,0:T(8,128)(2,1)S(1)} %get-tuple-element.75), channel_id=1, source_target_pairs={{0,4},{1,5},{2,6},{3,7},{4,0},{5,1},{6,2},{7,3},{8,12},{9,13},{10,... | collective-permute-start | bytes 442376 | tf_op jit(solution)/shard_map/ppermute | solution.py:27
  179.4 34.8 %collective-permute-start.68 = (bf16[4,32,576]{2,1,0:T(8,128)(2,1)S(1)}, bf16[4,32,576]{2,1,0:T(8,128)(2,1)S(1)}, u32[]{:S(2)}, u32[]{:S(2)}) collective-permute-start(bf16[4,32,576]{2,1,0:T(8,128)(2,1)S(1)} %get-tuple-element.73), channel_id=1, source_target_pairs={{0,2},{1,3},{2,0},{3,1},{4,6},{5,7},{6,4},{7,5},{8,10},{9,11},{10,... | collective-permute-start | bytes 442376 | tf_op jit(solution)/shard_map/ppermute | solution.py:27
  244.9 24.4 %collective-permute-start.50 = (bf16[128,896]{1,0:T(8,128)(2,1)S(1)}, bf16[128,896]{1,0:T(8,128)(2,1)S(1)}, u32[]{:S(2)}, u32[]{:S(2)}) collective-permute-start(bf16[128,896]{1,0:T(8,128)(2,1)S(1)} %get-tuple-element.59), channel_id=1, source_target_pairs={{0,1},{1,0},{2,3},{3,2},{4,5},{5,4},{6,7},{7,6},{8,9},{9,8},{10,11... | collective-permute-start | bytes 688136 | tf_op jit(solution)/shard_map/ppermute | solution.py:27
  255.1 22.4 %collective-permute-start.63 = (bf16[128,896]{1,0:T(8,128)(2,1)S(1)}, bf16[128,896]{1,0:T(8,128)(2,1)S(1)}, u32[]{:S(2)}, u32[]{:S(2)}) collective-permute-start(bf16[128,896]{1,0:T(8,128)(2,1)S(1)} %route_sums.9), channel_id=1, source_target_pairs={{0,1},{1,0},{2,3},{3,2},{4,5},{5,4},{6,7},{7,6},{8,9},{9,8},{10,11... | collective-permute-start | bytes 688136 | tf_op jit(solution)/shard_map/ppermute | solution.py:27
  255.7 20.4 %collective-permute-start.73 = (bf16[32,576]{1,0:T(8,128)(2,1)S(1)}, bf16[32,576]{1,0:T(8,128)(2,1)S(1)}, u32[]{:S(2)}, u32[]{:S(2)}) collective-permute-start(bf16[32,576]{1,0:T(8,128)(2,1)S(1)} %get-tuple-element.97), channel_id=1, source_target_pairs={{0,24},{8,16},{16,8},{24,0},{1,25},{9,17},{17,9},{25,1},{2,26},{10... | collective-permute-start | bytes 110600 | tf_op jit(solution)/shard_map/ppermute | solution.py:27
  256.8 19.4 %collective-permute-start.72 = (bf16[32,576]{1,0:T(8,128)(2,1)S(1)}, bf16[32,576]{1,0:T(8,128)(2,1)S(1)}, u32[]{:S(2)}, u32[]{:S(2)}) collective-permute-start(bf16[32,576]{1,0:T(8,128)(2,1)S(1)} %get-tuple-element.98), channel_id=1, source_target_pairs={{0,16},{8,24},{16,0},{24,8},{1,17},{9,25},{17,1},{25,9},{2,18},{10... | collective-permute-start | bytes 110600 | tf_op jit(solution)/shard_map/ppermute | solution.py:27
  257.8 19.1 %collective-permute-start.71 = (bf16[32,576]{1,0:T(8,128)(2,1)S(1)}, bf16[32,576]{1,0:T(8,128)(2,1)S(1)}, u32[]{:S(2)}, u32[]{:S(2)}) collective-permute-start(bf16[32,576]{1,0:T(8,128)(2,1)S(1)} %get-tuple-element.96), channel_id=1, source_target_pairs={{0,8},{8,0},{16,24},{24,16},{1,9},{9,1},{17,25},{25,17},{2,10},{10... | collective-permute-start | bytes 110600 | tf_op jit(solution)/shard_map/ppermute | solution.py:27
  276.0 19.4 %collective-permute-start.37 = (bf16[128,896]{1,0:T(8,128)(2,1)S(1)}, bf16[128,896]{1,0:T(8,128)(2,1)S(1)}, u32[]{:S(2)}, u32[]{:S(2)}) collective-permute-start(bf16[128,896]{1,0:T(8,128)(2,1)S(1)} %add_convert_fusion.2), channel_id=1, source_target_pairs={{0,4},{1,5},{2,6},{3,7},{4,0},{5,1},{6,2},{7,3},{8,12},{9,13},{10,... | collective-permute-start | bytes 688136 | tf_op jit(solution)/shard_map/ppermute | solution.py:27
  276.1 19.3 %collective-permute-start.23 = (bf16[128,896]{1,0:T(8,128)(2,1)S(1)}, bf16[128,896]{1,0:T(8,128)(2,1)S(1)}, u32[]{:S(2)}, u32[]{:S(2)}) collective-permute-start(bf16[128,896]{1,0:T(8,128)(2,1)S(1)} %add_convert_fusion.3), channel_id=1, source_target_pairs={{0,2},{1,3},{2,0},{3,1},{4,6},{5,7},{6,4},{7,5},{8,10},{9,11},{10,... | collective-permute-start | bytes 688136 | tf_op jit(solution)/shard_map/ppermute | solution.py:27
  (67 other events, 533.0 us)

commit v2 on v0

v2 whole, which is shorter than its diff:
```python
import functools

import jax
import jax.numpy as jnp
from jax import lax
from jax.experimental import pallas as pl
from jax.experimental.pallas import tpu as pltpu
from jax.sharding import PartitionSpec as P

SCORE_SCALE = 192.0 ** (-0.5)
MASKED = -1e30
BF16 = jnp.bfloat16
F32 = jnp.float32
META = 128
VMEM_LIMIT = 16 * 1024 * 1024
AHEAD = 3
FIRST_VMEM_LIMIT = 40 * 10**6


def swiglu_back(gate_pre, up_pre, hidden_grad):
    sigma = jax.nn.sigmoid(gate_pre)
    gate_back = hidden_grad * up_pre * sigma * (1.0 + gate_pre * (1.0 - sigma))
    up_back = hidden_grad * gate_pre * sigma
    return (gate_back.astype(BF16), up_back.astype(BF16))


def shift(value, bits, name):
    pairs = [(i, i ^ bits) for i in range(lax.axis_size("exp"))]
    with jax.named_scope(name):
        return lax.ppermute(value, "exp", pairs)


def declared(length):
    return pl.CostEstimate(
        flops=int(length * 10**9) + 1, bytes_accessed=int(length * 3 * 10**6) + 1, transcendentals=0
    )


LENGTH = [1]


def call(kernel, args, in_specs, out_shape, out_specs, deps=(), grid=(), scratch=(), limit=None, name=None):
    count = len(args)

    def body(*refs):
        kernel(*refs[:count], *refs[count + len(deps) :])

    return pl.pallas_call(
        body,
        out_shape=out_shape,
        grid=grid,
        in_specs=list(in_specs) + [pl.BlockSpec(memory_space=pl.ANY)] * len(deps),
        out_specs=out_specs,
        scratch_shapes=scratch,
        compiler_params=pltpu.CompilerParams(vmem_limit_bytes=limit or VMEM_LIMIT),
        cost_estimate=declared(LENGTH[0]),
        name=name,
    )(*args, *deps)


def dot(left, right):
    return jnp.dot(left, right, preferred_element_type=F32)


def dot_t(left, right):
    return lax.dot_general(left, right, (((1,), (1,)), ((), ())), preferred_element_type=F32)


def pack(experts, routes, gates, rows_in, rows_grad, out_ref):
    rows, width = rows_in.shape
    out_ref[:, :width] = rows_in
    out_ref[:, width : 2 * width] = rows_grad
    lane = lax.broadcasted_iota(jnp.int32, (rows, META), 1)
    expert = lane % experts
    section = lane // experts
    gate = jnp.zeros((rows, META), F32)
    named = jnp.zeros((rows, META), F32)
    for k in range(routes.shape[1]):
        hit = routes[:, k : k + 1] == expert
        gate = gate + jnp.where(hit, gates[:, k : k + 1], 0.0)
        named = named + jnp.where(hit, 1.0, 0.0)
    low = lax.broadcasted_iota(jnp.int32, (rows, rows), 0)
    high = lax.broadcasted_iota(jnp.int32, (rows, rows), 1)
    before = jnp.where(high < low, 1.0, 0.0).astype(BF16)
    slot = jnp.where(named > 0.0, dot(before, named.astype(BF16)), -1.0)
    gate_high = gate.astype(BF16).astype(F32)
    meta = jnp.where(section == 0, gate_high, jnp.where(section == 1, gate - gate_high, slot))
    out_ref[:, 2 * width :] = meta.astype(BF16)


def pack_kernel(experts, routes_ref, gates_ref, input_ref, grad_ref, out_ref):
    pack(experts, routes_ref[...].T, gates_ref[...].T, input_ref[...], grad_ref[...], out_ref)


def pack_tokens(moe_input, moe_grad, routes, gates, experts):
    rows, width = moe_input.shape
    return call(
        functools.partial(pack_kernel, experts),
        [routes.T, gates.T, moe_input, moe_grad],
        in_vmem(4),
        jax.ShapeDtypeStruct((rows, 2 * width + META), BF16),
        in_vmem(1)[0],
        name="pack_tokens",
    )


def first_kernel(blocks, experts, capacity, plan_ref, *refs):
    token_refs, args, refs = refs[:blocks], refs[blocks : blocks + 3], refs[blocks + 3 :]
    send_ref, keep_ref = refs[:2]
    weights, sem = refs[2:5], refs[5]
    local = weights[0].shape[0]
    quarter = weights[0].shape[2] // 4
    copies = [
        pltpu.make_async_copy(args[m].at[e], weights[m].at[e], sem.at[3 * e + m])
        for e in range(local)
        for m in range(3)
    ]
    for copy in copies[:AHEAD]:
        copy.start()
    for e in range(local):
        rows = slot_rows(plan_ref, e, experts, capacity, token_refs)
        for m in range(3):
            copies[3 * e + m].wait()
            if 3 * e + m + AHEAD < len(copies):
                copies[3 * e + m + AHEAD].start()
            for place, out_ref in ((1, send_ref), (3, keep_ref)):
                for j in range(2):
                    part = columns(plan_ref, place + j, quarter)
                    if m < 2:
                        value = dot(rows[0], weights[m][e, :, part])
                    else:
                        value = dot_t(rows[1], weights[m][e, part, :])
                    out_ref[j, e, m] = value.astype(BF16)


def first_products(plan, tokens, weights, capacity, experts):
    local, _, hidden = weights[0].shape
    part = jax.ShapeDtypeStruct((2, local, 3, len(tokens) * capacity, hidden // 4), BF16)
    return call(
        functools.partial(first_kernel, len(tokens), experts, capacity),
        [plan, *tokens, *weights],
        [pl.BlockSpec(memory_space=pltpu.SMEM)]
        + in_vmem(len(tokens))
        + [pl.BlockSpec(memory_space=pltpu.HBM)] * 3,
        [part, part] + [jax.ShapeDtypeStruct(w.shape, w.dtype) for w in weights],
        in_vmem(5),
        scratch=[pltpu.SemaphoreType.DMA((3 * local,))],
        limit=FIRST_VMEM_LIMIT,
        name="first_products",
    )


def slot_rows(plan_ref, expert, experts, capacity, token_refs):
    width = (token_refs[0].shape[1] - META) // 2
    tokens = token_refs[0].shape[0]
    lane = lax.broadcasted_iota(jnp.int32, (16, META), 1)
    pick = jnp.where(lane == 2 * experts + plan_ref[0] + expert, 1.0, 0.0).astype(BF16)
    slot = lax.broadcasted_iota(jnp.int32, (capacity, tokens), 0)
    parts_in, parts_grad = [], []
    for token_ref in token_refs:
        slot_of = dot_t(pick, token_ref[:, 2 * width :])[0:1, :].astype(jnp.int32)
        chosen = jnp.where(slot == slot_of, 1.0, 0.0).astype(BF16)
        parts_in.append(dot(chosen, token_ref[:, :width]).astype(BF16))
        parts_grad.append(dot(chosen, token_ref[:, width : 2 * width]).astype(BF16))
    return jnp.concatenate(parts_in, axis=0), jnp.concatenate(parts_grad, axis=0)


def columns(plan_ref, place, quarter):
    return pl.ds(pl.multiple_of(plan_ref[place] * quarter, quarter), quarter)


def products_kernel(blocks, experts, capacity, plan_ref, *refs):
    token_refs = refs[:blocks]
    gate_ref, up_ref, down_ref, send_ref, keep_ref = refs[blocks:]
    local = gate_ref.shape[0]
    quarter = gate_ref.shape[2] // 4
    rows = [slot_rows(plan_ref, e, experts, capacity, token_refs) for e in range(local)]
    for place, out_ref in ((1, send_ref), (3, keep_ref)):
        for j in range(2):
            part = columns(plan_ref, place + j, quarter)
            for e in range(local):
                out_ref[j, e, 0] = dot(rows[e][0], gate_ref[e, :, part]).astype(BF16)
                out_ref[j, e, 1] = dot(rows[e][0], up_ref[e, :, part]).astype(BF16)
                out_ref[j, e, 2] = dot_t(rows[e][1], down_ref[e, part, :]).astype(BF16)


def in_vmem(count):
    return [pl.BlockSpec(memory_space=pltpu.VMEM)] * count


def products(plan, tokens, w_gate, w_up, w_down, capacity, experts, deps):
    local, _, hidden = w_gate.shape
    slots = len(tokens) * capacity
    shape = jax.ShapeDtypeStruct((2, local, 3, slots, hidden // 4), BF16)
    return call(
        functools.partial(products_kernel, len(tokens), experts, capacity),
        [plan, *tokens, w_gate, w_up, w_down],
        [pl.BlockSpec(memory_space=pltpu.SMEM)] + in_vmem(len(tokens) + 3),
        [shape, shape],
        in_vmem(2),
        deps,
        name="products",
    )


def add_kernel(*refs):
    *terms, out_ref = refs
    value = terms[0][...].astype(F32)
    for term in terms[1:]:
        value = value + term[...].astype(F32)
    out_ref[...] = value.astype(out_ref.dtype)


def part_spec(part, shape):
    zeros = (0,) * (len(shape) - 1)
    return pl.BlockSpec((None, *shape[1:]), lambda i: (part, *zeros))


def add_parts(terms, dtype, deps=()):
    shape = terms[0][0].shape[1:]
    return call(
        add_kernel,
        [term for term, _ in terms],
        [part_spec(part, term.shape) for term, part in terms],
        jax.ShapeDtypeStruct(shape, dtype),
        pl.BlockSpec(shape, lambda i: (0,) * len(shape)),
        deps,
        grid=(1,),
        name="add_parts",
    )


def back_kernel(got_ref, kept_ref, other_ref, out_ref):
    for e in range(out_ref.shape[0]):
        gate_pre, up_pre, hidden_grad = (
            got_ref[0, e, m].astype(F32) + kept_ref[0, e, m].astype(F32) + other_ref[e, m].astype(F32)
            for m in range(3)
        )
        out_ref[e, 0], out_ref[e, 1] = swiglu_back(gate_pre, up_pre, hidden_grad)


def hidden_back(got, kept, other, deps):
    _, local, _, slots, quarter = got.shape
    last = pl.BlockSpec((1, local, 3, slots, quarter), lambda i: (1, 0, 0, 0, 0))
    return call(
        back_kernel,
        [got, kept, other],
        [last, last, pl.BlockSpec((local, 3, slots, quarter), lambda i: (0, 0, 0, 0))],
        jax.ShapeDtypeStruct((local, 2, slots, quarter), BF16),
        pl.BlockSpec((local, 2, slots, quarter), lambda i: (0, 0, 0, 0)),
        deps,
        grid=(1,),
        name="hidden_back",
    )


def join_kernel(own_ref, other_ref, out_ref):
    out_ref[0] = own_ref[...]
    out_ref[1] = other_ref[...]


def join(own, other, deps):
    shape = jax.ShapeDtypeStruct((2, *own.shape), own.dtype)
    return call(join_kernel, [own, other], in_vmem(2), shape, in_vmem(1)[0], deps, name="join")


def route_kernel(blocks, mine, experts, capacity, plan_ref, *refs):
    meta_refs, refs = refs[:blocks], refs[blocks:]
    piece_refs, (gate_ref, up_ref), out_refs = refs[:2], refs[2:4], refs[4:]
    local = gate_ref.shape[0]
    quarter = gate_ref.shape[2] // 4
    tokens = meta_refs[0].shape[0]
    row = lax.broadcasted_iota(jnp.int32, (META, META), 0)
    lane = lax.broadcasted_iota(jnp.int32, (META, META), 1)
    slot = lax.broadcasted_iota(jnp.int32, (tokens, capacity), 1)
    totals = [None] * blocks
    for e in range(local):
        route = None
        for p in range(4):
            piece_ref = piece_refs[p // 2]
            part = columns(plan_ref, 5 + p, quarter)
            value = dot_t(piece_ref[p % 2, e, 0], gate_ref[e, :, part])
            value = value + dot_t(piece_ref[p % 2, e, 1], up_ref[e, :, part])
            route = value if route is None else route + value
        route = route.astype(BF16)
        pick = jnp.where(lane == row * experts + plan_ref[0] + e, 1.0, 0.0).astype(BF16)
        for b in range(blocks):
            found = dot_t(meta_refs[b][...], pick)
            named = found[:, 2:3].astype(jnp.int32) == slot
            high = jnp.where(named, found[:, 0:1], 0.0).astype(BF16)
            low = jnp.where(named, found[:, 1:2], 0.0).astype(BF16)
            own = route[b * capacity : (b + 1) * capacity, :]
            value = dot(high, own) + dot(low, own)
            totals[b] = value if totals[b] is None else totals[b] + value
    out_refs = list(out_refs)
    if mine:
        mine_ref = out_refs.pop(0)
        for b in range(mine):
            mine_ref[b] = totals[b]
    for b in range(mine, blocks):
        out_refs[0][b - mine] = totals[b].astype(BF16)


def route_sums(plan, tokens, mine, pieces, w_gate, w_up, capacity, experts, deps):
    width = w_gate.shape[1]
    blocks = len(tokens)
    count = tokens[0].shape[0]
    meta_at = 2 * width // META
    out_shape = []
    if mine:
        out_shape.append(jax.ShapeDtypeStruct((mine, count, width), F32))
    if blocks > mine:
        out_shape.append(jax.ShapeDtypeStruct((blocks - mine, count, width), BF16))
    return call(
        functools.partial(route_kernel, blocks, mine, experts, capacity),
        [plan, *tokens, *pieces, w_gate, w_up],
        [pl.BlockSpec(memory_space=pltpu.SMEM)]
        + [pl.BlockSpec((count, META), lambda i: (0, meta_at))] * blocks
        + in_vmem(4),
        out_shape,
        in_vmem(len(out_shape)),
        deps,
        grid=(1,),
        name="route_sums",
    )


def plane_shift(value, near, name):
    count = lax.axis_size("exp")
    pairs = []
    for c in range(lax.axis_size("ctx")):
        for i in range(count):
            bits = 1 if (i % 2 == 0) == near else 2
            pairs.append((c * count + i, (c ^ bits) * count + i))
    with jax.named_scope(name):
        return lax.ppermute(value, ("ctx", "exp"), pairs)


class Chunk:
    def __init__(self, name, plan, weights, capacity, experts, mine):
        self.name, self.plan, self.weights, self.mine = name, plan, weights, mine
        self.capacity, self.experts = capacity, experts

    def multiply(self, tokens, *deps):
        return self.begin(
            tokens, *products(self.plan, tokens, *self.weights, self.capacity, self.experts, deps)
        )

    def begin(self, tokens, send, kept):
        self.tokens, self.kept = tokens, kept
        self.got = plane_shift(send, True, self.name + "_sums_near")
        return kept

    def add(self, *deps):
        half = add_parts([(self.got, 0), (self.kept, 0)], BF16, deps)
        self.other = plane_shift(half, False, self.name + "_sums_far")
        return half

    def turn(self, *deps):
        self.own = hidden_back(self.got, self.kept, self.other, deps)
        self.from_far = plane_shift(self.own, False, self.name + "_own_far")
        return self.own

    def forward(self, *deps):
        self.joined = join(self.own, self.from_far, deps)
        self.from_near = plane_shift(self.joined, True, self.name + "_both_near")
        return self.joined

    def finish(self, *deps):
        return route_sums(
            self.plan,
            self.tokens,
            self.mine,
            [self.joined, self.from_near],
            *self.weights[:2],
            self.capacity,
            self.experts,
            deps,
        )


def near_layers(
    moe_input, moe_grad, routes, gates, w_gate, w_up, w_down, queries, out_grad, positions, latents
):
    tok_rows = moe_input.shape[0]
    fanout = routes.shape[1]
    local = w_gate.shape[0]
    exp_count = lax.axis_size("exp")
    experts = local * exp_count
    capacity = tok_rows * fanout // experts * 5 // 4
    ctx, exp = lax.axis_index("ctx"), lax.axis_index("exp")
    x, y = ctx % 2, ctx // 2
    near = jnp.where(exp % 2 == 0, x, y)
    far = jnp.where(exp % 2 == 0, y, x)
    near_bit = jnp.where(exp % 2 == 0, 1, 2)
    plan = jnp.stack(
        [
            exp * local,
            (1 - near) * 2 + 1 - far,
            (1 - near) * 2 + far,
            near * 2 + 1 - far,
            near * 2 + far,
            near * 2 + far,
            near * 2 + 1 - far,
            (1 - near) * 2 + far,
            (1 - near) * 2 + 1 - far,
            exp,
            ctx,
            ctx ^ (3 - near_bit),
            ctx ^ near_bit,
            ctx ^ 3,
        ]
    ).astype(jnp.int32)

    def chunk(name, mine):
        return Chunk(name, plan, weights, capacity, experts, mine)

    own = pack_tokens(moe_input, moe_grad, routes, gates, experts)
    partner = shift(own, 1, "partner_move")
    first = [own, partner]
    LENGTH[0] = 10
    send, kept, *weights = first_products(plan, first, (w_gate, w_up, w_down), capacity, experts)
    a = chunk("a", 1)
    from_1 = shift(own, 2, "from_1_move")
    from_3 = shift(own, 6, "from_3_move")
    other_1 = shift(from_1, 1, "other_1_move")
    other_3 = shift(from_3, 1, "other_3_move")
    from_2 = shift(from_3, 2, "from_2_move")
    other_2 = shift(from_2, 1, "other_2_move")
    keys = latents.T
    keys_near = plane_shift(keys, True, "keys_near_move")
    keys_far = plane_shift(keys, False, "keys_far_move")
    keys_both = plane_shift(keys_near, False, "keys_both_move")
    made = {}

    def attend(*deps):
        made["queries"], give, made["keep"] = attention(
            plan, queries, out_grad, positions, [keys, keys_far, keys_near, keys_both], deps
        )
        made["got"] = shift(give, 1, "got_move")
        return made["keep"]

    def latent_cores(*deps):
        made["cores"] = both = add_parts([(made["keep"][None], 0), (made["got"][None], 0)], BF16, deps)
        made["terms"] = [shift(both[i], 2 * i, "latent_terms") for i in range(1, exp_count // 2)]
        return both

    def latent_chips(*deps):
        terms = [(made["cores"], 0)] + [(term[None], 0) for term in made["terms"]]
        made["chips"] = both = add_parts(terms, BF16, deps)
        made["crossed"] = plane_shift(both[2:], True, "crossed_move")
        return both

    def latent_near(*deps):
        terms = [(made["chips"][None, :2], 0), (made["crossed"][None], 0)]
        made["pair"] = both = add_parts(terms, BF16, deps)
        made["last"] = plane_shift(both[1], False, "last_move")
        return both

    def latent_far(*deps):
        terms = [(made["pair"], 0), (made["last"][None], 0)]
        made["latents"] = add_parts(terms, F32, deps)
        return made["latents"]

    def start_total(*deps):
        made["total"], theirs = a.finish(*deps)
        made["more"] = [(shift(theirs, 1, "a_other_move"), 0)]
        return theirs

    def finish(chunk):
        def act(*deps):
            *mine, theirs = chunk.finish(*deps)
            made[chunk.name] = mine
            made[chunk.name + "_other"] = shift(theirs, 1, chunk.name + "_other_move")
            return theirs

        return act

    def send_back(chunk, bits):
        def act(*deps):
            made[chunk.name + "_back"] = []
            for place, bit in enumerate(bits):
                terms = [(made[chunk.name][0], place), (made[chunk.name + "_other"], place)]
                both = add_parts(terms, BF16, deps)
                back = shift(both, bit, chunk.name + "_back_move")
                made[chunk.name + "_back"].append((back[None], 0))
            return both

        return act

    def receive(chunk, last):
        def act(*deps):
            terms = [(made["total"], 0)] + made.pop("more", []) + made[chunk.name + "_back"]
            total = add_parts(terms, BF16 if last else F32, deps)
            made["total"] = total[None]
            return total

        return act

    b = chunk("b", 1)
    c = chunk("c", 1)
    d = chunk("d", 1)
    order = (
        (a.add, 2),
        (a.turn, 2),
        (functools.partial(b.multiply, [from_1, other_1]), 2),
        (attend, 2),
        (a.forward, 2),
        (b.add, 2),
        (start_total, 2),
        (functools.partial(c.multiply, [from_3, other_3]), 2),
        (b.turn, 2),
        (latent_cores, 2),
        (b.forward, 2),
        (c.add, 2),
        (functools.partial(d.multiply, [from_2, other_2]), 2),
        (finish(b), 2),
        (latent_chips, 2),
        (c.turn, 2),
        (send_back(b, (2,)), 2),
        (d.add, 2),
        (c.forward, 2),
        (latent_near, 2),
        (d.turn, 2),
        (finish(c), 2),
        (receive(b, False), 2),
        (d.forward, 2),
        (send_back(c, (6,)), 2),
        (latent_far, 2),
        (receive(c, False), 2),
        (finish(d), 2),
        (send_back(d, (4,)), 2),
        (receive(d, True), 2),
    )
    step = a.begin(first, send, kept)
    for act, length, *waits in order:
        LENGTH[0] = length
        step = act(step, *waits)
    return (made["total"][0], made["queries"], made["latents"])


def attention_kernel(heads, plan_ref, queries_ref, grads_ref, positions_ref, *refs):
    key_refs, (query_ref, give_ref, keep_ref, total_ref) = refs[:4], refs[4:]
    rows = queries_ref.shape[0]
    width, keys = key_refs[0].shape
    values = grads_ref.shape[1] // heads
    chips, shards, own_keys, _ = give_ref.shape
    square = lax.broadcasted_iota(jnp.int32, (rows, rows), 0)
    diagonal = square == lax.broadcasted_iota(jnp.int32, (rows, rows), 1)
    position = jnp.sum(
        jnp.where(diagonal, positions_ref[...].astype(F32), 0.0), axis=1, keepdims=True
    ).astype(jnp.int32)
    offset = lax.broadcasted_iota(jnp.int32, (rows, keys), 1)
    visible = [offset + plan_ref[10 + r] * keys <= position for r in range(shards)]
    outs = []
    for h in range(heads):
        query = queries_ref[:, h * width : (h + 1) * width]
        grad = grads_ref[:, h * values : (h + 1) * values]
        scores = [
            jnp.where(visible[r], dot(query, key_refs[r][...]) * SCORE_SCALE, MASKED)
            for r in range(shards)
        ]
        peak = functools.reduce(jnp.maximum, scores)
        peak = jnp.max(peak, axis=1, keepdims=True)
        raw = [jnp.where(visible[r], jnp.exp(scores[r] - peak), 0.0) for r in range(shards)]
        whole = jnp.sum(functools.reduce(jnp.add, raw), axis=1, keepdims=True)
        attend = [part / whole for part in raw]
        value_dot = [dot(grad, key_refs[r][:values, :]) for r in range(shards)]
        row_dot = functools.reduce(jnp.add, [a * v for a, v in zip(attend, value_dot)])
        row_dot = jnp.sum(row_dot, axis=1, keepdims=True)
        query_grad = None
        for r in range(shards):
            score_grad = (attend[r] * (value_dot[r] - row_dot)).astype(BF16)
            term = dot_t(score_grad, key_refs[r][...])
            query_grad = term if query_grad is None else query_grad + term
            key_grad = dot_rows(score_grad, query) * SCORE_SCALE
            value_grad = dot_rows(attend[r].astype(BF16), grad)
            part = pl.ds(r * keys, keys)
            if h == 0:
                total_ref[part, :] = key_grad
            else:
                total_ref[part, :] += key_grad
            total_ref[part, :values] += value_grad
        outs.append((query_grad * SCORE_SCALE).astype(BF16))
    query_ref[...] = jnp.concatenate(outs, axis=1)
    core, chip = plan_ref[9] % 2, plan_ref[9] // 2
    for b in range(chips):
        for r in range(shards):
            start = r * keys + (chip ^ b) * (2 * own_keys)
            across = (r % 2) * 2 + r // 2
            for out_ref, which, place in ((give_ref, 1 - core, across), (keep_ref, core, r)):
                at = pl.multiple_of(start + which * own_keys, own_keys)
                out_ref[b, place] = total_ref[pl.ds(at, own_keys), :].astype(BF16)


def dot_rows(left, right):
    return lax.dot_general(left, right, (((0,), (0,)), ((), ())), preferred_element_type=F32)


def attention(plan, queries, out_grad, positions, keys, deps):
    rows = queries.shape[0]
    width, count = keys[0].shape
    heads = queries.shape[1] // width
    exp_count = lax.axis_size("exp")
    terms = jax.ShapeDtypeStruct((exp_count // 2, len(keys), count // exp_count, width), BF16)
    return call(
        functools.partial(attention_kernel, heads),
        [plan, queries, out_grad, positions.reshape(1, rows), *keys],
        [pl.BlockSpec(memory_space=pltpu.SMEM)] + in_vmem(3 + len(keys)),
        [jax.ShapeDtypeStruct(queries.shape, BF16), terms, terms],
        in_vmem(3),
        deps,
        scratch=[pltpu.VMEM((len(keys) * count, width), F32)],
        name="attention",
    )


def far_expert_layer(moe_input, moe_grad, routes, gates, w_gate, w_up, w_down):
    tok_rows, width_part = moe_input.shape
    fanout = routes.shape[1]
    local_experts = w_gate.shape[0]
    exp_count = lax.axis_size("exp")
    experts = local_experts * exp_count
    capacity = tok_rows * fanout // experts * 5 // 4
    flat_routes = routes.reshape(-1)
    onehot = (flat_routes[:, None] == jnp.arange(experts, dtype=jnp.int32)[None, :]).astype(
        jnp.int32
    )
    before = jnp.cumsum(onehot, axis=0) - onehot
    slot_index = jnp.sum(before * onehot, axis=1)
    target = flat_routes * capacity + slot_index
    source_rows = jnp.arange(tok_rows * fanout, dtype=jnp.int32) // fanout
    empty = jnp.zeros((experts * capacity, width_part), BF16)
    send_shape = (exp_count, local_experts * capacity, width_part)
    send_input = empty.at[target].set(moe_input[source_rows]).reshape(send_shape)
    send_grad = empty.at[target].set(moe_grad[source_rows]).reshape(send_shape)
    recv_input, recv_grad = (
        lax.all_to_all(send_input, "exp", split_axis=0, concat_axis=0, tiled=True),
        lax.all_to_all(send_grad, "exp", split_axis=0, concat_axis=0, tiled=True),
    )
    slot_shape = (exp_count, local_experts, capacity, width_part)
    recv_input = recv_input.reshape(slot_shape)
    recv_grad = recv_grad.reshape(slot_shape)
    gate_part = jnp.einsum("sekd,edh->sekh", recv_input, w_gate, preferred_element_type=F32)
    up_part = jnp.einsum("sekd,edh->sekh", recv_input, w_up, preferred_element_type=F32)
    down_part = jnp.einsum("sekd,ehd->sekh", recv_grad, w_down, preferred_element_type=F32)
    gate_pre, up_pre, hidden_grad = (
        lax.psum(gate_part.astype(BF16), "ctx").astype(F32),
        lax.psum(up_part.astype(BF16), "ctx").astype(F32),
        lax.psum(down_part.astype(BF16), "ctx").astype(F32),
    )
    gate_back, up_back = swiglu_back(gate_pre, up_pre, hidden_grad)
    route_part = jnp.einsum("sekh,edh->sekd", gate_back, w_gate, preferred_element_type=F32)
    route_part = route_part + jnp.einsum(
        "sekh,edh->sekd", up_back, w_up, preferred_element_type=F32
    )
    route_part = route_part.astype(BF16).reshape(send_shape)
    returned = lax.all_to_all(route_part, "exp", split_axis=0, concat_axis=0, tiled=True).reshape(
        experts * capacity, width_part
    )
    per_route = returned[target].reshape(tok_rows, fanout, width_part).astype(F32)
    return jnp.sum(per_route * gates[:, :, None], axis=1).astype(BF16)


def sum_latent_grad(part):
    keys, width = part.shape
    shards, exp_count = lax.axis_size("ctx"), lax.axis_size("exp")
    part = part.reshape(shards, exp_count, keys // shards // exp_count, width).swapaxes(0, 1)
    part = part.reshape(keys, width).astype(BF16)
    part = lax.psum_scatter(part, "exp", scatter_dimension=0, tiled=True)
    return lax.psum_scatter(part.astype(F32), "ctx", scatter_dimension=0, tiled=True)


def attention_layer(queries, out_grad, positions, latents):
    q_rows = queries.shape[0]
    lat_width = latents.shape[1]
    head_count = queries.shape[1] // lat_width
    val_width = out_grad.shape[1] // head_count
    query_heads = queries.reshape(q_rows, head_count, lat_width)
    grad_heads = out_grad.reshape(q_rows, head_count, val_width)
    gathered = lax.all_gather(latents, "ctx", axis=0, tiled=True)
    key_ids = jnp.arange(gathered.shape[0], dtype=jnp.int32)
    visible = (key_ids[None, :] <= positions[:, None])[None]
    scores = (
        jnp.einsum("qhc,kc->hqk", query_heads, gathered, preferred_element_type=F32) * SCORE_SCALE
    )
    scores = jnp.where(visible, scores, MASKED)
    peak = jnp.max(scores, axis=2, keepdims=True)
    raw = jnp.where(visible, jnp.exp(scores - peak), 0.0)
    attend = raw / jnp.sum(raw, axis=2, keepdims=True)
    value_dot = jnp.einsum(
        "qhv,kv->hqk", grad_heads, gathered[:, :val_width], preferred_element_type=F32
    )
    row_dot = jnp.sum(attend * value_dot, axis=2, keepdims=True)
    score_grad = (attend * (value_dot - row_dot)).astype(BF16)
    query_grad = (
        jnp.einsum("hqk,kc->qhc", score_grad, gathered, preferred_element_type=F32) * SCORE_SCALE
    )
    key_grad = (
        jnp.einsum("hqk,qhc->kc", score_grad, query_heads, preferred_element_type=F32)
        * SCORE_SCALE
    )
    value_grad = jnp.einsum(
        "hqk,qhv->kv", attend.astype(BF16), grad_heads, preferred_element_type=F32
    )
    latent_part = key_grad + jnp.pad(value_grad, ((0, 0), (0, lat_width - val_width)))
    latent_grad = sum_latent_grad(latent_part)
    query_out = query_grad.astype(BF16).reshape(q_rows, head_count * lat_width)
    return (query_out, latent_grad)


def per_device(
    moe_input, moe_grad, routes, gates, w_gate, w_up, w_down, queries, out_grad, positions, latents
):
    if lax.axis_size("exp") <= routes.shape[1]:
        return near_layers(
            moe_input, moe_grad, routes, gates, w_gate, w_up, w_down,
            queries, out_grad, positions, latents,
        )
    query_out, latent_grad = attention_layer(queries, out_grad, positions, latents)
    input_grad = far_expert_layer(moe_input, moe_grad, routes, gates, w_gate, w_up, w_down)
    return (input_grad, query_out, latent_grad)


def solution(mesh):
    return jax.shard_map(
        per_device,
        mesh=mesh,
        in_specs=(
            P("exp", "ctx"),
            P("exp", "ctx"),
            P("exp", None),
            P("exp", None),
            P("exp", "ctx", None),
            P("exp", "ctx", None),
            P("exp", None, "ctx"),
            P("ctx", "exp"),
            P("ctx", "exp"),
            P("ctx"),
            P("ctx", None),
        ),
        out_specs=(P("exp", "ctx"), P("ctx", "exp"), P(("ctx", "exp"), None)),
        check_vma=False,
    )
```

time: 469 us -> 183 us (0.39)
  waiting for transfers between devices: 353 us -> 77.2 us
  Pallas kernels: 0 us -> 46.2 us
  starting transfers between devices: 15.8 us -> 54.3 us
  local copies, waits for them, and re-layouts: 41.2 us -> 4.29 us
  matrix products: 35.9 us -> 0 us
  between operations: 13.9 us -> 0.95 us
  other arithmetic: 9 us -> 0 us
    psum x1 -> x0, waiting for transfers between devices: 156 us -> none  [expert_layer(): lax.psum(down_part.astype(jnp.bfloat16), 'ctx').astype(jnp.float32)]
    all_to_all x3 -> x0, waiting for transfers between devices: 143 us -> none  [the longest x1 63.5 us: expert_layer(): lax.all_to_all(route_part, 'exp', split_axis=0, concat_axis=0, tiled=True)]
    ppermute x0 -> x39, waiting for transfers between devices: none -> 77.2 us  [the longest x21 46.4 us: plane_shift(): return lax.ppermute(value, ('ctx', 'exp'), pairs)]
    ppermute x0 -> x39, starting transfers between devices: none -> 54.3 us  [the longest x18 29.7 us: shift(): return lax.ppermute(value, 'exp', pairs)]
    reduce_scatter x1 -> x0, waiting for transfers between devices: 53.1 us -> none  [attention_layer(): lax.psum_scatter(latent_part, ('ctx', 'exp'), scatter_dimension=0, tiled=...]
    pallas_call x0 -> x32, Pallas kernels: none -> 46.2 us  [call(): pl.pallas_call(body, out_shape=out_shape, grid=grid, in_specs=list(in_spe...]
    dot_general x9 -> x0, matrix products: 33.7 us -> none  [the longest x1 7.66 us: expert_layer(): jnp.einsum('sekh,edh->sekd', gate_back, w_gate, preferred_element_type=jn...]
    scatter x2 -> x0, local copies, waits for them, and re-layouts: 29.7 us -> none  [the longest x1 16 us: expert_layer(): send_grad = empty.at[target].set(moe_grad[source_rows]).reshape(send_shape)]
  transfers between devices with their start and end apart: 6 -> 39, of which waited for: 5 -> 16; matrix products, arithmetic and copies ran while one was open for 14% -> 0% of each run, Pallas kernels for 0% -> 19%
where the time goes in v2:
time: 183 us
  waiting for transfers between devices  77.2 us (42%)
  starting transfers between devices  54.3 us (30%)
  Pallas kernels  46.2 us (25%)
  local copies, waits for them, and re-layouts  4.29 us (2%)
    ppermute x21, waiting for transfers between devices, plane_shift(): return lax.ppermute(value, ('ctx', 'exp'), pairs)  46.4 us
    pallas_call x32, Pallas kernels, call(): pl.pallas_call(body, out_shape=out_shape, grid=grid, in_specs=list(in_spe...  46.2 us
    ppermute x18, waiting for transfers between devices, shift(): return lax.ppermute(value, 'exp', pairs)  30.8 us
    ppermute x18, starting transfers between devices, shift(): return lax.ppermute(value, 'exp', pairs)  29.7 us
    ppermute x21, starting transfers between devices, plane_shift(): return lax.ppermute(value, ('ctx', 'exp'), pairs)  24.6 us
    unnamed x18, local copies, waits for them, and re-layouts  4.14 us
  transfers between devices with their start and end apart: 39, of which 16 were waited for; matrix products, arithmetic and copies ran while one was open for 0% of the time, Pallas kernels for 19%

profile of v2, /device:TPU:0, one launch (start us, length us, event | category | flops | bytes accessed | tf_op | source)
XLA Modules:
  0.0 182.9 jit_solution(10304515414323240033)
XLA Ops:
  6.5 6.2 %first_products.1 = (bf16[2,2,3,160,256]{4,3,2,1,0:T(8,128)(2,1)S(1)}, bf16[2,2,3,160,256]{4,3,2,1,0:T(8,128)(2,1)S(1)}, bf16[2,896,1024]{2,1,0:T(8,128)(2,1)S(1...) custom-call(s32[14]{0:T(128)S(1)} %stack.47.refs_0_, bf16[128,1920]{1,0:T(8,128)(2,1)S(1)} %pack_tokens.1.refs_1_, ...), custom_call_target="tpu_custom_call" | custom-call | flops 10000000000 | bytes 30000000 | tf_op jit(solution)/shard_map/first_products/pallas_call | solution.py:48
  12.8 2.9 %collective-permute-start.1 = (bf16[2,2,3,160,256]{4,3,2,1,0:T(8,128)(2,1)S(1)}, bf16[2,2,3,160,256]{4,3,2,1,0:T(8,128)(2,1)S(1)}, u32[]{:S(2)}, u32[]{:S(2)}) collective-permute-start(bf16[2,2,3,160,256]{4,3,2,1,0:T(8,128)(2,1)S(1)} %get-tuple-element.25), channel_id=1, source_target_pairs={{0,8},{1,17},{2,10},{3,19},{4,12},{5,21},{6,14},{7,23},{8,0},{9,25... | collective-permute-start | bytes 2949128 | tf_op jit(solution)/shard_map/a_sums_near/ppermute | solution.py:336
  17.3 10.5 %collective-permute-done.1.refs_0_ = bf16[2,2,3,160,256]{4,3,2,1,0:T(8,128)(2,1)S(1)} collective-permute-done((bf16[2,2,3,160,256]{4,3,2,1,0:T(8,128)(2,1)S(1)}, bf16[2,2,3,160,256]{4,3,2,1,0:T(8,128)(2,1)S(1)}, u32[]{:S(2)}, u32[]{:S(2)}) %collective-permute-start.1) | collective-permute-done | bytes 983072 | tf_op jit(solution)/shard_map/a_sums_near/ppermute | solution.py:336
  27.9 2.1 %collective-permute-start.2 = (bf16[2,3,160,256]{3,2,1,0:T(8,128)(2,1)S(1)}, bf16[2,3,160,256]{3,2,1,0:T(8,128)(2,1)S(1)}, u32[]{:S(2)}, u32[]{:S(2)}) collective-permute-start(bf16[2,3,160,256]{3,2,1,0:T(8,128)(2,1)S(1)} %add_parts.14.refs_3_), channel_id=1, source_target_pairs={{0,16},{1,9},{2,18},{3,11},{4,20},{5,13},{6,22},{7,15},{8,24},{9,1... | collective-permute-start | bytes 1474568 | tf_op jit(solution)/shard_map/a_sums_far/ppermute | solution.py:336
  32.3 7.8 %collective-permute-done.5.refs_6_ = bf16[576,256]{1,0:T(8,128)(2,1)S(1)} collective-permute-done((bf16[576,256]{1,0:T(8,128)(2,1)S(1)}, bf16[576,256]{1,0:T(8,128)(2,1)S(1)}, u32[]{:S(2)}, u32[]{:S(2)}) %collective-permute-start.5) | collective-permute-done | bytes 294944 | tf_op jit(solution)/shard_map/keys_near_move/ppermute | solution.py:336
  42.4 4.2 %products.3 = (bf16[2,2,3,160,256]{4,3,2,1,0:T(8,128)(2,1)S(1)}, bf16[2,2,3,160,256]{4,3,2,1,0:T(8,128)(2,1)S(1)}) custom-call(s32[14]{0:T(128)S(1)} %stack.47.refs_0_, bf16[128,1920]{1,0:T(8,128)(2,1)S(1)} %collective-permute-done.7.refs_1_, bf16[128,1920]{1,0:T(8,128)(2,1)S(1)} %collective-permute-done.8.refs_2_, ...), custom_call_target="tpu_custom_call" | custom-call | flops 2000000000 | bytes 6000001 | tf_op jit(solution)/shard_map/products/pallas_call | solution.py:48
  48.2 3.6 %collective-permute-start.13 = (bf16[128,1920]{1,0:T(8,128)(2,1)S(1)}, bf16[128,1920]{1,0:T(8,128)(2,1)S(1)}, u32[]{:S(2)}, u32[]{:S(2)}) collective-permute-start(bf16[128,1920]{1,0:T(8,128)(2,1)S(1)} %pack_tokens.1.refs_1_), channel_id=1, source_target_pairs={{0,6},{1,7},{2,4},{3,5},{4,2},{5,3},{6,0},{7,1},{8,14},{9,15},{10,... | collective-permute-start | bytes 1474568 | tf_op jit(solution)/shard_map/from_3_move/ppermute | solution.py:30
  51.8 4.9 %attention.1 = (bf16[128,1152]{1,0:T(8,128)(2,1)}, bf16[4,4,32,576]{3,2,1,0:T(8,128)(2,1)S(1)}, bf16[4,4,32,576]{3,2,1,0:T(8,128)(2,1)S(1)}) custom-call(s32[14]{0:T(128)S(1)} %stack.47.refs_0_, bf16[128,1152]{1,0:T(8,128)(2,1)S(1)} %copy-done, bf16[128,1024]{1,0:T(8,128)(2,1)S(1)} %copy-done.2, s32[1,128]{1,0:T(1,128)S(1)} %bitcast.51, ...), custom_call_target="tpu_custom_call" | custom-call | flops 2000000000 | bytes 6000001 | tf_op jit(solution)/shard_map/attention/pallas_call | solution.py:48
  57.3 3.6 %collective-permute-done.13.refs_1_ = bf16[128,1920]{1,0:T(8,128)(2,1)S(1)} collective-permute-done((bf16[128,1920]{1,0:T(8,128)(2,1)S(1)}, bf16[128,1920]{1,0:T(8,128)(2,1)S(1)}, u32[]{:S(2)}, u32[]{:S(2)}) %collective-permute-start.13) | collective-permute-done | bytes 491552 | tf_op jit(solution)/shard_map/from_3_move/ppermute | solution.py:30
  63.2 8.0 %collective-permute-done.9.refs_4_ = bf16[2,2,2,160,256]{4,3,2,1,0:T(8,128)(2,1)S(1)} collective-permute-done((bf16[2,2,2,160,256]{4,3,2,1,0:T(8,128)(2,1)S(1)}, bf16[2,2,2,160,256]{4,3,2,1,0:T(8,128)(2,1)S(1)}, u32[]{:S(2)}, u32[]{:S(2)}) %collective-permute-start.9) | collective-permute-done | bytes 655392 | tf_op jit(solution)/shard_map/a_both_near/ppermute | solution.py:336
  71.3 4.7 %route_sums.4 = (f32[1,128,896]{2,1,0:T(8,128)S(1)}, bf16[1,128,896]{2,1,0:T(8,128)(2,1)S(1)}) custom-call(s32[14]{0:T(128)S(1)} %stack.47.refs_0_, bf16[128,1920]{1,0:T(8,128)(2,1)S(1)} %pack_tokens.1.refs_1_, bf16[128,1920]{1,0:T(8,128)(2,1)S(1)} %collective-permute-done.refs_2_, bf16[2,2,2,160,256]{4,3,2,1,0:T(8,128)(2,1)S(1)} %join.4.refs_2_.refs_3_, ...), custom_call_target="tpu_custom_call" | custom-call | flops 2000000000 | bytes 6000001 | tf_op jit(solution)/shard_map/route_sums/pallas_call | solution.py:48
  75.9 4.2 %products.4 = (bf16[2,2,3,160,256]{4,3,2,1,0:T(8,128)(2,1)S(1)}, bf16[2,2,3,160,256]{4,3,2,1,0:T(8,128)(2,1)S(1)}) custom-call(s32[14]{0:T(128)S(1)} %stack.47.refs_0_, bf16[128,1920]{1,0:T(8,128)(2,1)S(1)} %collective-permute-done.13.refs_1_, bf16[128,1920]{1,0:T(8,128)(2,1)S(1)} %collective-permute-done.14.refs_2_, ...), custom_call_target="tpu_custom_call" | custom-call | flops 2000000000 | bytes 6000001 | tf_op jit(solution)/shard_map/products/pallas_call | solution.py:48
  81.7 2.1 %collective-permute-start.18 = (bf16[128,1920]{1,0:T(8,128)(2,1)S(1)}, bf16[128,1920]{1,0:T(8,128)(2,1)S(1)}, u32[]{:S(2)}, u32[]{:S(2)}) collective-permute-start(bf16[128,1920]{1,0:T(8,128)(2,1)S(1)} %collective-permute-done.13.refs_1_), channel_id=1, source_target_pairs={{0,2},{1,3},{2,0},{3,1},{4,6},{5,7},{6,4},{7,5},{8,10},{9,11},{10,... | collective-permute-start | bytes 1474568 | tf_op jit(solution)/shard_map/from_2_move/ppermute | solution.py:30
  84.7 10.0 %collective-permute-done.18.refs_1_ = bf16[128,1920]{1,0:T(8,128)(2,1)S(1)} collective-permute-done((bf16[128,1920]{1,0:T(8,128)(2,1)S(1)}, bf16[128,1920]{1,0:T(8,128)(2,1)S(1)}, u32[]{:S(2)}, u32[]{:S(2)}) %collective-permute-start.18) | collective-permute-done | bytes 491552 | tf_op jit(solution)/shard_map/from_2_move/ppermute | solution.py:30
  95.6 2.2 %collective-permute-done.20.refs_0_ = bf16[2,2,3,160,256]{4,3,2,1,0:T(8,128)(2,1)S(1)} collective-permute-done((bf16[2,2,3,160,256]{4,3,2,1,0:T(8,128)(2,1)S(1)}, bf16[2,2,3,160,256]{4,3,2,1,0:T(8,128)(2,1)S(1)}, u32[]{:S(2)}, u32[]{:S(2)}) %collective-permute-start.20) | collective-permute-done | bytes 983072 | tf_op jit(solution)/shard_map/c_sums_near/ppermute | solution.py:336
  98.0 4.2 %products.5 = (bf16[2,2,3,160,256]{4,3,2,1,0:T(8,128)(2,1)S(1)}, bf16[2,2,3,160,256]{4,3,2,1,0:T(8,128)(2,1)S(1)}) custom-call(s32[14]{0:T(128)S(1)} %stack.47.refs_0_, bf16[128,1920]{1,0:T(8,128)(2,1)S(1)} %collective-permute-done.18.refs_1_, bf16[128,1920]{1,0:T(8,128)(2,1)S(1)} %collective-permute-done.19.refs_2_, ...), custom_call_target="tpu_custom_call" | custom-call | flops 2000000000 | bytes 6000001 | tf_op jit(solution)/shard_map/products/pallas_call | solution.py:48
  103.8 2.2 %collective-permute-start.23 = (bf16[4,32,576]{2,1,0:T(8,128)(2,1)S(1)}, bf16[4,32,576]{2,1,0:T(8,128)(2,1)S(1)}, u32[]{:S(2)}, u32[]{:S(2)}) collective-permute-start(bf16[4,32,576]{2,1,0:T(8,128)(2,1)S(1)} %get-tuple-element.49), channel_id=1, source_target_pairs={{0,2},{1,3},{2,0},{3,1},{4,6},{5,7},{6,4},{7,5},{8,10},{9,11},{10,... | collective-permute-start | bytes 442376 | tf_op jit(solution)/shard_map/latent_terms/ppermute | solution.py:30
  106.0 2.1 %collective-permute-start.24 = (bf16[4,32,576]{2,1,0:T(8,128)(2,1)S(1)}, bf16[4,32,576]{2,1,0:T(8,128)(2,1)S(1)}, u32[]{:S(2)}, u32[]{:S(2)}) collective-permute-start(bf16[4,32,576]{2,1,0:T(8,128)(2,1)S(1)} %get-tuple-element.48), channel_id=1, source_target_pairs={{0,4},{1,5},{2,6},{3,7},{4,0},{5,1},{6,2},{7,3},{8,12},{9,13},{10,... | collective-permute-start | bytes 442376 | tf_op jit(solution)/shard_map/latent_terms/ppermute | solution.py:30
  108.1 2.6 %collective-permute-done.17.refs_4_ = bf16[2,2,2,160,256]{4,3,2,1,0:T(8,128)(2,1)S(1)} collective-permute-done((bf16[2,2,2,160,256]{4,3,2,1,0:T(8,128)(2,1)S(1)}, bf16[2,2,2,160,256]{4,3,2,1,0:T(8,128)(2,1)S(1)}, u32[]{:S(2)}, u32[]{:S(2)}) %collective-permute-start.17) | collective-permute-done | bytes 655392 | tf_op jit(solution)/shard_map/b_both_near/ppermute | solution.py:336
  110.8 3.0 %collective-permute-start.25 = (bf16[4,32,576]{2,1,0:T(8,128)(2,1)S(1)}, bf16[4,32,576]{2,1,0:T(8,128)(2,1)S(1)}, u32[]{:S(2)}, u32[]{:S(2)}) collective-permute-start(bf16[4,32,576]{2,1,0:T(8,128)(2,1)S(1)} %get-tuple-element.47), channel_id=1, source_target_pairs={{0,6},{1,7},{2,4},{3,5},{4,2},{5,3},{6,0},{7,1},{8,14},{9,15},{10,... | collective-permute-start | bytes 442376 | tf_op jit(solution)/shard_map/latent_terms/ppermute | solution.py:30
  113.8 4.5 %route_sums.5 = (f32[1,128,896]{2,1,0:T(8,128)S(1)}, bf16[1,128,896]{2,1,0:T(8,128)(2,1)S(1)}) custom-call(s32[14]{0:T(128)S(1)} %stack.47.refs_0_, bf16[128,1920]{1,0:T(8,128)(2,1)S(1)} %collective-permute-done.7.refs_1_, bf16[128,1920]{1,0:T(8,128)(2,1)S(1)} %collective-permute-done.8.refs_2_, bf16[2,2,2,160,256]{4,3,2,1,0:T(8,128)(2,1)S(1)} %join.5.refs_2_.refs_3_, ...), custom_call_target="tpu_custom_call" | custom-call | flops 2000000000 | bytes 6000001 | tf_op jit(solution)/shard_map/route_sums/pallas_call | solution.py:48
  122.6 4.8 %collective-permute-done.27.refs_1_ = bf16[2,2,160,256]{3,2,1,0:T(8,128)(2,1)S(1)} collective-permute-done((bf16[2,2,160,256]{3,2,1,0:T(8,128)(2,1)S(1)}, bf16[2,2,160,256]{3,2,1,0:T(8,128)(2,1)S(1)}, u32[]{:S(2)}, u32[]{:S(2)}) %collective-permute-start.27) | collective-permute-done | bytes 327712 | tf_op jit(solution)/shard_map/c_own_far/ppermute | solution.py:336
  129.8 2.9 %collective-permute-start.26 = (bf16[128,896]{1,0:T(8,128)(2,1)S(1)}, bf16[128,896]{1,0:T(8,128)(2,1)S(1)}, u32[]{:S(2)}, u32[]{:S(2)}) collective-permute-start(bf16[128,896]{1,0:T(8,128)(2,1)S(1)} %add_parts.19.refs_2_), channel_id=1, source_target_pairs={{0,2},{1,3},{2,0},{3,1},{4,6},{5,7},{6,4},{7,5},{8,10},{9,11},{10,... | collective-permute-start | bytes 688136 | tf_op jit(solution)/shard_map/b_back_move/ppermute | solution.py:30
  132.7 6.3 %collective-permute-done.31 = bf16[2,32,576]{2,1,0:T(8,128)(2,1)S(1)} collective-permute-done((bf16[2,32,576]{2,1,0:T(8,128)(2,1)S(1)}, bf16[2,32,576]{2,1,0:T(8,128)(2,1)S(1)}, u32[]{:S(2)}, u32[]{:S(2)}) %collective-permute-start.31) | collective-permute-done | bytes 73760 | tf_op jit(solution)/shard_map/crossed_move/ppermute | solution.py:336
  139.9 4.5 %route_sums.6 = (f32[1,128,896]{2,1,0:T(8,128)S(1)}, bf16[1,128,896]{2,1,0:T(8,128)(2,1)S(1)}) custom-call(s32[14]{0:T(128)S(1)} %stack.47.refs_0_, bf16[128,1920]{1,0:T(8,128)(2,1)S(1)} %collective-permute-done.13.refs_1_, bf16[128,1920]{1,0:T(8,128)(2,1)S(1)} %collective-permute-done.14.refs_2_, bf16[2,2,2,160,256]{4,3,2,1,0:T(8,128)(2,1)S(1)} %join.6.refs_2_.refs_3_, ...), custom_call_target="tpu_custom_call" | custom-call | flops 2000000000 | bytes 6000001 | tf_op jit(solution)/shard_map/route_sums/pallas_call | solution.py:48
  144.4 2.4 %collective-permute-start.32 = (bf16[1,128,896]{2,1,0:T(8,128)(2,1)S(1)}, bf16[1,128,896]{2,1,0:T(8,128)(2,1)S(1)}, u32[]{:S(2)}, u32[]{:S(2)}) collective-permute-start(bf16[1,128,896]{2,1,0:T(8,128)(2,1)S(1)} %get-tuple-element.42.refs_3_), channel_id=1, source_target_pairs={{0,1},{1,0},{2,3},{3,2},{4,5},{5,4},{6,7},{7,6},{8,9},{9,8},{10,11... | collective-permute-start | bytes 688136 | tf_op jit(solution)/shard_map/c_other_move/ppermute | solution.py:30
  148.4 2.3 %collective-permute-start.34 = (bf16[128,896]{1,0:T(8,128)(2,1)S(1)}, bf16[128,896]{1,0:T(8,128)(2,1)S(1)}, u32[]{:S(2)}, u32[]{:S(2)}) collective-permute-start(bf16[128,896]{1,0:T(8,128)(2,1)S(1)} %add_parts.23.refs_2_), channel_id=1, source_target_pairs={{0,6},{1,7},{2,4},{3,5},{4,2},{5,3},{6,0},{7,1},{8,14},{9,15},{10,... | collective-permute-start | bytes 688136 | tf_op jit(solution)/shard_map/c_back_move/ppermute | solution.py:30
  151.4 3.8 %collective-permute-done.35 = bf16[32,576]{1,0:T(8,128)(2,1)S(1)} collective-permute-done((bf16[32,576]{1,0:T(8,128)(2,1)S(1)}, bf16[32,576]{1,0:T(8,128)(2,1)S(1)}, u32[]{:S(2)}, u32[]{:S(2)}) %collective-permute-start.35) | collective-permute-done | bytes 36896 | tf_op jit(solution)/shard_map/last_move/ppermute | solution.py:336
  155.8 2.1 %collective-permute-done.34 = bf16[128,896]{1,0:T(8,128)(2,1)S(1)} collective-permute-done((bf16[128,896]{1,0:T(8,128)(2,1)S(1)}, bf16[128,896]{1,0:T(8,128)(2,1)S(1)}, u32[]{:S(2)}, u32[]{:S(2)}) %collective-permute-start.34) | collective-permute-done | bytes 229408 | tf_op jit(solution)/shard_map/c_back_move/ppermute | solution.py:30
  158.8 4.5 %route_sums.7 = (f32[1,128,896]{2,1,0:T(8,128)S(1)}, bf16[1,128,896]{2,1,0:T(8,128)(2,1)S(1)}) custom-call(s32[14]{0:T(128)S(1)} %stack.47.refs_0_, bf16[128,1920]{1,0:T(8,128)(2,1)S(1)} %collective-permute-done.18.refs_1_, bf16[128,1920]{1,0:T(8,128)(2,1)S(1)} %collective-permute-done.19.refs_2_, bf16[2,2,2,160,256]{4,3,2,1,0:T(8,128)(2,1)S(1)} %join.7.refs_2_.refs_3_, ...), custom_call_target="tpu_custom_call" | custom-call | flops 2000000000 | bytes 6000001 | tf_op jit(solution)/shard_map/route_sums/pallas_call | solution.py:48
  164.9 6.5 %collective-permute-start.38 = (bf16[128,896]{1,0:T(8,128)(2,1)S(1)}, bf16[128,896]{1,0:T(8,128)(2,1)S(1)}, u32[]{:S(2)}, u32[]{:S(2)}) collective-permute-start(bf16[128,896]{1,0:T(8,128)(2,1)S(1)} %add_parts.26.refs_2_), channel_id=1, source_target_pairs={{0,4},{1,5},{2,6},{3,7},{4,0},{5,1},{6,2},{7,3},{8,12},{9,13},{10,... | collective-permute-start | bytes 688136 | tf_op jit(solution)/shard_map/d_back_move/ppermute | solution.py:30
  171.4 10.8 %collective-permute-done.38 = bf16[128,896]{1,0:T(8,128)(2,1)S(1)} collective-permute-done((bf16[128,896]{1,0:T(8,128)(2,1)S(1)}, bf16[128,896]{1,0:T(8,128)(2,1)S(1)}, u32[]{:S(2)}, u32[]{:S(2)}) %collective-permute-start.38) | collective-permute-done | bytes 229408 | tf_op jit(solution)/shard_map/d_back_move/ppermute | solution.py:30
  (100 shorter events, 35.7 us)
Async XLA Ops:
  12.8 15.0 %collective-permute-start.1 = (bf16[2,2,3,160,256]{4,3,2,1,0:T(8,128)(2,1)S(1)}, bf16[2,2,3,160,256]{4,3,2,1,0:T(8,128)(2,1)S(1)}, u32[]{:S(2)}, u32[]{:S(2)}) collective-permute-start(bf16[2,2,3,160,256]{4,3,2,1,0:T(8,128)(2,1)S(1)} %get-tuple-element.25), channel_id=1, source_target_pairs={{0,8},{1,17},{2,10},{3,19},{4,12},{5,21},{6,14},{7,23},{8,0},{9,25... | collective-permute-start | bytes 2949128 | tf_op jit(solution)/shard_map/a_sums_near/ppermute | solution.py:336
  15.7 14.3 %collective-permute-start.7 = (bf16[128,1920]{1,0:T(8,128)(2,1)S(1)}, bf16[128,1920]{1,0:T(8,128)(2,1)S(1)}, u32[]{:S(2)}, u32[]{:S(2)}) collective-permute-start(bf16[128,1920]{1,0:T(8,128)(2,1)S(1)} %pack_tokens.1.refs_1_), channel_id=1, source_target_pairs={{0,2},{1,3},{2,0},{3,1},{4,6},{5,7},{6,4},{7,5},{8,10},{9,11},{10,... | collective-permute-start | bytes 1474568 | tf_op jit(solution)/shard_map/from_1_move/ppermute | solution.py:30
  27.9 12.8 %collective-permute-start.2 = (bf16[2,3,160,256]{3,2,1,0:T(8,128)(2,1)S(1)}, bf16[2,3,160,256]{3,2,1,0:T(8,128)(2,1)S(1)}, u32[]{:S(2)}, u32[]{:S(2)}) collective-permute-start(bf16[2,3,160,256]{3,2,1,0:T(8,128)(2,1)S(1)} %add_parts.14.refs_3_), channel_id=1, source_target_pairs={{0,16},{1,9},{2,18},{3,11},{4,20},{5,13},{6,22},{7,15},{8,24},{9,1... | collective-permute-start | bytes 1474568 | tf_op jit(solution)/shard_map/a_sums_far/ppermute | solution.py:336
  30.0 12.4 %collective-permute-start.8 = (bf16[128,1920]{1,0:T(8,128)(2,1)S(1)}, bf16[128,1920]{1,0:T(8,128)(2,1)S(1)}, u32[]{:S(2)}, u32[]{:S(2)}) collective-permute-start(bf16[128,1920]{1,0:T(8,128)(2,1)S(1)} %collective-permute-done.7.refs_1_), channel_id=1, source_target_pairs={{0,1},{1,0},{2,3},{3,2},{4,5},{5,4},{6,7},{7,6},{8,9},{9,8},{10,11... | collective-permute-start | bytes 1474568 | tf_op jit(solution)/shard_map/other_1_move/ppermute | solution.py:30
  30.0 10.0 %collective-permute-start.5 = (bf16[576,256]{1,0:T(8,128)(2,1)S(1)}, bf16[576,256]{1,0:T(8,128)(2,1)S(1)}, u32[]{:S(2)}, u32[]{:S(2)}) collective-permute-start(bf16[576,256]{1,0:T(8,128)(2,1)S(1)} %bitcast.38), channel_id=1, source_target_pairs={{0,8},{1,17},{2,10},{3,19},{4,12},{5,21},{6,14},{7,23},{8,0},{9,25... | collective-permute-start | bytes 884744 | tf_op jit(solution)/shard_map/keys_near_move/ppermute | solution.py:336
  31.6 20.2 %collective-permute-start.4 = (bf16[576,256]{1,0:T(8,128)(2,1)S(1)}, bf16[576,256]{1,0:T(8,128)(2,1)S(1)}, u32[]{:S(2)}, u32[]{:S(2)}) collective-permute-start(bf16[576,256]{1,0:T(8,128)(2,1)S(1)} %bitcast.39), channel_id=1, source_target_pairs={{0,16},{1,9},{2,18},{3,11},{4,20},{5,13},{6,22},{7,15},{8,24},{9,1... | collective-permute-start | bytes 884744 | tf_op jit(solution)/shard_map/keys_far_move/ppermute | solution.py:336
  40.0 11.8 %collective-permute-start.6 = (bf16[576,256]{1,0:T(8,128)(2,1)S(1)}, bf16[576,256]{1,0:T(8,128)(2,1)S(1)}, u32[]{:S(2)}, u32[]{:S(2)}) collective-permute-start(bf16[576,256]{1,0:T(8,128)(2,1)S(1)} %collective-permute-done.5.refs_6_), channel_id=1, source_target_pairs={{0,16},{1,9},{2,18},{3,11},{4,20},{5,13},{6,22},{7,15},{8,24},{9,1... | collective-permute-start | bytes 884744 | tf_op jit(solution)/shard_map/keys_both_move/ppermute | solution.py:336
  41.0 15.7 %collective-permute-start.3 = (bf16[2,2,160,256]{3,2,1,0:T(8,128)(2,1)S(1)}, bf16[2,2,160,256]{3,2,1,0:T(8,128)(2,1)S(1)}, u32[]{:S(2)}, u32[]{:S(2)}) collective-permute-start(bf16[2,2,160,256]{3,2,1,0:T(8,128)(2,1)S(1)} %hidden_back.4.refs_6_.refs_0_), channel_id=1, source_target_pairs={{0,16},{1,9},{2,18},{3,11},{4,20},{5,13},{6,22},{7,15},{8,24},{9,1... | collective-permute-start | bytes 983048 | tf_op jit(solution)/shard_map/a_own_far/ppermute | solution.py:336
  46.6 14.9 %collective-permute-start.10 = (bf16[2,2,3,160,256]{4,3,2,1,0:T(8,128)(2,1)S(1)}, bf16[2,2,3,160,256]{4,3,2,1,0:T(8,128)(2,1)S(1)}, u32[]{:S(2)}, u32[]{:S(2)}) collective-permute-start(bf16[2,2,3,160,256]{4,3,2,1,0:T(8,128)(2,1)S(1)} %get-tuple-element.32), channel_id=1, source_target_pairs={{0,8},{1,17},{2,10},{3,19},{4,12},{5,21},{6,14},{7,23},{8,0},{9,25... | collective-permute-start | bytes 2949128 | tf_op jit(solution)/shard_map/b_sums_near/ppermute | solution.py:336
  48.2 12.8 %collective-permute-start.13 = (bf16[128,1920]{1,0:T(8,128)(2,1)S(1)}, bf16[128,1920]{1,0:T(8,128)(2,1)S(1)}, u32[]{:S(2)}, u32[]{:S(2)}) collective-permute-start(bf16[128,1920]{1,0:T(8,128)(2,1)S(1)} %pack_tokens.1.refs_1_), channel_id=1, source_target_pairs={{0,6},{1,7},{2,4},{3,5},{4,2},{5,3},{6,0},{7,1},{8,14},{9,15},{10,... | collective-permute-start | bytes 1474568 | tf_op jit(solution)/shard_map/from_3_move/ppermute | solution.py:30
  56.7 14.5 %collective-permute-start.9 = (bf16[2,2,2,160,256]{4,3,2,1,0:T(8,128)(2,1)S(1)}, bf16[2,2,2,160,256]{4,3,2,1,0:T(8,128)(2,1)S(1)}, u32[]{:S(2)}, u32[]{:S(2)}) collective-permute-start(bf16[2,2,2,160,256]{4,3,2,1,0:T(8,128)(2,1)S(1)} %join.4.refs_2_.refs_3_), channel_id=1, source_target_pairs={{0,8},{1,17},{2,10},{3,19},{4,12},{5,21},{6,14},{7,23},{8,0},{9,25... | collective-permute-start | bytes 1966088 | tf_op jit(solution)/shard_map/a_both_near/ppermute | solution.py:336
  61.0 15.0 %collective-permute-start.14 = (bf16[128,1920]{1,0:T(8,128)(2,1)S(1)}, bf16[128,1920]{1,0:T(8,128)(2,1)S(1)}, u32[]{:S(2)}, u32[]{:S(2)}) collective-permute-start(bf16[128,1920]{1,0:T(8,128)(2,1)S(1)} %collective-permute-done.13.refs_1_), channel_id=1, source_target_pairs={{0,1},{1,0},{2,3},{3,2},{4,5},{5,4},{6,7},{7,6},{8,9},{9,8},{10,11... | collective-permute-start | bytes 1474568 | tf_op jit(solution)/shard_map/other_3_move/ppermute | solution.py:30
  61.0 33.7 %collective-permute-start.16 = (bf16[4,4,32,576]{3,2,1,0:T(8,128)(2,1)S(1)}, bf16[4,4,32,576]{3,2,1,0:T(8,128)(2,1)S(1)}, u32[]{:S(2)}, u32[]{:S(2)}) collective-permute-start(bf16[4,4,32,576]{3,2,1,0:T(8,128)(2,1)S(1)} %get-tuple-element.36), channel_id=1, source_target_pairs={{0,1},{1,0},{2,3},{3,2},{4,5},{5,4},{6,7},{7,6},{8,9},{9,8},{10,11... | collective-permute-start | bytes 1769480 | tf_op jit(solution)/shard_map/got_move/ppermute | solution.py:30
  61.6 22.2 %collective-permute-start.12 = (bf16[2,3,160,256]{3,2,1,0:T(8,128)(2,1)S(1)}, bf16[2,3,160,256]{3,2,1,0:T(8,128)(2,1)S(1)}, u32[]{:S(2)}, u32[]{:S(2)}) collective-permute-start(bf16[2,3,160,256]{3,2,1,0:T(8,128)(2,1)S(1)} %add_parts.15.refs_7_), channel_id=1, source_target_pairs={{0,16},{1,9},{2,18},{3,11},{4,20},{5,13},{6,22},{7,15},{8,24},{9,1... | collective-permute-start | bytes 1474568 | tf_op jit(solution)/shard_map/b_sums_far/ppermute | solution.py:336
  80.1 17.7 %collective-permute-start.20 = (bf16[2,2,3,160,256]{4,3,2,1,0:T(8,128)(2,1)S(1)}, bf16[2,2,3,160,256]{4,3,2,1,0:T(8,128)(2,1)S(1)}, u32[]{:S(2)}, u32[]{:S(2)}) collective-permute-start(bf16[2,2,3,160,256]{4,3,2,1,0:T(8,128)(2,1)S(1)} %get-tuple-element.37), channel_id=1, source_target_pairs={{0,8},{1,17},{2,10},{3,19},{4,12},{5,21},{6,14},{7,23},{8,0},{9,25... | collective-permute-start | bytes 2949128 | tf_op jit(solution)/shard_map/c_sums_near/ppermute | solution.py:336
  81.7 12.9 %collective-permute-start.18 = (bf16[128,1920]{1,0:T(8,128)(2,1)S(1)}, bf16[128,1920]{1,0:T(8,128)(2,1)S(1)}, u32[]{:S(2)}, u32[]{:S(2)}) collective-permute-start(bf16[128,1920]{1,0:T(8,128)(2,1)S(1)} %collective-permute-done.13.refs_1_), channel_id=1, source_target_pairs={{0,2},{1,3},{2,0},{3,1},{4,6},{5,7},{6,4},{7,5},{8,10},{9,11},{10,... | collective-permute-start | bytes 1474568 | tf_op jit(solution)/shard_map/from_2_move/ppermute | solution.py:30
  84.1 10.7 %collective-permute-start.15 = (bf16[2,2,160,256]{3,2,1,0:T(8,128)(2,1)S(1)}, bf16[2,2,160,256]{3,2,1,0:T(8,128)(2,1)S(1)}, u32[]{:S(2)}, u32[]{:S(2)}) collective-permute-start(bf16[2,2,160,256]{3,2,1,0:T(8,128)(2,1)S(1)} %hidden_back.5.refs_2_.refs_0_), channel_id=1, source_target_pairs={{0,16},{1,9},{2,18},{3,11},{4,20},{5,13},{6,22},{7,15},{8,24},{9,1... | collective-permute-start | bytes 983048 | tf_op jit(solution)/shard_map/b_own_far/ppermute | solution.py:336
  94.8 15.9 %collective-permute-start.17 = (bf16[2,2,2,160,256]{4,3,2,1,0:T(8,128)(2,1)S(1)}, bf16[2,2,2,160,256]{4,3,2,1,0:T(8,128)(2,1)S(1)}, u32[]{:S(2)}, u32[]{:S(2)}) collective-permute-start(bf16[2,2,2,160,256]{4,3,2,1,0:T(8,128)(2,1)S(1)} %join.5.refs_2_.refs_3_), channel_id=1, source_target_pairs={{0,8},{1,17},{2,10},{3,19},{4,12},{5,21},{6,14},{7,23},{8,0},{9,25... | collective-permute-start | bytes 1966088 | tf_op jit(solution)/shard_map/b_both_near/ppermute | solution.py:336
  98.0 21.9 %collective-permute-start.22 = (bf16[2,3,160,256]{3,2,1,0:T(8,128)(2,1)S(1)}, bf16[2,3,160,256]{3,2,1,0:T(8,128)(2,1)S(1)}, u32[]{:S(2)}, u32[]{:S(2)}) collective-permute-start(bf16[2,3,160,256]{3,2,1,0:T(8,128)(2,1)S(1)} %add_parts.17.refs_6_), channel_id=1, source_target_pairs={{0,16},{1,9},{2,18},{3,11},{4,20},{5,13},{6,22},{7,15},{8,24},{9,1... | collective-permute-start | bytes 1474568 | tf_op jit(solution)/shard_map/c_sums_far/ppermute | solution.py:336
  102.3 19.0 %collective-permute-start.28 = (bf16[2,2,3,160,256]{4,3,2,1,0:T(8,128)(2,1)S(1)}, bf16[2,2,3,160,256]{4,3,2,1,0:T(8,128)(2,1)S(1)}, u32[]{:S(2)}, u32[]{:S(2)}) collective-permute-start(bf16[2,2,3,160,256]{4,3,2,1,0:T(8,128)(2,1)S(1)} %get-tuple-element.41), channel_id=1, source_target_pairs={{0,8},{1,17},{2,10},{3,19},{4,12},{5,21},{6,14},{7,23},{8,0},{9,25... | collective-permute-start | bytes 2949128 | tf_op jit(solution)/shard_map/d_sums_near/ppermute | solution.py:336
  103.8 14.4 %collective-permute-start.23 = (bf16[4,32,576]{2,1,0:T(8,128)(2,1)S(1)}, bf16[4,32,576]{2,1,0:T(8,128)(2,1)S(1)}, u32[]{:S(2)}, u32[]{:S(2)}) collective-permute-start(bf16[4,32,576]{2,1,0:T(8,128)(2,1)S(1)} %get-tuple-element.49), channel_id=1, source_target_pairs={{0,2},{1,3},{2,0},{3,1},{4,6},{5,7},{6,4},{7,5},{8,10},{9,11},{10,... | collective-permute-start | bytes 442376 | tf_op jit(solution)/shard_map/latent_terms/ppermute | solution.py:30
  106.0 13.8 %collective-permute-start.24 = (bf16[4,32,576]{2,1,0:T(8,128)(2,1)S(1)}, bf16[4,32,576]{2,1,0:T(8,128)(2,1)S(1)}, u32[]{:S(2)}, u32[]{:S(2)}) collective-permute-start(bf16[4,32,576]{2,1,0:T(8,128)(2,1)S(1)} %get-tuple-element.48), channel_id=1, source_target_pairs={{0,4},{1,5},{2,6},{3,7},{4,0},{5,1},{6,2},{7,3},{8,12},{9,13},{10,... | collective-permute-start | bytes 442376 | tf_op jit(solution)/shard_map/latent_terms/ppermute | solution.py:30
  110.8 9.0 %collective-permute-start.25 = (bf16[4,32,576]{2,1,0:T(8,128)(2,1)S(1)}, bf16[4,32,576]{2,1,0:T(8,128)(2,1)S(1)}, u32[]{:S(2)}, u32[]{:S(2)}) collective-permute-start(bf16[4,32,576]{2,1,0:T(8,128)(2,1)S(1)} %get-tuple-element.47), channel_id=1, source_target_pairs={{0,6},{1,7},{2,4},{3,5},{4,2},{5,3},{6,0},{7,1},{8,14},{9,15},{10,... | collective-permute-start | bytes 442376 | tf_op jit(solution)/shard_map/latent_terms/ppermute | solution.py:30
  121.4 17.5 %collective-permute-start.30 = (bf16[2,3,160,256]{3,2,1,0:T(8,128)(2,1)S(1)}, bf16[2,3,160,256]{3,2,1,0:T(8,128)(2,1)S(1)}, u32[]{:S(2)}, u32[]{:S(2)}) collective-permute-start(bf16[2,3,160,256]{3,2,1,0:T(8,128)(2,1)S(1)} %add_parts.20.refs_2_), channel_id=1, source_target_pairs={{0,16},{1,9},{2,18},{3,11},{4,20},{5,13},{6,22},{7,15},{8,24},{9,1... | collective-permute-start | bytes 1474568 | tf_op jit(solution)/shard_map/d_sums_far/ppermute | solution.py:336
  127.4 12.5 %collective-permute-start.29 = (bf16[2,2,2,160,256]{4,3,2,1,0:T(8,128)(2,1)S(1)}, bf16[2,2,2,160,256]{4,3,2,1,0:T(8,128)(2,1)S(1)}, u32[]{:S(2)}, u32[]{:S(2)}) collective-permute-start(bf16[2,2,2,160,256]{4,3,2,1,0:T(8,128)(2,1)S(1)} %join.6.refs_2_.refs_3_), channel_id=1, source_target_pairs={{0,8},{1,17},{2,10},{3,19},{4,12},{5,21},{6,14},{7,23},{8,0},{9,25... | collective-permute-start | bytes 1966088 | tf_op jit(solution)/shard_map/c_both_near/ppermute | solution.py:336
  129.3 9.6 %collective-permute-start.31 = (bf16[2,32,576]{2,1,0:T(8,128)(2,1)S(1)}, bf16[2,32,576]{2,1,0:T(8,128)(2,1)S(1)}, u32[]{:S(2)}, u32[]{:S(2)}) collective-permute-start(bf16[2,32,576]{2,1,0:T(8,128)(2,1)S(1)} %get-tuple-element.50), channel_id=1, source_target_pairs={{0,8},{1,17},{2,10},{3,19},{4,12},{5,21},{6,14},{7,23},{8,0},{9,25... | collective-permute-start | bytes 221192 | tf_op jit(solution)/shard_map/crossed_move/ppermute | solution.py:336
  129.8 17.0 %collective-permute-start.11 = (bf16[1,128,896]{2,1,0:T(8,128)(2,1)S(1)}, bf16[1,128,896]{2,1,0:T(8,128)(2,1)S(1)}, u32[]{:S(2)}, u32[]{:S(2)}) collective-permute-start(bf16[1,128,896]{2,1,0:T(8,128)(2,1)S(1)} %get-tuple-element.34.refs_6_), channel_id=1, source_target_pairs={{0,1},{1,0},{2,3},{3,2},{4,5},{5,4},{6,7},{7,6},{8,9},{9,8},{10,11... | collective-permute-start | bytes 688136 | tf_op jit(solution)/shard_map/a_other_move/ppermute | solution.py:30
  129.8 17.0 %collective-permute-start.26 = (bf16[128,896]{1,0:T(8,128)(2,1)S(1)}, bf16[128,896]{1,0:T(8,128)(2,1)S(1)}, u32[]{:S(2)}, u32[]{:S(2)}) collective-permute-start(bf16[128,896]{1,0:T(8,128)(2,1)S(1)} %add_parts.19.refs_2_), channel_id=1, source_target_pairs={{0,2},{1,3},{2,0},{3,1},{4,6},{5,7},{6,4},{7,5},{8,10},{9,11},{10,... | collective-permute-start | bytes 688136 | tf_op jit(solution)/shard_map/b_back_move/ppermute | solution.py:30
  139.3 7.7 %collective-permute-start.33 = (bf16[2,2,160,256]{3,2,1,0:T(8,128)(2,1)S(1)}, bf16[2,2,160,256]{3,2,1,0:T(8,128)(2,1)S(1)}, u32[]{:S(2)}, u32[]{:S(2)}) collective-permute-start(bf16[2,2,160,256]{3,2,1,0:T(8,128)(2,1)S(1)} %hidden_back.7.refs_7_.refs_0_), channel_id=1, source_target_pairs={{0,16},{1,9},{2,18},{3,11},{4,20},{5,13},{6,22},{7,15},{8,24},{9,1... | collective-permute-start | bytes 983048 | tf_op jit(solution)/shard_map/d_own_far/ppermute | solution.py:336
  147.0 11.8 %collective-permute-start.36 = (bf16[2,2,2,160,256]{4,3,2,1,0:T(8,128)(2,1)S(1)}, bf16[2,2,2,160,256]{4,3,2,1,0:T(8,128)(2,1)S(1)}, u32[]{:S(2)}, u32[]{:S(2)}) collective-permute-start(bf16[2,2,2,160,256]{4,3,2,1,0:T(8,128)(2,1)S(1)} %join.7.refs_2_.refs_3_), channel_id=1, source_target_pairs={{0,8},{1,17},{2,10},{3,19},{4,12},{5,21},{6,14},{7,23},{8,0},{9,25... | collective-permute-start | bytes 1966088 | tf_op jit(solution)/shard_map/d_both_near/ppermute | solution.py:336
  148.4 9.5 %collective-permute-start.34 = (bf16[128,896]{1,0:T(8,128)(2,1)S(1)}, bf16[128,896]{1,0:T(8,128)(2,1)S(1)}, u32[]{:S(2)}, u32[]{:S(2)}) collective-permute-start(bf16[128,896]{1,0:T(8,128)(2,1)S(1)} %add_parts.23.refs_2_), channel_id=1, source_target_pairs={{0,6},{1,7},{2,4},{3,5},{4,2},{5,3},{6,0},{7,1},{8,14},{9,15},{10,... | collective-permute-start | bytes 688136 | tf_op jit(solution)/shard_map/c_back_move/ppermute | solution.py:30
  164.9 17.3 %collective-permute-start.38 = (bf16[128,896]{1,0:T(8,128)(2,1)S(1)}, bf16[128,896]{1,0:T(8,128)(2,1)S(1)}, u32[]{:S(2)}, u32[]{:S(2)}) collective-permute-start(bf16[128,896]{1,0:T(8,128)(2,1)S(1)} %add_parts.26.refs_2_), channel_id=1, source_target_pairs={{0,4},{1,5},{2,6},{3,7},{4,0},{5,1},{6,2},{7,3},{8,12},{9,13},{10,... | collective-permute-start | bytes 688136 | tf_op jit(solution)/shard_map/d_back_move/ppermute | solution.py:30
  (16 other events, 59.6 us)

commit v3 on v2

--- a/solution.py
+++ b/solution.py
@@ -501,22 +501,22 @@
     c = chunk("c", 1)
     d = chunk("d", 1)
     order = (
+        (functools.partial(b.multiply, [from_1, other_1]), 2),
         (a.add, 2),
         (a.turn, 2),
-        (functools.partial(b.multiply, [from_1, other_1]), 2),
         (attend, 2),
         (a.forward, 2),
         (b.add, 2),
         (start_total, 2),
         (functools.partial(c.multiply, [from_3, other_3]), 2),
-        (b.turn, 2),
+        (b.turn, 2, from_2),
         (latent_cores, 2),
         (b.forward, 2),
         (c.add, 2),
         (functools.partial(d.multiply, [from_2, other_2]), 2),
         (finish(b), 2),
         (latent_chips, 2),
-        (c.turn, 2),
+        (c.turn, 0),
         (send_back(b, (2,)), 2),
         (d.add, 2),
         (c.forward, 2),
@@ -527,8 +527,8 @@
         (d.forward, 2),
         (send_back(c, (6,)), 2),
         (latent_far, 2),
+        (finish(d), 2),
         (receive(c, False), 2),
-        (finish(d), 2),
         (send_back(d, (4,)), 2),
         (receive(d, True), 2),
     )

time: 183 us -> 177 us (0.967)
  starting transfers between devices: 54.3 us -> 51 us
  waiting for transfers between devices: 77.2 us -> 74.8 us
    ppermute x18, waiting for transfers between devices: 30.8 us -> 23.9 us  [shift(): return lax.ppermute(value, 'exp', pairs)]
    ppermute x21, waiting for transfers between devices: 46.4 us -> 51 us  [plane_shift(): return lax.ppermute(value, ('ctx', 'exp'), pairs)]
    ppermute x21, starting transfers between devices: 24.6 us -> 22.7 us  [plane_shift(): return lax.ppermute(value, ('ctx', 'exp'), pairs)]
  transfers between devices with their start and end apart: 39 -> 39, of which waited for: 16 -> 19; matrix products, arithmetic and copies ran while one was open for 0% -> 0% of each run, Pallas kernels for 19% -> 25%
where the time goes in v3:
time: 177 us
  waiting for transfers between devices  74.8 us (42%)
  starting transfers between devices  51 us (29%)
  Pallas kernels  46.1 us (26%)
  local copies, waits for them, and re-layouts  4.3 us (2%)
    ppermute x21, waiting for transfers between devices, plane_shift(): return lax.ppermute(value, ('ctx', 'exp'), pairs)  51 us
    pallas_call x32, Pallas kernels, call(): pl.pallas_call(body, out_shape=out_shape, grid=grid, in_specs=list(in_spe...  46.1 us
    ppermute x18, starting transfers between devices, shift(): return lax.ppermute(value, 'exp', pairs)  28.3 us
    ppermute x18, waiting for transfers between devices, shift(): return lax.ppermute(value, 'exp', pairs)  23.9 us
    ppermute x21, starting transfers between devices, plane_shift(): return lax.ppermute(value, ('ctx', 'exp'), pairs)  22.7 us
    unnamed x18, local copies, waits for them, and re-layouts  4.14 us
  transfers between devices with their start and end apart: 39, of which 19 were waited for; matrix products, arithmetic and copies ran while one was open for 0% of the time, Pallas kernels for 25%

profile of v3, /device:TPU:0, one launch (start us, length us, event | category | flops | bytes accessed | tf_op | source)
XLA Modules:
  0.0 177.2 jit_solution(13169173245271317195)
XLA Ops:
  5.0 2.6 %collective-permute-start.2 = (bf16[128,1920]{1,0:T(8,128)(2,1)S(1)}, bf16[128,1920]{1,0:T(8,128)(2,1)S(1)}, u32[]{:S(2)}, u32[]{:S(2)}) collective-permute-start(bf16[128,1920]{1,0:T(8,128)(2,1)S(1)} %pack_tokens.1.refs_1_), channel_id=1, source_target_pairs={{0,2},{1,3},{2,0},{3,1},{4,6},{5,7},{6,4},{7,5},{8,10},{9,11},{10,... | collective-permute-start | bytes 1474568 | tf_op jit(solution)/shard_map/from_1_move/ppermute | solution.py:30
  7.8 6.3 %first_products.1 = (bf16[2,2,3,160,256]{4,3,2,1,0:T(8,128)(2,1)S(1)}, bf16[2,2,3,160,256]{4,3,2,1,0:T(8,128)(2,1)S(1)}, bf16[2,896,1024]{2,1,0:T(8,128)(2,1)S(1...) custom-call(s32[14]{0:T(128)S(1)} %stack.47.refs_0_, bf16[128,1920]{1,0:T(8,128)(2,1)S(1)} %pack_tokens.1.refs_1_, ...), custom_call_target="tpu_custom_call" | custom-call | flops 10000000000 | bytes 30000000 | tf_op jit(solution)/shard_map/first_products/pallas_call | solution.py:48
  15.7 3.8 %collective-permute-done.2.refs_1_ = bf16[128,1920]{1,0:T(8,128)(2,1)S(1)} collective-permute-done((bf16[128,1920]{1,0:T(8,128)(2,1)S(1)}, bf16[128,1920]{1,0:T(8,128)(2,1)S(1)}, u32[]{:S(2)}, u32[]{:S(2)}) %collective-permute-start.2) | collective-permute-done | bytes 491552 | tf_op jit(solution)/shard_map/from_1_move/ppermute | solution.py:30
  19.5 1.9 %collective-permute-done.3.refs_2_ = bf16[128,1920]{1,0:T(8,128)(2,1)S(1)} collective-permute-done((bf16[128,1920]{1,0:T(8,128)(2,1)S(1)}, bf16[128,1920]{1,0:T(8,128)(2,1)S(1)}, u32[]{:S(2)}, u32[]{:S(2)}) %collective-permute-start.3) | collective-permute-done | bytes 491552 | tf_op jit(solution)/shard_map/other_1_move/ppermute | solution.py:30
  21.3 4.2 %products.3 = (bf16[2,2,3,160,256]{4,3,2,1,0:T(8,128)(2,1)S(1)}, bf16[2,2,3,160,256]{4,3,2,1,0:T(8,128)(2,1)S(1)}) custom-call(s32[14]{0:T(128)S(1)} %stack.47.refs_0_, bf16[128,1920]{1,0:T(8,128)(2,1)S(1)} %collective-permute-done.2.refs_1_, bf16[128,1920]{1,0:T(8,128)(2,1)S(1)} %collective-permute-done.3.refs_2_, ...), custom_call_target="tpu_custom_call" | custom-call | flops 2000000000 | bytes 6000001 | tf_op jit(solution)/shard_map/products/pallas_call | solution.py:48
  25.5 2.6 %collective-permute-done.1.refs_0_ = bf16[2,2,3,160,256]{4,3,2,1,0:T(8,128)(2,1)S(1)} collective-permute-done((bf16[2,2,3,160,256]{4,3,2,1,0:T(8,128)(2,1)S(1)}, bf16[2,2,3,160,256]{4,3,2,1,0:T(8,128)(2,1)S(1)}, u32[]{:S(2)}, u32[]{:S(2)}) %collective-permute-start.1) | collective-permute-done | bytes 983072 | tf_op jit(solution)/shard_map/a_sums_near/ppermute | solution.py:336
  32.3 7.8 %collective-permute-done.7.refs_6_ = bf16[576,256]{1,0:T(8,128)(2,1)S(1)} collective-permute-done((bf16[576,256]{1,0:T(8,128)(2,1)S(1)}, bf16[576,256]{1,0:T(8,128)(2,1)S(1)}, u32[]{:S(2)}, u32[]{:S(2)}) %collective-permute-start.7) | collective-permute-done | bytes 294944 | tf_op jit(solution)/shard_map/keys_near_move/ppermute | solution.py:336
  43.9 3.6 %collective-permute-start.13 = (bf16[128,1920]{1,0:T(8,128)(2,1)S(1)}, bf16[128,1920]{1,0:T(8,128)(2,1)S(1)}, u32[]{:S(2)}, u32[]{:S(2)}) collective-permute-start(bf16[128,1920]{1,0:T(8,128)(2,1)S(1)} %pack_tokens.1.refs_1_), channel_id=1, source_target_pairs={{0,6},{1,7},{2,4},{3,5},{4,2},{5,3},{6,0},{7,1},{8,14},{9,15},{10,... | collective-permute-start | bytes 1474568 | tf_op jit(solution)/shard_map/from_3_move/ppermute | solution.py:30
  47.5 2.8 %collective-permute-done.8.refs_7_ = bf16[576,256]{1,0:T(8,128)(2,1)S(1)} collective-permute-done((bf16[576,256]{1,0:T(8,128)(2,1)S(1)}, bf16[576,256]{1,0:T(8,128)(2,1)S(1)}, u32[]{:S(2)}, u32[]{:S(2)}) %collective-permute-start.8) | collective-permute-done | bytes 294944 | tf_op jit(solution)/shard_map/keys_both_move/ppermute | solution.py:336
  50.3 4.8 %attention.1 = (bf16[128,1152]{1,0:T(8,128)(2,1)}, bf16[4,4,32,576]{3,2,1,0:T(8,128)(2,1)S(1)}, bf16[4,4,32,576]{3,2,1,0:T(8,128)(2,1)S(1)}) custom-call(s32[14]{0:T(128)S(1)} %stack.47.refs_0_, bf16[128,1152]{1,0:T(8,128)(2,1)S(1)} %copy-done.1, bf16[128,1024]{1,0:T(8,128)(2,1)S(1)} %copy-done.3, s32[1,128]{1,0:T(1,128)S(1)} %bitcast.50, ...), custom_call_target="tpu_custom_call" | custom-call | flops 2000000000 | bytes 6000001 | tf_op jit(solution)/shard_map/attention/pallas_call | solution.py:48
  55.1 2.3 %collective-permute-done.5.refs_1_ = bf16[2,2,160,256]{3,2,1,0:T(8,128)(2,1)S(1)} collective-permute-done((bf16[2,2,160,256]{3,2,1,0:T(8,128)(2,1)S(1)}, bf16[2,2,160,256]{3,2,1,0:T(8,128)(2,1)S(1)}, u32[]{:S(2)}, u32[]{:S(2)}) %collective-permute-start.5) | collective-permute-done | bytes 327712 | tf_op jit(solution)/shard_map/a_own_far/ppermute | solution.py:336
  58.9 7.6 %collective-permute-start.15 = (bf16[128,1920]{1,0:T(8,128)(2,1)S(1)}, bf16[128,1920]{1,0:T(8,128)(2,1)S(1)}, u32[]{:S(2)}, u32[]{:S(2)}) collective-permute-start(bf16[128,1920]{1,0:T(8,128)(2,1)S(1)} %collective-permute-done.13.refs_1_), channel_id=1, source_target_pairs={{0,2},{1,3},{2,0},{3,1},{4,6},{5,7},{6,4},{7,5},{8,10},{9,11},{10,... | collective-permute-start | bytes 1474568 | tf_op jit(solution)/shard_map/from_2_move/ppermute | solution.py:30
  68.0 4.7 %route_sums.4 = (f32[1,128,896]{2,1,0:T(8,128)S(1)}, bf16[1,128,896]{2,1,0:T(8,128)(2,1)S(1)}) custom-call(s32[14]{0:T(128)S(1)} %stack.47.refs_0_, bf16[128,1920]{1,0:T(8,128)(2,1)S(1)} %pack_tokens.1.refs_1_, bf16[128,1920]{1,0:T(8,128)(2,1)S(1)} %collective-permute-done.refs_2_, bf16[2,2,2,160,256]{4,3,2,1,0:T(8,128)(2,1)S(1)} %join.4.refs_2_.refs_3_, ...), custom_call_target="tpu_custom_call" | custom-call | flops 2000000000 | bytes 6000001 | tf_op jit(solution)/shard_map/route_sums/pallas_call | solution.py:48
  72.7 4.2 %products.4 = (bf16[2,2,3,160,256]{4,3,2,1,0:T(8,128)(2,1)S(1)}, bf16[2,2,3,160,256]{4,3,2,1,0:T(8,128)(2,1)S(1)}) custom-call(s32[14]{0:T(128)S(1)} %stack.47.refs_0_, bf16[128,1920]{1,0:T(8,128)(2,1)S(1)} %collective-permute-done.13.refs_1_, bf16[128,1920]{1,0:T(8,128)(2,1)S(1)} %collective-permute-done.14.refs_2_, ...), custom_call_target="tpu_custom_call" | custom-call | flops 2000000000 | bytes 6000001 | tf_op jit(solution)/shard_map/products/pallas_call | solution.py:48
  78.7 1.7 collective-permute-start.16
  80.7 8.8 %collective-permute-done.16.refs_1_ = bf16[2,2,160,256]{3,2,1,0:T(8,128)(2,1)S(1)} collective-permute-done((bf16[2,2,160,256]{3,2,1,0:T(8,128)(2,1)S(1)}, bf16[2,2,160,256]{3,2,1,0:T(8,128)(2,1)S(1)}, u32[]{:S(2)}, u32[]{:S(2)}) %collective-permute-start.16) | collective-permute-done | bytes 327712 | tf_op jit(solution)/shard_map/b_own_far/ppermute | solution.py:336
  90.1 4.4 %collective-permute-done.20.refs_0_ = bf16[2,2,3,160,256]{4,3,2,1,0:T(8,128)(2,1)S(1)} collective-permute-done((bf16[2,2,3,160,256]{4,3,2,1,0:T(8,128)(2,1)S(1)}, bf16[2,2,3,160,256]{4,3,2,1,0:T(8,128)(2,1)S(1)}, u32[]{:S(2)}, u32[]{:S(2)}) %collective-permute-start.20) | collective-permute-done | bytes 983072 | tf_op jit(solution)/shard_map/c_sums_near/ppermute | solution.py:336
  94.7 4.2 %products.5 = (bf16[2,2,3,160,256]{4,3,2,1,0:T(8,128)(2,1)S(1)}, bf16[2,2,3,160,256]{4,3,2,1,0:T(8,128)(2,1)S(1)}) custom-call(s32[14]{0:T(128)S(1)} %stack.47.refs_0_, bf16[128,1920]{1,0:T(8,128)(2,1)S(1)} %collective-permute-done.15.refs_4_.refs_1_, bf16[128,1920]{1,0:T(8,128)(2,1)S(1)} %collective-permute-done.19.refs_2_, ...), custom_call_target="tpu_custom_call" | custom-call | flops 2000000000 | bytes 6000001 | tf_op jit(solution)/shard_map/products/pallas_call | solution.py:48
  102.1 3.0 %collective-permute-start.23 = (bf16[4,32,576]{2,1,0:T(8,128)(2,1)S(1)}, bf16[4,32,576]{2,1,0:T(8,128)(2,1)S(1)}, u32[]{:S(2)}, u32[]{:S(2)}) collective-permute-start(bf16[4,32,576]{2,1,0:T(8,128)(2,1)S(1)} %get-tuple-element.49), channel_id=1, source_target_pairs={{0,2},{1,3},{2,0},{3,1},{4,6},{5,7},{6,4},{7,5},{8,10},{9,11},{10,... | collective-permute-start | bytes 442376 | tf_op jit(solution)/shard_map/latent_terms/ppermute | solution.py:30
  105.1 2.4 %collective-permute-start.24 = (bf16[4,32,576]{2,1,0:T(8,128)(2,1)S(1)}, bf16[4,32,576]{2,1,0:T(8,128)(2,1)S(1)}, u32[]{:S(2)}, u32[]{:S(2)}) collective-permute-start(bf16[4,32,576]{2,1,0:T(8,128)(2,1)S(1)} %get-tuple-element.48), channel_id=1, source_target_pairs={{0,4},{1,5},{2,6},{3,7},{4,0},{5,1},{6,2},{7,3},{8,12},{9,13},{10,... | collective-permute-start | bytes 442376 | tf_op jit(solution)/shard_map/latent_terms/ppermute | solution.py:30
  107.5 4.5 %route_sums.5 = (f32[1,128,896]{2,1,0:T(8,128)S(1)}, bf16[1,128,896]{2,1,0:T(8,128)(2,1)S(1)}) custom-call(s32[14]{0:T(128)S(1)} %stack.47.refs_0_, bf16[128,1920]{1,0:T(8,128)(2,1)S(1)} %collective-permute-done.2.refs_1_, bf16[128,1920]{1,0:T(8,128)(2,1)S(1)} %collective-permute-done.3.refs_2_, bf16[2,2,2,160,256]{4,3,2,1,0:T(8,128)(2,1)S(1)} %join.5.refs_2_.refs_3_, ...), custom_call_target="tpu_custom_call" | custom-call | flops 2000000000 | bytes 6000001 | tf_op jit(solution)/shard_map/route_sums/pallas_call | solution.py:48
  112.1 5.1 %collective-permute-done.24 = bf16[4,32,576]{2,1,0:T(8,128)(2,1)S(1)} collective-permute-done((bf16[4,32,576]{2,1,0:T(8,128)(2,1)S(1)}, bf16[4,32,576]{2,1,0:T(8,128)(2,1)S(1)}, u32[]{:S(2)}, u32[]{:S(2)}) %collective-permute-start.24) | collective-permute-done | bytes 147488 | tf_op jit(solution)/shard_map/latent_terms/ppermute | solution.py:30
  120.0 6.0 %collective-permute-done.27.refs_1_ = bf16[2,2,160,256]{3,2,1,0:T(8,128)(2,1)S(1)} collective-permute-done((bf16[2,2,160,256]{3,2,1,0:T(8,128)(2,1)S(1)}, bf16[2,2,160,256]{3,2,1,0:T(8,128)(2,1)S(1)}, u32[]{:S(2)}, u32[]{:S(2)}) %collective-permute-start.27) | collective-permute-done | bytes 327712 | tf_op jit(solution)/shard_map/c_own_far/ppermute | solution.py:336
  126.1 2.3 %collective-permute-start.31 = (bf16[2,32,576]{2,1,0:T(8,128)(2,1)S(1)}, bf16[2,32,576]{2,1,0:T(8,128)(2,1)S(1)}, u32[]{:S(2)}, u32[]{:S(2)}) collective-permute-start(bf16[2,32,576]{2,1,0:T(8,128)(2,1)S(1)} %get-tuple-element.50), channel_id=1, source_target_pairs={{0,8},{1,17},{2,10},{3,19},{4,12},{5,21},{6,14},{7,23},{8,0},{9,25... | collective-permute-start | bytes 221192 | tf_op jit(solution)/shard_map/crossed_move/ppermute | solution.py:336
  129.5 8.0 %collective-permute-done.31 = bf16[2,32,576]{2,1,0:T(8,128)(2,1)S(1)} collective-permute-done((bf16[2,32,576]{2,1,0:T(8,128)(2,1)S(1)}, bf16[2,32,576]{2,1,0:T(8,128)(2,1)S(1)}, u32[]{:S(2)}, u32[]{:S(2)}) %collective-permute-start.31) | collective-permute-done | bytes 73760 | tf_op jit(solution)/shard_map/crossed_move/ppermute | solution.py:336
  138.0 4.5 %route_sums.6 = (f32[1,128,896]{2,1,0:T(8,128)S(1)}, bf16[1,128,896]{2,1,0:T(8,128)(2,1)S(1)}) custom-call(s32[14]{0:T(128)S(1)} %stack.47.refs_0_, bf16[128,1920]{1,0:T(8,128)(2,1)S(1)} %collective-permute-done.13.refs_1_, bf16[128,1920]{1,0:T(8,128)(2,1)S(1)} %collective-permute-done.14.refs_2_, bf16[2,2,2,160,256]{4,3,2,1,0:T(8,128)(2,1)S(1)} %join.6.refs_2_.refs_3_, ...), custom_call_target="tpu_custom_call" | custom-call | flops 2000000000 | bytes 6000001 | tf_op jit(solution)/shard_map/route_sums/pallas_call | solution.py:48
  142.6 2.4 %collective-permute-done.33.refs_1_ = bf16[2,2,160,256]{3,2,1,0:T(8,128)(2,1)S(1)} collective-permute-done((bf16[2,2,160,256]{3,2,1,0:T(8,128)(2,1)S(1)}, bf16[2,2,160,256]{3,2,1,0:T(8,128)(2,1)S(1)}, u32[]{:S(2)}, u32[]{:S(2)}) %collective-permute-start.33) | collective-permute-done | bytes 327712 | tf_op jit(solution)/shard_map/d_own_far/ppermute | solution.py:336
  146.7 4.8 %collective-permute-start.34 = (bf16[128,896]{1,0:T(8,128)(2,1)S(1)}, bf16[128,896]{1,0:T(8,128)(2,1)S(1)}, u32[]{:S(2)}, u32[]{:S(2)}) collective-permute-start(bf16[128,896]{1,0:T(8,128)(2,1)S(1)} %add_parts.23.refs_2_), channel_id=1, source_target_pairs={{0,6},{1,7},{2,4},{3,5},{4,2},{5,3},{6,0},{7,1},{8,14},{9,15},{10,... | collective-permute-start | bytes 688136 | tf_op jit(solution)/shard_map/c_back_move/ppermute | solution.py:30
  152.2 3.8 %collective-permute-done.35.refs_4_ = bf16[2,2,2,160,256]{4,3,2,1,0:T(8,128)(2,1)S(1)} collective-permute-done((bf16[2,2,2,160,256]{4,3,2,1,0:T(8,128)(2,1)S(1)}, bf16[2,2,2,160,256]{4,3,2,1,0:T(8,128)(2,1)S(1)}, u32[]{:S(2)}, u32[]{:S(2)}) %collective-permute-start.35) | collective-permute-done | bytes 655392 | tf_op jit(solution)/shard_map/d_both_near/ppermute | solution.py:336
  156.9 4.5 %route_sums.7 = (f32[1,128,896]{2,1,0:T(8,128)S(1)}, bf16[1,128,896]{2,1,0:T(8,128)(2,1)S(1)}) custom-call(s32[14]{0:T(128)S(1)} %stack.47.refs_0_, bf16[128,1920]{1,0:T(8,128)(2,1)S(1)} %collective-permute-done.15.refs_4_.refs_1_, bf16[128,1920]{1,0:T(8,128)(2,1)S(1)} %collective-permute-done.19.refs_2_, ...), custom_call_target="tpu_custom_call" | custom-call | flops 2000000000 | bytes 6000001 | tf_op jit(solution)/shard_map/route_sums/pallas_call | solution.py:48
  163.0 2.4 %collective-permute-start.38 = (bf16[128,896]{1,0:T(8,128)(2,1)S(1)}, bf16[128,896]{1,0:T(8,128)(2,1)S(1)}, u32[]{:S(2)}, u32[]{:S(2)}) collective-permute-start(bf16[128,896]{1,0:T(8,128)(2,1)S(1)} %add_parts.26.refs_2_), channel_id=1, source_target_pairs={{0,4},{1,5},{2,6},{3,7},{4,0},{5,1},{6,2},{7,3},{8,12},{9,13},{10,... | collective-permute-start | bytes 688136 | tf_op jit(solution)/shard_map/d_back_move/ppermute | solution.py:30
  165.3 11.1 %collective-permute-done.38 = bf16[128,896]{1,0:T(8,128)(2,1)S(1)} collective-permute-done((bf16[128,896]{1,0:T(8,128)(2,1)S(1)}, bf16[128,896]{1,0:T(8,128)(2,1)S(1)}, u32[]{:S(2)}, u32[]{:S(2)}) %collective-permute-start.38) | collective-permute-done | bytes 229408 | tf_op jit(solution)/shard_map/d_back_move/ppermute | solution.py:30
  (100 shorter events, 33.3 us)
Async XLA Ops:
  5.0 14.5 %collective-permute-start.2 = (bf16[128,1920]{1,0:T(8,128)(2,1)S(1)}, bf16[128,1920]{1,0:T(8,128)(2,1)S(1)}, u32[]{:S(2)}, u32[]{:S(2)}) collective-permute-start(bf16[128,1920]{1,0:T(8,128)(2,1)S(1)} %pack_tokens.1.refs_1_), channel_id=1, source_target_pairs={{0,2},{1,3},{2,0},{3,1},{4,6},{5,7},{6,4},{7,5},{8,10},{9,11},{10,... | collective-permute-start | bytes 1474568 | tf_op jit(solution)/shard_map/from_1_move/ppermute | solution.py:30
  14.0 14.2 %collective-permute-start.1 = (bf16[2,2,3,160,256]{4,3,2,1,0:T(8,128)(2,1)S(1)}, bf16[2,2,3,160,256]{4,3,2,1,0:T(8,128)(2,1)S(1)}, u32[]{:S(2)}, u32[]{:S(2)}) collective-permute-start(bf16[2,2,3,160,256]{4,3,2,1,0:T(8,128)(2,1)S(1)} %get-tuple-element.25), channel_id=1, source_target_pairs={{0,8},{1,17},{2,10},{3,19},{4,12},{5,21},{6,14},{7,23},{8,0},{9,25... | collective-permute-start | bytes 2949128 | tf_op jit(solution)/shard_map/a_sums_near/ppermute | solution.py:336
  28.3 12.4 %collective-permute-start.4 = (bf16[2,3,160,256]{3,2,1,0:T(8,128)(2,1)S(1)}, bf16[2,3,160,256]{3,2,1,0:T(8,128)(2,1)S(1)}, u32[]{:S(2)}, u32[]{:S(2)}) collective-permute-start(bf16[2,3,160,256]{3,2,1,0:T(8,128)(2,1)S(1)} %add_parts.14.refs_3_), channel_id=1, source_target_pairs={{0,16},{1,9},{2,18},{3,11},{4,20},{5,13},{6,22},{7,15},{8,24},{9,1... | collective-permute-start | bytes 1474568 | tf_op jit(solution)/shard_map/a_sums_far/ppermute | solution.py:336
  30.0 10.0 %collective-permute-start.7 = (bf16[576,256]{1,0:T(8,128)(2,1)S(1)}, bf16[576,256]{1,0:T(8,128)(2,1)S(1)}, u32[]{:S(2)}, u32[]{:S(2)}) collective-permute-start(bf16[576,256]{1,0:T(8,128)(2,1)S(1)} %bitcast.37), channel_id=1, source_target_pairs={{0,8},{1,17},{2,10},{3,19},{4,12},{5,21},{6,14},{7,23},{8,0},{9,25... | collective-permute-start | bytes 884744 | tf_op jit(solution)/shard_map/keys_near_move/ppermute | solution.py:336
  31.6 15.9 %collective-permute-start.6 = (bf16[576,256]{1,0:T(8,128)(2,1)S(1)}, bf16[576,256]{1,0:T(8,128)(2,1)S(1)}, u32[]{:S(2)}, u32[]{:S(2)}) collective-permute-start(bf16[576,256]{1,0:T(8,128)(2,1)S(1)} %bitcast.38), channel_id=1, source_target_pairs={{0,16},{1,9},{2,18},{3,11},{4,20},{5,13},{6,22},{7,15},{8,24},{9,1... | collective-permute-start | bytes 884744 | tf_op jit(solution)/shard_map/keys_far_move/ppermute | solution.py:336
  40.0 10.3 %collective-permute-start.8 = (bf16[576,256]{1,0:T(8,128)(2,1)S(1)}, bf16[576,256]{1,0:T(8,128)(2,1)S(1)}, u32[]{:S(2)}, u32[]{:S(2)}) collective-permute-start(bf16[576,256]{1,0:T(8,128)(2,1)S(1)} %collective-permute-done.7.refs_6_), channel_id=1, source_target_pairs={{0,16},{1,9},{2,18},{3,11},{4,20},{5,13},{6,22},{7,15},{8,24},{9,1... | collective-permute-start | bytes 884744 | tf_op jit(solution)/shard_map/keys_both_move/ppermute | solution.py:336
  41.0 16.3 %collective-permute-start.5 = (bf16[2,2,160,256]{3,2,1,0:T(8,128)(2,1)S(1)}, bf16[2,2,160,256]{3,2,1,0:T(8,128)(2,1)S(1)}, u32[]{:S(2)}, u32[]{:S(2)}) collective-permute-start(bf16[2,2,160,256]{3,2,1,0:T(8,128)(2,1)S(1)} %hidden_back.4.refs_8_.refs_0_), channel_id=1, source_target_pairs={{0,16},{1,9},{2,18},{3,11},{4,20},{5,13},{6,22},{7,15},{8,24},{9,1... | collective-permute-start | bytes 983048 | tf_op jit(solution)/shard_map/a_own_far/ppermute | solution.py:336
  42.4 24.1 %collective-permute-start.10 = (bf16[2,2,3,160,256]{4,3,2,1,0:T(8,128)(2,1)S(1)}, bf16[2,2,3,160,256]{4,3,2,1,0:T(8,128)(2,1)S(1)}, u32[]{:S(2)}, u32[]{:S(2)}) collective-permute-start(bf16[2,2,3,160,256]{4,3,2,1,0:T(8,128)(2,1)S(1)} %get-tuple-element.32), channel_id=1, source_target_pairs={{0,8},{1,17},{2,10},{3,19},{4,12},{5,21},{6,14},{7,23},{8,0},{9,25... | collective-permute-start | bytes 2949128 | tf_op jit(solution)/shard_map/b_sums_near/ppermute | solution.py:336
  43.9 15.0 %collective-permute-start.13 = (bf16[128,1920]{1,0:T(8,128)(2,1)S(1)}, bf16[128,1920]{1,0:T(8,128)(2,1)S(1)}, u32[]{:S(2)}, u32[]{:S(2)}) collective-permute-start(bf16[128,1920]{1,0:T(8,128)(2,1)S(1)} %pack_tokens.1.refs_1_), channel_id=1, source_target_pairs={{0,6},{1,7},{2,4},{3,5},{4,2},{5,3},{6,0},{7,1},{8,14},{9,15},{10,... | collective-permute-start | bytes 1474568 | tf_op jit(solution)/shard_map/from_3_move/ppermute | solution.py:30
  57.4 10.7 %collective-permute-start.9 = (bf16[2,2,2,160,256]{4,3,2,1,0:T(8,128)(2,1)S(1)}, bf16[2,2,2,160,256]{4,3,2,1,0:T(8,128)(2,1)S(1)}, u32[]{:S(2)}, u32[]{:S(2)}) collective-permute-start(bf16[2,2,2,160,256]{4,3,2,1,0:T(8,128)(2,1)S(1)} %join.4.refs_2_.refs_3_), channel_id=1, source_target_pairs={{0,8},{1,17},{2,10},{3,19},{4,12},{5,21},{6,14},{7,23},{8,0},{9,25... | collective-permute-start | bytes 1966088 | tf_op jit(solution)/shard_map/a_both_near/ppermute | solution.py:336
  58.9 13.8 %collective-permute-start.14 = (bf16[128,1920]{1,0:T(8,128)(2,1)S(1)}, bf16[128,1920]{1,0:T(8,128)(2,1)S(1)}, u32[]{:S(2)}, u32[]{:S(2)}) collective-permute-start(bf16[128,1920]{1,0:T(8,128)(2,1)S(1)} %collective-permute-done.13.refs_1_), channel_id=1, source_target_pairs={{0,1},{1,0},{2,3},{3,2},{4,5},{5,4},{6,7},{7,6},{8,9},{9,8},{10,11... | collective-permute-start | bytes 1474568 | tf_op jit(solution)/shard_map/other_3_move/ppermute | solution.py:30
  58.9 19.5 %collective-permute-start.15 = (bf16[128,1920]{1,0:T(8,128)(2,1)S(1)}, bf16[128,1920]{1,0:T(8,128)(2,1)S(1)}, u32[]{:S(2)}, u32[]{:S(2)}) collective-permute-start(bf16[128,1920]{1,0:T(8,128)(2,1)S(1)} %collective-permute-done.13.refs_1_), channel_id=1, source_target_pairs={{0,2},{1,3},{2,0},{3,1},{4,6},{5,7},{6,4},{7,5},{8,10},{9,11},{10,... | collective-permute-start | bytes 1474568 | tf_op jit(solution)/shard_map/from_2_move/ppermute | solution.py:30
  66.6 11.8 %collective-permute-start.12 = (bf16[2,3,160,256]{3,2,1,0:T(8,128)(2,1)S(1)}, bf16[2,3,160,256]{3,2,1,0:T(8,128)(2,1)S(1)}, u32[]{:S(2)}, u32[]{:S(2)}) collective-permute-start(bf16[2,3,160,256]{3,2,1,0:T(8,128)(2,1)S(1)} %add_parts.15.refs_7_), channel_id=1, source_target_pairs={{0,16},{1,9},{2,18},{3,11},{4,20},{5,13},{6,22},{7,15},{8,24},{9,1... | collective-permute-start | bytes 1474568 | tf_op jit(solution)/shard_map/b_sums_far/ppermute | solution.py:336
  76.9 17.7 %collective-permute-start.20 = (bf16[2,2,3,160,256]{4,3,2,1,0:T(8,128)(2,1)S(1)}, bf16[2,2,3,160,256]{4,3,2,1,0:T(8,128)(2,1)S(1)}, u32[]{:S(2)}, u32[]{:S(2)}) collective-permute-start(bf16[2,2,3,160,256]{4,3,2,1,0:T(8,128)(2,1)S(1)} %get-tuple-element.37), channel_id=1, source_target_pairs={{0,8},{1,17},{2,10},{3,19},{4,12},{5,21},{6,14},{7,23},{8,0},{9,25... | collective-permute-start | bytes 2949128 | tf_op jit(solution)/shard_map/c_sums_near/ppermute | solution.py:336
  78.7 10.7 %collective-permute-start.16 = (bf16[2,2,160,256]{3,2,1,0:T(8,128)(2,1)S(1)}, bf16[2,2,160,256]{3,2,1,0:T(8,128)(2,1)S(1)}, u32[]{:S(2)}, u32[]{:S(2)}) collective-permute-start(bf16[2,2,160,256]{3,2,1,0:T(8,128)(2,1)S(1)} %hidden_back.5.refs_2_.refs_0_), channel_id=1, source_target_pairs={{0,16},{1,9},{2,18},{3,11},{4,20},{5,13},{6,22},{7,15},{8,24},{9,1... | collective-permute-start | bytes 983048 | tf_op jit(solution)/shard_map/b_own_far/ppermute | solution.py:336
  80.4 14.3 %collective-permute-start.19 = (bf16[128,1920]{1,0:T(8,128)(2,1)S(1)}, bf16[128,1920]{1,0:T(8,128)(2,1)S(1)}, u32[]{:S(2)}, u32[]{:S(2)}) collective-permute-start(bf16[128,1920]{1,0:T(8,128)(2,1)S(1)} %collective-permute-done.15.refs_4_.refs_1_), channel_id=1, source_target_pairs={{0,1},{1,0},{2,3},{3,2},{4,5},{5,4},{6,7},{7,6},{8,9},{9,8},{10,11... | collective-permute-start | bytes 1474568 | tf_op jit(solution)/shard_map/other_2_move/ppermute | solution.py:30
  89.5 18.0 %collective-permute-start.18 = (bf16[2,2,2,160,256]{4,3,2,1,0:T(8,128)(2,1)S(1)}, bf16[2,2,2,160,256]{4,3,2,1,0:T(8,128)(2,1)S(1)}, u32[]{:S(2)}, u32[]{:S(2)}) collective-permute-start(bf16[2,2,2,160,256]{4,3,2,1,0:T(8,128)(2,1)S(1)} %join.5.refs_2_.refs_3_), channel_id=1, source_target_pairs={{0,8},{1,17},{2,10},{3,19},{4,12},{5,21},{6,14},{7,23},{8,0},{9,25... | collective-permute-start | bytes 1966088 | tf_op jit(solution)/shard_map/b_both_near/ppermute | solution.py:336
  98.9 20.1 %collective-permute-start.28 = (bf16[2,2,3,160,256]{4,3,2,1,0:T(8,128)(2,1)S(1)}, bf16[2,2,3,160,256]{4,3,2,1,0:T(8,128)(2,1)S(1)}, u32[]{:S(2)}, u32[]{:S(2)}) collective-permute-start(bf16[2,2,3,160,256]{4,3,2,1,0:T(8,128)(2,1)S(1)} %get-tuple-element.41), channel_id=1, source_target_pairs={{0,8},{1,17},{2,10},{3,19},{4,12},{5,21},{6,14},{7,23},{8,0},{9,25... | collective-permute-start | bytes 2949128 | tf_op jit(solution)/shard_map/d_sums_near/ppermute | solution.py:336
  100.4 16.9 %collective-permute-start.22 = (bf16[2,3,160,256]{3,2,1,0:T(8,128)(2,1)S(1)}, bf16[2,3,160,256]{3,2,1,0:T(8,128)(2,1)S(1)}, u32[]{:S(2)}, u32[]{:S(2)}) collective-permute-start(bf16[2,3,160,256]{3,2,1,0:T(8,128)(2,1)S(1)} %add_parts.17.refs_6_), channel_id=1, source_target_pairs={{0,16},{1,9},{2,18},{3,11},{4,20},{5,13},{6,22},{7,15},{8,24},{9,1... | collective-permute-start | bytes 1474568 | tf_op jit(solution)/shard_map/c_sums_far/ppermute | solution.py:336
  102.1 10.0 %collective-permute-start.23 = (bf16[4,32,576]{2,1,0:T(8,128)(2,1)S(1)}, bf16[4,32,576]{2,1,0:T(8,128)(2,1)S(1)}, u32[]{:S(2)}, u32[]{:S(2)}) collective-permute-start(bf16[4,32,576]{2,1,0:T(8,128)(2,1)S(1)} %get-tuple-element.49), channel_id=1, source_target_pairs={{0,2},{1,3},{2,0},{3,1},{4,6},{5,7},{6,4},{7,5},{8,10},{9,11},{10,... | collective-permute-start | bytes 442376 | tf_op jit(solution)/shard_map/latent_terms/ppermute | solution.py:30
  105.1 12.1 %collective-permute-start.24 = (bf16[4,32,576]{2,1,0:T(8,128)(2,1)S(1)}, bf16[4,32,576]{2,1,0:T(8,128)(2,1)S(1)}, u32[]{:S(2)}, u32[]{:S(2)}) collective-permute-start(bf16[4,32,576]{2,1,0:T(8,128)(2,1)S(1)} %get-tuple-element.48), channel_id=1, source_target_pairs={{0,4},{1,5},{2,6},{3,7},{4,0},{5,1},{6,2},{7,3},{8,12},{9,13},{10,... | collective-permute-start | bytes 442376 | tf_op jit(solution)/shard_map/latent_terms/ppermute | solution.py:30
  107.5 9.7 %collective-permute-start.25 = (bf16[4,32,576]{2,1,0:T(8,128)(2,1)S(1)}, bf16[4,32,576]{2,1,0:T(8,128)(2,1)S(1)}, u32[]{:S(2)}, u32[]{:S(2)}) collective-permute-start(bf16[4,32,576]{2,1,0:T(8,128)(2,1)S(1)} %get-tuple-element.47), channel_id=1, source_target_pairs={{0,6},{1,7},{2,4},{3,5},{4,2},{5,3},{6,0},{7,1},{8,14},{9,15},{10,... | collective-permute-start | bytes 442376 | tf_op jit(solution)/shard_map/latent_terms/ppermute | solution.py:30
  117.6 8.4 %collective-permute-start.27 = (bf16[2,2,160,256]{3,2,1,0:T(8,128)(2,1)S(1)}, bf16[2,2,160,256]{3,2,1,0:T(8,128)(2,1)S(1)}, u32[]{:S(2)}, u32[]{:S(2)}) collective-permute-start(bf16[2,2,160,256]{3,2,1,0:T(8,128)(2,1)S(1)} %hidden_back.6.refs_2_.refs_0_), channel_id=1, source_target_pairs={{0,16},{1,9},{2,18},{3,11},{4,20},{5,13},{6,22},{7,15},{8,24},{9,1... | collective-permute-start | bytes 983048 | tf_op jit(solution)/shard_map/c_own_far/ppermute | solution.py:336
  119.2 18.4 %collective-permute-start.30 = (bf16[2,3,160,256]{3,2,1,0:T(8,128)(2,1)S(1)}, bf16[2,3,160,256]{3,2,1,0:T(8,128)(2,1)S(1)}, u32[]{:S(2)}, u32[]{:S(2)}) collective-permute-start(bf16[2,3,160,256]{3,2,1,0:T(8,128)(2,1)S(1)} %add_parts.20.refs_2_), channel_id=1, source_target_pairs={{0,16},{1,9},{2,18},{3,11},{4,20},{5,13},{6,22},{7,15},{8,24},{9,1... | collective-permute-start | bytes 1474568 | tf_op jit(solution)/shard_map/d_sums_far/ppermute | solution.py:336
  126.0 11.9 %collective-permute-start.29 = (bf16[2,2,2,160,256]{4,3,2,1,0:T(8,128)(2,1)S(1)}, bf16[2,2,2,160,256]{4,3,2,1,0:T(8,128)(2,1)S(1)}, u32[]{:S(2)}, u32[]{:S(2)}) collective-permute-start(bf16[2,2,2,160,256]{4,3,2,1,0:T(8,128)(2,1)S(1)} %join.6.refs_2_.refs_3_), channel_id=1, source_target_pairs={{0,8},{1,17},{2,10},{3,19},{4,12},{5,21},{6,14},{7,23},{8,0},{9,25... | collective-permute-start | bytes 1966088 | tf_op jit(solution)/shard_map/c_both_near/ppermute | solution.py:336
  126.1 11.4 %collective-permute-start.31 = (bf16[2,32,576]{2,1,0:T(8,128)(2,1)S(1)}, bf16[2,32,576]{2,1,0:T(8,128)(2,1)S(1)}, u32[]{:S(2)}, u32[]{:S(2)}) collective-permute-start(bf16[2,32,576]{2,1,0:T(8,128)(2,1)S(1)} %get-tuple-element.50), channel_id=1, source_target_pairs={{0,8},{1,17},{2,10},{3,19},{4,12},{5,21},{6,14},{7,23},{8,0},{9,25... | collective-permute-start | bytes 221192 | tf_op jit(solution)/shard_map/crossed_move/ppermute | solution.py:336
  128.4 14.1 %collective-permute-start.11 = (bf16[1,128,896]{2,1,0:T(8,128)(2,1)S(1)}, bf16[1,128,896]{2,1,0:T(8,128)(2,1)S(1)}, u32[]{:S(2)}, u32[]{:S(2)}) collective-permute-start(bf16[1,128,896]{2,1,0:T(8,128)(2,1)S(1)} %get-tuple-element.34.refs_6_), channel_id=1, source_target_pairs={{0,1},{1,0},{2,3},{3,2},{4,5},{5,4},{6,7},{7,6},{8,9},{9,8},{10,11... | collective-permute-start | bytes 688136 | tf_op jit(solution)/shard_map/a_other_move/ppermute | solution.py:30
  128.4 14.1 %collective-permute-start.26 = (bf16[128,896]{1,0:T(8,128)(2,1)S(1)}, bf16[128,896]{1,0:T(8,128)(2,1)S(1)}, u32[]{:S(2)}, u32[]{:S(2)}) collective-permute-start(bf16[128,896]{1,0:T(8,128)(2,1)S(1)} %add_parts.19.refs_2_), channel_id=1, source_target_pairs={{0,2},{1,3},{2,0},{3,1},{4,6},{5,7},{6,4},{7,5},{8,10},{9,11},{10,... | collective-permute-start | bytes 688136 | tf_op jit(solution)/shard_map/b_back_move/ppermute | solution.py:30
  137.9 7.1 %collective-permute-start.33 = (bf16[2,2,160,256]{3,2,1,0:T(8,128)(2,1)S(1)}, bf16[2,2,160,256]{3,2,1,0:T(8,128)(2,1)S(1)}, u32[]{:S(2)}, u32[]{:S(2)}) collective-permute-start(bf16[2,2,160,256]{3,2,1,0:T(8,128)(2,1)S(1)} %hidden_back.7.refs_7_.refs_0_), channel_id=1, source_target_pairs={{0,16},{1,9},{2,18},{3,11},{4,20},{5,13},{6,22},{7,15},{8,24},{9,1... | collective-permute-start | bytes 983048 | tf_op jit(solution)/shard_map/d_own_far/ppermute | solution.py:336
  145.1 10.9 %collective-permute-start.35 = (bf16[2,2,2,160,256]{4,3,2,1,0:T(8,128)(2,1)S(1)}, bf16[2,2,2,160,256]{4,3,2,1,0:T(8,128)(2,1)S(1)}, u32[]{:S(2)}, u32[]{:S(2)}) collective-permute-start(bf16[2,2,2,160,256]{4,3,2,1,0:T(8,128)(2,1)S(1)} %join.7.refs_2_.refs_3_), channel_id=1, source_target_pairs={{0,8},{1,17},{2,10},{3,19},{4,12},{5,21},{6,14},{7,23},{8,0},{9,25... | collective-permute-start | bytes 1966088 | tf_op jit(solution)/shard_map/d_both_near/ppermute | solution.py:336
  146.7 14.7 %collective-permute-start.34 = (bf16[128,896]{1,0:T(8,128)(2,1)S(1)}, bf16[128,896]{1,0:T(8,128)(2,1)S(1)}, u32[]{:S(2)}, u32[]{:S(2)}) collective-permute-start(bf16[128,896]{1,0:T(8,128)(2,1)S(1)} %add_parts.23.refs_2_), channel_id=1, source_target_pairs={{0,6},{1,7},{2,4},{3,5},{4,2},{5,3},{6,0},{7,1},{8,14},{9,15},{10,... | collective-permute-start | bytes 688136 | tf_op jit(solution)/shard_map/c_back_move/ppermute | solution.py:30
  163.0 13.5 %collective-permute-start.38 = (bf16[128,896]{1,0:T(8,128)(2,1)S(1)}, bf16[128,896]{1,0:T(8,128)(2,1)S(1)}, u32[]{:S(2)}, u32[]{:S(2)}) collective-permute-start(bf16[128,896]{1,0:T(8,128)(2,1)S(1)} %add_parts.26.refs_2_), channel_id=1, source_target_pairs={{0,4},{1,5},{2,6},{3,7},{4,0},{5,1},{6,2},{7,3},{8,12},{9,13},{10,... | collective-permute-start | bytes 688136 | tf_op jit(solution)/shard_map/d_back_move/ppermute | solution.py:30
  (16 other events, 89.4 us)

commit v4 on v3

--- a/solution.py
+++ b/solution.py
@@ -510,7 +510,7 @@
         (start_total, 2),
         (functools.partial(c.multiply, [from_3, other_3]), 2),
         (b.turn, 2, from_2),
-        (latent_cores, 2),
+        (latent_cores, 2, keys_both),
         (b.forward, 2),
         (c.add, 2),
         (functools.partial(d.multiply, [from_2, other_2]), 2),

time: 177 us -> 177 us (level)
  no operation moved by 1% of the time
where the time goes in v4:
time: 177 us
  waiting for transfers between devices  74.8 us (42%)
  starting transfers between devices  51 us (29%)
  Pallas kernels  46.1 us (26%)
  local copies, waits for them, and re-layouts  4.3 us (2%)
    ppermute x21, waiting for transfers between devices, plane_shift(): return lax.ppermute(value, ('ctx', 'exp'), pairs)  50.9 us
    pallas_call x32, Pallas kernels, call(): pl.pallas_call(body, out_shape=out_shape, grid=grid, in_specs=list(in_spe...  46.1 us
    ppermute x18, starting transfers between devices, shift(): return lax.ppermute(value, 'exp', pairs)  28.3 us
    ppermute x18, waiting for transfers between devices, shift(): return lax.ppermute(value, 'exp', pairs)  23.9 us
    ppermute x21, starting transfers between devices, plane_shift(): return lax.ppermute(value, ('ctx', 'exp'), pairs)  22.7 us
    unnamed x18, local copies, waits for them, and re-layouts  4.14 us
  transfers between devices with their start and end apart: 39, of which 19 were waited for; matrix products, arithmetic and copies ran while one was open for 0% of the time, Pallas kernels for 25%

profile of v4, /device:TPU:0, one launch (start us, length us, event | category | flops | bytes accessed | tf_op | source)
XLA Modules:
  0.0 177.2 jit_solution(10083611843880732173)
XLA Ops:
  5.0 2.6 %collective-permute-start.2 = (bf16[128,1920]{1,0:T(8,128)(2,1)S(1)}, bf16[128,1920]{1,0:T(8,128)(2,1)S(1)}, u32[]{:S(2)}, u32[]{:S(2)}) collective-permute-start(bf16[128,1920]{1,0:T(8,128)(2,1)S(1)} %pack_tokens.1.refs_1_), channel_id=1, source_target_pairs={{0,2},{1,3},{2,0},{3,1},{4,6},{5,7},{6,4},{7,5},{8,10},{9,11},{10,... | collective-permute-start | bytes 1474568 | tf_op jit(solution)/shard_map/from_1_move/ppermute | solution.py:30
  7.8 6.3 %first_products.1 = (bf16[2,2,3,160,256]{4,3,2,1,0:T(8,128)(2,1)S(1)}, bf16[2,2,3,160,256]{4,3,2,1,0:T(8,128)(2,1)S(1)}, bf16[2,896,1024]{2,1,0:T(8,128)(2,1)S(1...) custom-call(s32[14]{0:T(128)S(1)} %stack.47.refs_0_, bf16[128,1920]{1,0:T(8,128)(2,1)S(1)} %pack_tokens.1.refs_1_, ...), custom_call_target="tpu_custom_call" | custom-call | flops 10000000000 | bytes 30000000 | tf_op jit(solution)/shard_map/first_products/pallas_call | solution.py:48
  15.7 3.8 %collective-permute-done.2.refs_1_ = bf16[128,1920]{1,0:T(8,128)(2,1)S(1)} collective-permute-done((bf16[128,1920]{1,0:T(8,128)(2,1)S(1)}, bf16[128,1920]{1,0:T(8,128)(2,1)S(1)}, u32[]{:S(2)}, u32[]{:S(2)}) %collective-permute-start.2) | collective-permute-done | bytes 491552 | tf_op jit(solution)/shard_map/from_1_move/ppermute | solution.py:30
  19.5 1.9 %collective-permute-done.3.refs_2_ = bf16[128,1920]{1,0:T(8,128)(2,1)S(1)} collective-permute-done((bf16[128,1920]{1,0:T(8,128)(2,1)S(1)}, bf16[128,1920]{1,0:T(8,128)(2,1)S(1)}, u32[]{:S(2)}, u32[]{:S(2)}) %collective-permute-start.3) | collective-permute-done | bytes 491552 | tf_op jit(solution)/shard_map/other_1_move/ppermute | solution.py:30
  21.3 4.2 %products.3 = (bf16[2,2,3,160,256]{4,3,2,1,0:T(8,128)(2,1)S(1)}, bf16[2,2,3,160,256]{4,3,2,1,0:T(8,128)(2,1)S(1)}) custom-call(s32[14]{0:T(128)S(1)} %stack.47.refs_0_, bf16[128,1920]{1,0:T(8,128)(2,1)S(1)} %collective-permute-done.2.refs_1_, bf16[128,1920]{1,0:T(8,128)(2,1)S(1)} %collective-permute-done.3.refs_2_, ...), custom_call_target="tpu_custom_call" | custom-call | flops 2000000000 | bytes 6000001 | tf_op jit(solution)/shard_map/products/pallas_call | solution.py:48
  25.5 2.6 %collective-permute-done.1.refs_0_ = bf16[2,2,3,160,256]{4,3,2,1,0:T(8,128)(2,1)S(1)} collective-permute-done((bf16[2,2,3,160,256]{4,3,2,1,0:T(8,128)(2,1)S(1)}, bf16[2,2,3,160,256]{4,3,2,1,0:T(8,128)(2,1)S(1)}, u32[]{:S(2)}, u32[]{:S(2)}) %collective-permute-start.1) | collective-permute-done | bytes 983072 | tf_op jit(solution)/shard_map/a_sums_near/ppermute | solution.py:336
  32.3 7.8 %collective-permute-done.7.refs_6_ = bf16[576,256]{1,0:T(8,128)(2,1)S(1)} collective-permute-done((bf16[576,256]{1,0:T(8,128)(2,1)S(1)}, bf16[576,256]{1,0:T(8,128)(2,1)S(1)}, u32[]{:S(2)}, u32[]{:S(2)}) %collective-permute-start.7) | collective-permute-done | bytes 294944 | tf_op jit(solution)/shard_map/keys_near_move/ppermute | solution.py:336
  43.9 3.6 %collective-permute-start.13 = (bf16[128,1920]{1,0:T(8,128)(2,1)S(1)}, bf16[128,1920]{1,0:T(8,128)(2,1)S(1)}, u32[]{:S(2)}, u32[]{:S(2)}) collective-permute-start(bf16[128,1920]{1,0:T(8,128)(2,1)S(1)} %pack_tokens.1.refs_1_), channel_id=1, source_target_pairs={{0,6},{1,7},{2,4},{3,5},{4,2},{5,3},{6,0},{7,1},{8,14},{9,15},{10,... | collective-permute-start | bytes 1474568 | tf_op jit(solution)/shard_map/from_3_move/ppermute | solution.py:30
  47.5 2.8 %collective-permute-done.8.refs_7_.refs_3_ = bf16[576,256]{1,0:T(8,128)(2,1)S(1)} collective-permute-done((bf16[576,256]{1,0:T(8,128)(2,1)S(1)}, bf16[576,256]{1,0:T(8,128)(2,1)S(1)}, u32[]{:S(2)}, u32[]{:S(2)}) %collective-permute-start.8) | collective-permute-done | bytes 294944 | tf_op jit(solution)/shard_map/keys_both_move/ppermute | solution.py:336
  50.3 4.8 %attention.1 = (bf16[128,1152]{1,0:T(8,128)(2,1)}, bf16[4,4,32,576]{3,2,1,0:T(8,128)(2,1)S(1)}, bf16[4,4,32,576]{3,2,1,0:T(8,128)(2,1)S(1)}) custom-call(s32[14]{0:T(128)S(1)} %stack.47.refs_0_, bf16[128,1152]{1,0:T(8,128)(2,1)S(1)} %copy-done.1, bf16[128,1024]{1,0:T(8,128)(2,1)S(1)} %copy-done.3, s32[1,128]{1,0:T(1,128)S(1)} %bitcast.50, ...), custom_call_target="tpu_custom_call" | custom-call | flops 2000000000 | bytes 6000001 | tf_op jit(solution)/shard_map/attention/pallas_call | solution.py:48
  55.1 2.3 %collective-permute-done.5.refs_1_ = bf16[2,2,160,256]{3,2,1,0:T(8,128)(2,1)S(1)} collective-permute-done((bf16[2,2,160,256]{3,2,1,0:T(8,128)(2,1)S(1)}, bf16[2,2,160,256]{3,2,1,0:T(8,128)(2,1)S(1)}, u32[]{:S(2)}, u32[]{:S(2)}) %collective-permute-start.5) | collective-permute-done | bytes 327712 | tf_op jit(solution)/shard_map/a_own_far/ppermute | solution.py:336
  58.9 7.6 %collective-permute-start.15 = (bf16[128,1920]{1,0:T(8,128)(2,1)S(1)}, bf16[128,1920]{1,0:T(8,128)(2,1)S(1)}, u32[]{:S(2)}, u32[]{:S(2)}) collective-permute-start(bf16[128,1920]{1,0:T(8,128)(2,1)S(1)} %collective-permute-done.13.refs_1_), channel_id=1, source_target_pairs={{0,2},{1,3},{2,0},{3,1},{4,6},{5,7},{6,4},{7,5},{8,10},{9,11},{10,... | collective-permute-start | bytes 1474568 | tf_op jit(solution)/shard_map/from_2_move/ppermute | solution.py:30
  68.0 4.7 %route_sums.4 = (f32[1,128,896]{2,1,0:T(8,128)S(1)}, bf16[1,128,896]{2,1,0:T(8,128)(2,1)S(1)}) custom-call(s32[14]{0:T(128)S(1)} %stack.47.refs_0_, bf16[128,1920]{1,0:T(8,128)(2,1)S(1)} %pack_tokens.1.refs_1_, bf16[128,1920]{1,0:T(8,128)(2,1)S(1)} %collective-permute-done.refs_2_, bf16[2,2,2,160,256]{4,3,2,1,0:T(8,128)(2,1)S(1)} %join.4.refs_2_.refs_3_, ...), custom_call_target="tpu_custom_call" | custom-call | flops 2000000000 | bytes 6000001 | tf_op jit(solution)/shard_map/route_sums/pallas_call | solution.py:48
  72.7 4.2 %products.4 = (bf16[2,2,3,160,256]{4,3,2,1,0:T(8,128)(2,1)S(1)}, bf16[2,2,3,160,256]{4,3,2,1,0:T(8,128)(2,1)S(1)}) custom-call(s32[14]{0:T(128)S(1)} %stack.47.refs_0_, bf16[128,1920]{1,0:T(8,128)(2,1)S(1)} %collective-permute-done.13.refs_1_, bf16[128,1920]{1,0:T(8,128)(2,1)S(1)} %collective-permute-done.14.refs_2_, ...), custom_call_target="tpu_custom_call" | custom-call | flops 2000000000 | bytes 6000001 | tf_op jit(solution)/shard_map/products/pallas_call | solution.py:48
  78.7 1.7 collective-permute-start.16
  80.7 8.7 %collective-permute-done.16.refs_1_ = bf16[2,2,160,256]{3,2,1,0:T(8,128)(2,1)S(1)} collective-permute-done((bf16[2,2,160,256]{3,2,1,0:T(8,128)(2,1)S(1)}, bf16[2,2,160,256]{3,2,1,0:T(8,128)(2,1)S(1)}, u32[]{:S(2)}, u32[]{:S(2)}) %collective-permute-start.16) | collective-permute-done | bytes 327712 | tf_op jit(solution)/shard_map/b_own_far/ppermute | solution.py:336
  90.1 4.4 %collective-permute-done.20.refs_0_ = bf16[2,2,3,160,256]{4,3,2,1,0:T(8,128)(2,1)S(1)} collective-permute-done((bf16[2,2,3,160,256]{4,3,2,1,0:T(8,128)(2,1)S(1)}, bf16[2,2,3,160,256]{4,3,2,1,0:T(8,128)(2,1)S(1)}, u32[]{:S(2)}, u32[]{:S(2)}) %collective-permute-start.20) | collective-permute-done | bytes 983072 | tf_op jit(solution)/shard_map/c_sums_near/ppermute | solution.py:336
  94.7 4.2 %products.5 = (bf16[2,2,3,160,256]{4,3,2,1,0:T(8,128)(2,1)S(1)}, bf16[2,2,3,160,256]{4,3,2,1,0:T(8,128)(2,1)S(1)}) custom-call(s32[14]{0:T(128)S(1)} %stack.47.refs_0_, bf16[128,1920]{1,0:T(8,128)(2,1)S(1)} %collective-permute-done.15.refs_4_.refs_1_, bf16[128,1920]{1,0:T(8,128)(2,1)S(1)} %collective-permute-done.19.refs_2_, ...), custom_call_target="tpu_custom_call" | custom-call | flops 2000000000 | bytes 6000001 | tf_op jit(solution)/shard_map/products/pallas_call | solution.py:48
  102.1 3.0 %collective-permute-start.23 = (bf16[4,32,576]{2,1,0:T(8,128)(2,1)S(1)}, bf16[4,32,576]{2,1,0:T(8,128)(2,1)S(1)}, u32[]{:S(2)}, u32[]{:S(2)}) collective-permute-start(bf16[4,32,576]{2,1,0:T(8,128)(2,1)S(1)} %get-tuple-element.49), channel_id=1, source_target_pairs={{0,2},{1,3},{2,0},{3,1},{4,6},{5,7},{6,4},{7,5},{8,10},{9,11},{10,... | collective-permute-start | bytes 442376 | tf_op jit(solution)/shard_map/latent_terms/ppermute | solution.py:30
  105.1 2.4 %collective-permute-start.24 = (bf16[4,32,576]{2,1,0:T(8,128)(2,1)S(1)}, bf16[4,32,576]{2,1,0:T(8,128)(2,1)S(1)}, u32[]{:S(2)}, u32[]{:S(2)}) collective-permute-start(bf16[4,32,576]{2,1,0:T(8,128)(2,1)S(1)} %get-tuple-element.48), channel_id=1, source_target_pairs={{0,4},{1,5},{2,6},{3,7},{4,0},{5,1},{6,2},{7,3},{8,12},{9,13},{10,... | collective-permute-start | bytes 442376 | tf_op jit(solution)/shard_map/latent_terms/ppermute | solution.py:30
  107.5 4.5 %route_sums.5 = (f32[1,128,896]{2,1,0:T(8,128)S(1)}, bf16[1,128,896]{2,1,0:T(8,128)(2,1)S(1)}) custom-call(s32[14]{0:T(128)S(1)} %stack.47.refs_0_, bf16[128,1920]{1,0:T(8,128)(2,1)S(1)} %collective-permute-done.2.refs_1_, bf16[128,1920]{1,0:T(8,128)(2,1)S(1)} %collective-permute-done.3.refs_2_, bf16[2,2,2,160,256]{4,3,2,1,0:T(8,128)(2,1)S(1)} %join.5.refs_2_.refs_3_, ...), custom_call_target="tpu_custom_call" | custom-call | flops 2000000000 | bytes 6000001 | tf_op jit(solution)/shard_map/route_sums/pallas_call | solution.py:48
  112.1 5.1 %collective-permute-done.24 = bf16[4,32,576]{2,1,0:T(8,128)(2,1)S(1)} collective-permute-done((bf16[4,32,576]{2,1,0:T(8,128)(2,1)S(1)}, bf16[4,32,576]{2,1,0:T(8,128)(2,1)S(1)}, u32[]{:S(2)}, u32[]{:S(2)}) %collective-permute-start.24) | collective-permute-done | bytes 147488 | tf_op jit(solution)/shard_map/latent_terms/ppermute | solution.py:30
  120.0 6.0 %collective-permute-done.27.refs_1_ = bf16[2,2,160,256]{3,2,1,0:T(8,128)(2,1)S(1)} collective-permute-done((bf16[2,2,160,256]{3,2,1,0:T(8,128)(2,1)S(1)}, bf16[2,2,160,256]{3,2,1,0:T(8,128)(2,1)S(1)}, u32[]{:S(2)}, u32[]{:S(2)}) %collective-permute-start.27) | collective-permute-done | bytes 327712 | tf_op jit(solution)/shard_map/c_own_far/ppermute | solution.py:336
  126.1 2.3 %collective-permute-start.31 = (bf16[2,32,576]{2,1,0:T(8,128)(2,1)S(1)}, bf16[2,32,576]{2,1,0:T(8,128)(2,1)S(1)}, u32[]{:S(2)}, u32[]{:S(2)}) collective-permute-start(bf16[2,32,576]{2,1,0:T(8,128)(2,1)S(1)} %get-tuple-element.50), channel_id=1, source_target_pairs={{0,8},{1,17},{2,10},{3,19},{4,12},{5,21},{6,14},{7,23},{8,0},{9,25... | collective-permute-start | bytes 221192 | tf_op jit(solution)/shard_map/crossed_move/ppermute | solution.py:336
  129.5 8.0 %collective-permute-done.31 = bf16[2,32,576]{2,1,0:T(8,128)(2,1)S(1)} collective-permute-done((bf16[2,32,576]{2,1,0:T(8,128)(2,1)S(1)}, bf16[2,32,576]{2,1,0:T(8,128)(2,1)S(1)}, u32[]{:S(2)}, u32[]{:S(2)}) %collective-permute-start.31) | collective-permute-done | bytes 73760 | tf_op jit(solution)/shard_map/crossed_move/ppermute | solution.py:336
  138.0 4.5 %route_sums.6 = (f32[1,128,896]{2,1,0:T(8,128)S(1)}, bf16[1,128,896]{2,1,0:T(8,128)(2,1)S(1)}) custom-call(s32[14]{0:T(128)S(1)} %stack.47.refs_0_, bf16[128,1920]{1,0:T(8,128)(2,1)S(1)} %collective-permute-done.13.refs_1_, bf16[128,1920]{1,0:T(8,128)(2,1)S(1)} %collective-permute-done.14.refs_2_, bf16[2,2,2,160,256]{4,3,2,1,0:T(8,128)(2,1)S(1)} %join.6.refs_2_.refs_3_, ...), custom_call_target="tpu_custom_call" | custom-call | flops 2000000000 | bytes 6000001 | tf_op jit(solution)/shard_map/route_sums/pallas_call | solution.py:48
  142.6 2.4 %collective-permute-done.33.refs_1_ = bf16[2,2,160,256]{3,2,1,0:T(8,128)(2,1)S(1)} collective-permute-done((bf16[2,2,160,256]{3,2,1,0:T(8,128)(2,1)S(1)}, bf16[2,2,160,256]{3,2,1,0:T(8,128)(2,1)S(1)}, u32[]{:S(2)}, u32[]{:S(2)}) %collective-permute-start.33) | collective-permute-done | bytes 327712 | tf_op jit(solution)/shard_map/d_own_far/ppermute | solution.py:336
  146.7 4.8 %collective-permute-start.34 = (bf16[128,896]{1,0:T(8,128)(2,1)S(1)}, bf16[128,896]{1,0:T(8,128)(2,1)S(1)}, u32[]{:S(2)}, u32[]{:S(2)}) collective-permute-start(bf16[128,896]{1,0:T(8,128)(2,1)S(1)} %add_parts.23.refs_2_), channel_id=1, source_target_pairs={{0,6},{1,7},{2,4},{3,5},{4,2},{5,3},{6,0},{7,1},{8,14},{9,15},{10,... | collective-permute-start | bytes 688136 | tf_op jit(solution)/shard_map/c_back_move/ppermute | solution.py:30
  152.2 3.8 %collective-permute-done.35.refs_4_ = bf16[2,2,2,160,256]{4,3,2,1,0:T(8,128)(2,1)S(1)} collective-permute-done((bf16[2,2,2,160,256]{4,3,2,1,0:T(8,128)(2,1)S(1)}, bf16[2,2,2,160,256]{4,3,2,1,0:T(8,128)(2,1)S(1)}, u32[]{:S(2)}, u32[]{:S(2)}) %collective-permute-start.35) | collective-permute-done | bytes 655392 | tf_op jit(solution)/shard_map/d_both_near/ppermute | solution.py:336
  156.9 4.5 %route_sums.7 = (f32[1,128,896]{2,1,0:T(8,128)S(1)}, bf16[1,128,896]{2,1,0:T(8,128)(2,1)S(1)}) custom-call(s32[14]{0:T(128)S(1)} %stack.47.refs_0_, bf16[128,1920]{1,0:T(8,128)(2,1)S(1)} %collective-permute-done.15.refs_4_.refs_1_, bf16[128,1920]{1,0:T(8,128)(2,1)S(1)} %collective-permute-done.19.refs_2_, ...), custom_call_target="tpu_custom_call" | custom-call | flops 2000000000 | bytes 6000001 | tf_op jit(solution)/shard_map/route_sums/pallas_call | solution.py:48
  163.0 2.4 %collective-permute-start.38 = (bf16[128,896]{1,0:T(8,128)(2,1)S(1)}, bf16[128,896]{1,0:T(8,128)(2,1)S(1)}, u32[]{:S(2)}, u32[]{:S(2)}) collective-permute-start(bf16[128,896]{1,0:T(8,128)(2,1)S(1)} %add_parts.26.refs_2_), channel_id=1, source_target_pairs={{0,4},{1,5},{2,6},{3,7},{4,0},{5,1},{6,2},{7,3},{8,12},{9,13},{10,... | collective-permute-start | bytes 688136 | tf_op jit(solution)/shard_map/d_back_move/ppermute | solution.py:30
  165.3 11.1 %collective-permute-done.38 = bf16[128,896]{1,0:T(8,128)(2,1)S(1)} collective-permute-done((bf16[128,896]{1,0:T(8,128)(2,1)S(1)}, bf16[128,896]{1,0:T(8,128)(2,1)S(1)}, u32[]{:S(2)}, u32[]{:S(2)}) %collective-permute-start.38) | collective-permute-done | bytes 229408 | tf_op jit(solution)/shard_map/d_back_move/ppermute | solution.py:30
  (100 shorter events, 33.3 us)
Async XLA Ops:
  5.0 14.5 %collective-permute-start.2 = (bf16[128,1920]{1,0:T(8,128)(2,1)S(1)}, bf16[128,1920]{1,0:T(8,128)(2,1)S(1)}, u32[]{:S(2)}, u32[]{:S(2)}) collective-permute-start(bf16[128,1920]{1,0:T(8,128)(2,1)S(1)} %pack_tokens.1.refs_1_), channel_id=1, source_target_pairs={{0,2},{1,3},{2,0},{3,1},{4,6},{5,7},{6,4},{7,5},{8,10},{9,11},{10,... | collective-permute-start | bytes 1474568 | tf_op jit(solution)/shard_map/from_1_move/ppermute | solution.py:30
  14.0 14.2 %collective-permute-start.1 = (bf16[2,2,3,160,256]{4,3,2,1,0:T(8,128)(2,1)S(1)}, bf16[2,2,3,160,256]{4,3,2,1,0:T(8,128)(2,1)S(1)}, u32[]{:S(2)}, u32[]{:S(2)}) collective-permute-start(bf16[2,2,3,160,256]{4,3,2,1,0:T(8,128)(2,1)S(1)} %get-tuple-element.25), channel_id=1, source_target_pairs={{0,8},{1,17},{2,10},{3,19},{4,12},{5,21},{6,14},{7,23},{8,0},{9,25... | collective-permute-start | bytes 2949128 | tf_op jit(solution)/shard_map/a_sums_near/ppermute | solution.py:336
  28.3 12.4 %collective-permute-start.4 = (bf16[2,3,160,256]{3,2,1,0:T(8,128)(2,1)S(1)}, bf16[2,3,160,256]{3,2,1,0:T(8,128)(2,1)S(1)}, u32[]{:S(2)}, u32[]{:S(2)}) collective-permute-start(bf16[2,3,160,256]{3,2,1,0:T(8,128)(2,1)S(1)} %add_parts.14.refs_3_), channel_id=1, source_target_pairs={{0,16},{1,9},{2,18},{3,11},{4,20},{5,13},{6,22},{7,15},{8,24},{9,1... | collective-permute-start | bytes 1474568 | tf_op jit(solution)/shard_map/a_sums_far/ppermute | solution.py:336
  30.0 10.0 %collective-permute-start.7 = (bf16[576,256]{1,0:T(8,128)(2,1)S(1)}, bf16[576,256]{1,0:T(8,128)(2,1)S(1)}, u32[]{:S(2)}, u32[]{:S(2)}) collective-permute-start(bf16[576,256]{1,0:T(8,128)(2,1)S(1)} %bitcast.37), channel_id=1, source_target_pairs={{0,8},{1,17},{2,10},{3,19},{4,12},{5,21},{6,14},{7,23},{8,0},{9,25... | collective-permute-start | bytes 884744 | tf_op jit(solution)/shard_map/keys_near_move/ppermute | solution.py:336
  31.6 15.9 %collective-permute-start.6 = (bf16[576,256]{1,0:T(8,128)(2,1)S(1)}, bf16[576,256]{1,0:T(8,128)(2,1)S(1)}, u32[]{:S(2)}, u32[]{:S(2)}) collective-permute-start(bf16[576,256]{1,0:T(8,128)(2,1)S(1)} %bitcast.38), channel_id=1, source_target_pairs={{0,16},{1,9},{2,18},{3,11},{4,20},{5,13},{6,22},{7,15},{8,24},{9,1... | collective-permute-start | bytes 884744 | tf_op jit(solution)/shard_map/keys_far_move/ppermute | solution.py:336
  40.0 10.3 %collective-permute-start.8 = (bf16[576,256]{1,0:T(8,128)(2,1)S(1)}, bf16[576,256]{1,0:T(8,128)(2,1)S(1)}, u32[]{:S(2)}, u32[]{:S(2)}) collective-permute-start(bf16[576,256]{1,0:T(8,128)(2,1)S(1)} %collective-permute-done.7.refs_6_), channel_id=1, source_target_pairs={{0,16},{1,9},{2,18},{3,11},{4,20},{5,13},{6,22},{7,15},{8,24},{9,1... | collective-permute-start | bytes 884744 | tf_op jit(solution)/shard_map/keys_both_move/ppermute | solution.py:336
  41.0 16.3 %collective-permute-start.5 = (bf16[2,2,160,256]{3,2,1,0:T(8,128)(2,1)S(1)}, bf16[2,2,160,256]{3,2,1,0:T(8,128)(2,1)S(1)}, u32[]{:S(2)}, u32[]{:S(2)}) collective-permute-start(bf16[2,2,160,256]{3,2,1,0:T(8,128)(2,1)S(1)} %hidden_back.4.refs_8_.refs_0_), channel_id=1, source_target_pairs={{0,16},{1,9},{2,18},{3,11},{4,20},{5,13},{6,22},{7,15},{8,24},{9,1... | collective-permute-start | bytes 983048 | tf_op jit(solution)/shard_map/a_own_far/ppermute | solution.py:336
  42.4 24.1 %collective-permute-start.10 = (bf16[2,2,3,160,256]{4,3,2,1,0:T(8,128)(2,1)S(1)}, bf16[2,2,3,160,256]{4,3,2,1,0:T(8,128)(2,1)S(1)}, u32[]{:S(2)}, u32[]{:S(2)}) collective-permute-start(bf16[2,2,3,160,256]{4,3,2,1,0:T(8,128)(2,1)S(1)} %get-tuple-element.32), channel_id=1, source_target_pairs={{0,8},{1,17},{2,10},{3,19},{4,12},{5,21},{6,14},{7,23},{8,0},{9,25... | collective-permute-start | bytes 2949128 | tf_op jit(solution)/shard_map/b_sums_near/ppermute | solution.py:336
  43.9 15.0 %collective-permute-start.13 = (bf16[128,1920]{1,0:T(8,128)(2,1)S(1)}, bf16[128,1920]{1,0:T(8,128)(2,1)S(1)}, u32[]{:S(2)}, u32[]{:S(2)}) collective-permute-start(bf16[128,1920]{1,0:T(8,128)(2,1)S(1)} %pack_tokens.1.refs_1_), channel_id=1, source_target_pairs={{0,6},{1,7},{2,4},{3,5},{4,2},{5,3},{6,0},{7,1},{8,14},{9,15},{10,... | collective-permute-start | bytes 1474568 | tf_op jit(solution)/shard_map/from_3_move/ppermute | solution.py:30
  57.4 10.7 %collective-permute-start.9 = (bf16[2,2,2,160,256]{4,3,2,1,0:T(8,128)(2,1)S(1)}, bf16[2,2,2,160,256]{4,3,2,1,0:T(8,128)(2,1)S(1)}, u32[]{:S(2)}, u32[]{:S(2)}) collective-permute-start(bf16[2,2,2,160,256]{4,3,2,1,0:T(8,128)(2,1)S(1)} %join.4.refs_2_.refs_3_), channel_id=1, source_target_pairs={{0,8},{1,17},{2,10},{3,19},{4,12},{5,21},{6,14},{7,23},{8,0},{9,25... | collective-permute-start | bytes 1966088 | tf_op jit(solution)/shard_map/a_both_near/ppermute | solution.py:336
  58.9 13.8 %collective-permute-start.14 = (bf16[128,1920]{1,0:T(8,128)(2,1)S(1)}, bf16[128,1920]{1,0:T(8,128)(2,1)S(1)}, u32[]{:S(2)}, u32[]{:S(2)}) collective-permute-start(bf16[128,1920]{1,0:T(8,128)(2,1)S(1)} %collective-permute-done.13.refs_1_), channel_id=1, source_target_pairs={{0,1},{1,0},{2,3},{3,2},{4,5},{5,4},{6,7},{7,6},{8,9},{9,8},{10,11... | collective-permute-start | bytes 1474568 | tf_op jit(solution)/shard_map/other_3_move/ppermute | solution.py:30
  58.9 19.5 %collective-permute-start.15 = (bf16[128,1920]{1,0:T(8,128)(2,1)S(1)}, bf16[128,1920]{1,0:T(8,128)(2,1)S(1)}, u32[]{:S(2)}, u32[]{:S(2)}) collective-permute-start(bf16[128,1920]{1,0:T(8,128)(2,1)S(1)} %collective-permute-done.13.refs_1_), channel_id=1, source_target_pairs={{0,2},{1,3},{2,0},{3,1},{4,6},{5,7},{6,4},{7,5},{8,10},{9,11},{10,... | collective-permute-start | bytes 1474568 | tf_op jit(solution)/shard_map/from_2_move/ppermute | solution.py:30
  66.6 11.8 %collective-permute-start.12 = (bf16[2,3,160,256]{3,2,1,0:T(8,128)(2,1)S(1)}, bf16[2,3,160,256]{3,2,1,0:T(8,128)(2,1)S(1)}, u32[]{:S(2)}, u32[]{:S(2)}) collective-permute-start(bf16[2,3,160,256]{3,2,1,0:T(8,128)(2,1)S(1)} %add_parts.15.refs_7_), channel_id=1, source_target_pairs={{0,16},{1,9},{2,18},{3,11},{4,20},{5,13},{6,22},{7,15},{8,24},{9,1... | collective-permute-start | bytes 1474568 | tf_op jit(solution)/shard_map/b_sums_far/ppermute | solution.py:336
  76.9 17.7 %collective-permute-start.20 = (bf16[2,2,3,160,256]{4,3,2,1,0:T(8,128)(2,1)S(1)}, bf16[2,2,3,160,256]{4,3,2,1,0:T(8,128)(2,1)S(1)}, u32[]{:S(2)}, u32[]{:S(2)}) collective-permute-start(bf16[2,2,3,160,256]{4,3,2,1,0:T(8,128)(2,1)S(1)} %get-tuple-element.37), channel_id=1, source_target_pairs={{0,8},{1,17},{2,10},{3,19},{4,12},{5,21},{6,14},{7,23},{8,0},{9,25... | collective-permute-start | bytes 2949128 | tf_op jit(solution)/shard_map/c_sums_near/ppermute | solution.py:336
  78.7 10.7 %collective-permute-start.16 = (bf16[2,2,160,256]{3,2,1,0:T(8,128)(2,1)S(1)}, bf16[2,2,160,256]{3,2,1,0:T(8,128)(2,1)S(1)}, u32[]{:S(2)}, u32[]{:S(2)}) collective-permute-start(bf16[2,2,160,256]{3,2,1,0:T(8,128)(2,1)S(1)} %hidden_back.5.refs_2_.refs_0_), channel_id=1, source_target_pairs={{0,16},{1,9},{2,18},{3,11},{4,20},{5,13},{6,22},{7,15},{8,24},{9,1... | collective-permute-start | bytes 983048 | tf_op jit(solution)/shard_map/b_own_far/ppermute | solution.py:336
  80.4 14.3 %collective-permute-start.19 = (bf16[128,1920]{1,0:T(8,128)(2,1)S(1)}, bf16[128,1920]{1,0:T(8,128)(2,1)S(1)}, u32[]{:S(2)}, u32[]{:S(2)}) collective-permute-start(bf16[128,1920]{1,0:T(8,128)(2,1)S(1)} %collective-permute-done.15.refs_4_.refs_1_), channel_id=1, source_target_pairs={{0,1},{1,0},{2,3},{3,2},{4,5},{5,4},{6,7},{7,6},{8,9},{9,8},{10,11... | collective-permute-start | bytes 1474568 | tf_op jit(solution)/shard_map/other_2_move/ppermute | solution.py:30
  89.5 18.0 %collective-permute-start.18 = (bf16[2,2,2,160,256]{4,3,2,1,0:T(8,128)(2,1)S(1)}, bf16[2,2,2,160,256]{4,3,2,1,0:T(8,128)(2,1)S(1)}, u32[]{:S(2)}, u32[]{:S(2)}) collective-permute-start(bf16[2,2,2,160,256]{4,3,2,1,0:T(8,128)(2,1)S(1)} %join.5.refs_2_.refs_3_), channel_id=1, source_target_pairs={{0,8},{1,17},{2,10},{3,19},{4,12},{5,21},{6,14},{7,23},{8,0},{9,25... | collective-permute-start | bytes 1966088 | tf_op jit(solution)/shard_map/b_both_near/ppermute | solution.py:336
  98.9 20.1 %collective-permute-start.28 = (bf16[2,2,3,160,256]{4,3,2,1,0:T(8,128)(2,1)S(1)}, bf16[2,2,3,160,256]{4,3,2,1,0:T(8,128)(2,1)S(1)}, u32[]{:S(2)}, u32[]{:S(2)}) collective-permute-start(bf16[2,2,3,160,256]{4,3,2,1,0:T(8,128)(2,1)S(1)} %get-tuple-element.41), channel_id=1, source_target_pairs={{0,8},{1,17},{2,10},{3,19},{4,12},{5,21},{6,14},{7,23},{8,0},{9,25... | collective-permute-start | bytes 2949128 | tf_op jit(solution)/shard_map/d_sums_near/ppermute | solution.py:336
  100.4 16.9 %collective-permute-start.22 = (bf16[2,3,160,256]{3,2,1,0:T(8,128)(2,1)S(1)}, bf16[2,3,160,256]{3,2,1,0:T(8,128)(2,1)S(1)}, u32[]{:S(2)}, u32[]{:S(2)}) collective-permute-start(bf16[2,3,160,256]{3,2,1,0:T(8,128)(2,1)S(1)} %add_parts.17.refs_6_), channel_id=1, source_target_pairs={{0,16},{1,9},{2,18},{3,11},{4,20},{5,13},{6,22},{7,15},{8,24},{9,1... | collective-permute-start | bytes 1474568 | tf_op jit(solution)/shard_map/c_sums_far/ppermute | solution.py:336
  102.1 10.0 %collective-permute-start.23 = (bf16[4,32,576]{2,1,0:T(8,128)(2,1)S(1)}, bf16[4,32,576]{2,1,0:T(8,128)(2,1)S(1)}, u32[]{:S(2)}, u32[]{:S(2)}) collective-permute-start(bf16[4,32,576]{2,1,0:T(8,128)(2,1)S(1)} %get-tuple-element.49), channel_id=1, source_target_pairs={{0,2},{1,3},{2,0},{3,1},{4,6},{5,7},{6,4},{7,5},{8,10},{9,11},{10,... | collective-permute-start | bytes 442376 | tf_op jit(solution)/shard_map/latent_terms/ppermute | solution.py:30
  105.1 12.1 %collective-permute-start.24 = (bf16[4,32,576]{2,1,0:T(8,128)(2,1)S(1)}, bf16[4,32,576]{2,1,0:T(8,128)(2,1)S(1)}, u32[]{:S(2)}, u32[]{:S(2)}) collective-permute-start(bf16[4,32,576]{2,1,0:T(8,128)(2,1)S(1)} %get-tuple-element.48), channel_id=1, source_target_pairs={{0,4},{1,5},{2,6},{3,7},{4,0},{5,1},{6,2},{7,3},{8,12},{9,13},{10,... | collective-permute-start | bytes 442376 | tf_op jit(solution)/shard_map/latent_terms/ppermute | solution.py:30
  107.5 9.7 %collective-permute-start.25 = (bf16[4,32,576]{2,1,0:T(8,128)(2,1)S(1)}, bf16[4,32,576]{2,1,0:T(8,128)(2,1)S(1)}, u32[]{:S(2)}, u32[]{:S(2)}) collective-permute-start(bf16[4,32,576]{2,1,0:T(8,128)(2,1)S(1)} %get-tuple-element.47), channel_id=1, source_target_pairs={{0,6},{1,7},{2,4},{3,5},{4,2},{5,3},{6,0},{7,1},{8,14},{9,15},{10,... | collective-permute-start | bytes 442376 | tf_op jit(solution)/shard_map/latent_terms/ppermute | solution.py:30
  117.6 8.4 %collective-permute-start.27 = (bf16[2,2,160,256]{3,2,1,0:T(8,128)(2,1)S(1)}, bf16[2,2,160,256]{3,2,1,0:T(8,128)(2,1)S(1)}, u32[]{:S(2)}, u32[]{:S(2)}) collective-permute-start(bf16[2,2,160,256]{3,2,1,0:T(8,128)(2,1)S(1)} %hidden_back.6.refs_2_.refs_0_), channel_id=1, source_target_pairs={{0,16},{1,9},{2,18},{3,11},{4,20},{5,13},{6,22},{7,15},{8,24},{9,1... | collective-permute-start | bytes 983048 | tf_op jit(solution)/shard_map/c_own_far/ppermute | solution.py:336
  119.2 18.4 %collective-permute-start.30 = (bf16[2,3,160,256]{3,2,1,0:T(8,128)(2,1)S(1)}, bf16[2,3,160,256]{3,2,1,0:T(8,128)(2,1)S(1)}, u32[]{:S(2)}, u32[]{:S(2)}) collective-permute-start(bf16[2,3,160,256]{3,2,1,0:T(8,128)(2,1)S(1)} %add_parts.20.refs_2_), channel_id=1, source_target_pairs={{0,16},{1,9},{2,18},{3,11},{4,20},{5,13},{6,22},{7,15},{8,24},{9,1... | collective-permute-start | bytes 1474568 | tf_op jit(solution)/shard_map/d_sums_far/ppermute | solution.py:336
  126.0 11.9 %collective-permute-start.29 = (bf16[2,2,2,160,256]{4,3,2,1,0:T(8,128)(2,1)S(1)}, bf16[2,2,2,160,256]{4,3,2,1,0:T(8,128)(2,1)S(1)}, u32[]{:S(2)}, u32[]{:S(2)}) collective-permute-start(bf16[2,2,2,160,256]{4,3,2,1,0:T(8,128)(2,1)S(1)} %join.6.refs_2_.refs_3_), channel_id=1, source_target_pairs={{0,8},{1,17},{2,10},{3,19},{4,12},{5,21},{6,14},{7,23},{8,0},{9,25... | collective-permute-start | bytes 1966088 | tf_op jit(solution)/shard_map/c_both_near/ppermute | solution.py:336
  126.1 11.4 %collective-permute-start.31 = (bf16[2,32,576]{2,1,0:T(8,128)(2,1)S(1)}, bf16[2,32,576]{2,1,0:T(8,128)(2,1)S(1)}, u32[]{:S(2)}, u32[]{:S(2)}) collective-permute-start(bf16[2,32,576]{2,1,0:T(8,128)(2,1)S(1)} %get-tuple-element.50), channel_id=1, source_target_pairs={{0,8},{1,17},{2,10},{3,19},{4,12},{5,21},{6,14},{7,23},{8,0},{9,25... | collective-permute-start | bytes 221192 | tf_op jit(solution)/shard_map/crossed_move/ppermute | solution.py:336
  128.4 14.1 %collective-permute-start.11 = (bf16[1,128,896]{2,1,0:T(8,128)(2,1)S(1)}, bf16[1,128,896]{2,1,0:T(8,128)(2,1)S(1)}, u32[]{:S(2)}, u32[]{:S(2)}) collective-permute-start(bf16[1,128,896]{2,1,0:T(8,128)(2,1)S(1)} %get-tuple-element.34.refs_6_), channel_id=1, source_target_pairs={{0,1},{1,0},{2,3},{3,2},{4,5},{5,4},{6,7},{7,6},{8,9},{9,8},{10,11... | collective-permute-start | bytes 688136 | tf_op jit(solution)/shard_map/a_other_move/ppermute | solution.py:30
  128.4 14.1 %collective-permute-start.26 = (bf16[128,896]{1,0:T(8,128)(2,1)S(1)}, bf16[128,896]{1,0:T(8,128)(2,1)S(1)}, u32[]{:S(2)}, u32[]{:S(2)}) collective-permute-start(bf16[128,896]{1,0:T(8,128)(2,1)S(1)} %add_parts.19.refs_2_), channel_id=1, source_target_pairs={{0,2},{1,3},{2,0},{3,1},{4,6},{5,7},{6,4},{7,5},{8,10},{9,11},{10,... | collective-permute-start | bytes 688136 | tf_op jit(solution)/shard_map/b_back_move/ppermute | solution.py:30
  137.9 7.1 %collective-permute-start.33 = (bf16[2,2,160,256]{3,2,1,0:T(8,128)(2,1)S(1)}, bf16[2,2,160,256]{3,2,1,0:T(8,128)(2,1)S(1)}, u32[]{:S(2)}, u32[]{:S(2)}) collective-permute-start(bf16[2,2,160,256]{3,2,1,0:T(8,128)(2,1)S(1)} %hidden_back.7.refs_7_.refs_0_), channel_id=1, source_target_pairs={{0,16},{1,9},{2,18},{3,11},{4,20},{5,13},{6,22},{7,15},{8,24},{9,1... | collective-permute-start | bytes 983048 | tf_op jit(solution)/shard_map/d_own_far/ppermute | solution.py:336
  145.1 10.9 %collective-permute-start.35 = (bf16[2,2,2,160,256]{4,3,2,1,0:T(8,128)(2,1)S(1)}, bf16[2,2,2,160,256]{4,3,2,1,0:T(8,128)(2,1)S(1)}, u32[]{:S(2)}, u32[]{:S(2)}) collective-permute-start(bf16[2,2,2,160,256]{4,3,2,1,0:T(8,128)(2,1)S(1)} %join.7.refs_2_.refs_3_), channel_id=1, source_target_pairs={{0,8},{1,17},{2,10},{3,19},{4,12},{5,21},{6,14},{7,23},{8,0},{9,25... | collective-permute-start | bytes 1966088 | tf_op jit(solution)/shard_map/d_both_near/ppermute | solution.py:336
  146.7 14.7 %collective-permute-start.34 = (bf16[128,896]{1,0:T(8,128)(2,1)S(1)}, bf16[128,896]{1,0:T(8,128)(2,1)S(1)}, u32[]{:S(2)}, u32[]{:S(2)}) collective-permute-start(bf16[128,896]{1,0:T(8,128)(2,1)S(1)} %add_parts.23.refs_2_), channel_id=1, source_target_pairs={{0,6},{1,7},{2,4},{3,5},{4,2},{5,3},{6,0},{7,1},{8,14},{9,15},{10,... | collective-permute-start | bytes 688136 | tf_op jit(solution)/shard_map/c_back_move/ppermute | solution.py:30
  163.0 13.5 %collective-permute-start.38 = (bf16[128,896]{1,0:T(8,128)(2,1)S(1)}, bf16[128,896]{1,0:T(8,128)(2,1)S(1)}, u32[]{:S(2)}, u32[]{:S(2)}) collective-permute-start(bf16[128,896]{1,0:T(8,128)(2,1)S(1)} %add_parts.26.refs_2_), channel_id=1, source_target_pairs={{0,4},{1,5},{2,6},{3,7},{4,0},{5,1},{6,2},{7,3},{8,12},{9,13},{10,... | collective-permute-start | bytes 688136 | tf_op jit(solution)/shard_map/d_back_move/ppermute | solution.py:30
  (16 other events, 89.4 us)
